TPU v7x, 512 devices: a whole 4x4x16 slice. The times are simulated.
512 devices in a mesh: row: 16 (over z_lo, core), col: 32 (over y, x, z_hi).
Axes of the slice: x: 4, y: 4, z: 16 (z_hi: 2, z_lo: 8; z = z_hi * 8 + z_lo), core: 2. Of those that a mesh axis runs over, the one named last changes fastest.
Arguments:
- amplitudes: float32 [6144, 6144], P(('row', 'col')), may hold values from -6 to 6
- integrals: float32 [6144, 6144], P(('row', 'col')), may hold values from -0.078125 to 0.078125
- occupied_energy: float32 [150], replicated, may hold values from -1.5 to -0.3
- virtual_energy: float32 [1536], replicated, may hold values from 0.2 to 4
- window_i: int32 [4], replicated, may hold values from 0 to 149
- window_j: int32 [4], replicated, may hold values from 0 to 149
Outputs:
- update: float32 [6144, 6144], P(('row', 'col'))
Inputs may be any that keep to these rules, and one draw needn't show every extreme that they name: `window_i`: indices of occupied orbitals. `window_j`: indices of occupied orbitals.
All inputs are finite; a program needn't handle non-finite values.
Results may differ from a plain program's by a relative error of at most 0.00007.
Values sent between devices are 32-bit elements; how exact they have to be, the bound alone decides.
No kernel may reach another device: no remote copies, remote signals or barrier semaphores. Data moves between devices by JAX's collectives and lax.ppermute only.
A program may use at most 128 MiB of HBM per device.

v0:
```python
import jax
import jax.numpy as jnp
from jax import lax
from jax.sharding import PartitionSpec as P


def per_device(amplitudes, integrals, occupied_energy, virtual_energy, window_i, window_j):
    col_count = lax.axis_size("col")
    local_rows = amplitudes.shape[0]
    grid_block = lax.all_to_all(integrals, "col", split_axis=1, concat_axis=0, tiled=True)
    column_panel = lax.all_gather(grid_block, "row", axis=0, tiled=True)
    amp_block = lax.all_to_all(amplitudes, "col", split_axis=1, concat_axis=0, tiled=True)
    cycle_block = jnp.dot(
        lax.all_gather(amp_block, "col", axis=1, tiled=True),
        column_panel,
        precision=lax.Precision.HIGHEST,
        preferred_element_type=jnp.float32,
    )
    stored = lax.all_to_all(cycle_block, "col", split_axis=0, concat_axis=1, tiled=True)
    row_start = (lax.axis_index("row") * col_count + lax.axis_index("col")) * local_rows
    row_shift = (occupied_energy[window_i][:, None] - virtual_energy[None, :]).reshape(-1)
    col_shift = (occupied_energy[window_j][:, None] - virtual_energy[None, :]).reshape(-1)
    local_shift = lax.dynamic_slice_in_dim(row_shift, row_start, local_rows, 0)
    return stored / (local_shift[:, None] + col_shift[None, :])


def solution(mesh):
    in_specs = (P(("row", "col"), None), P(("row", "col"), None), P(), P(), P(), P())
    out_specs = P(("row", "col"), None)
    return jax.shard_map(
        per_device, mesh=mesh, in_specs=in_specs, out_specs=out_specs, check_vma=False
    )
```

profile of v0, /device:TPU:97, one launch (start us, length us, event | category | flops | bytes accessed | tf_op | source)
XLA Modules:
  0.0 513.8 jit_solution(5254499772243333509)
XLA Ops:
  6.5 0.0 copy-start
  6.5 0.0 all-gather.5.cloned.1.call-start
  6.5 1.2 all_to_all.46
  7.7 0.2 copy.17
  8.0 49.9 %all_to_all.57 = f32[12,32,192]{2,0,1:T(8,128)S(1)} all-to-all(f32[12,32,192]{2,0,1:T(8,128)S(1)} %copy.17), channel_id=1, replica_groups=mesh['row'=16,'col'=32] {'col'}, dimensions={1} | all-to-all | bytes 589824 | tf_op jit(solution)/shard_map/all_to_all | solution.py:10
  57.9 0.8 all_to_all.49
  58.7 0.0 all-gather.5.cloned.1.call-update
  58.7 0.0 all-gather.3.cloned.1.call-start
  58.8 1.2 all_to_all.42
  59.9 0.2 copy.15
  60.2 26.6 %all_to_all.58 = f32[12,32,192]{2,0,1:T(8,128)S(1)} all-to-all(f32[12,32,192]{2,0,1:T(8,128)S(1)} %copy.15), channel_id=1, replica_groups=mesh['row'=16,'col'=32] {'col'}, dimensions={1} | all-to-all | bytes 589824 | tf_op jit(solution)/shard_map/all_to_all | solution.py:12
  86.8 0.0 copy-start.2
  86.8 0.9 copy.16
  87.7 0.0 all-gather.3.cloned.1.call-update
  87.7 0.0 copy-start.1
  87.7 63.0 %all-gather.5.cloned.1.call-done = f32[6144,192]{1,0:T(8,128)} async-done(((f32[384,192]{1,0:T(8,128)}), f32[6144,192]{1,0:T(8,128)}) %all-gather.5.cloned.1.call-update) | async-done | bytes 4718608 | tf_op jit(solution)/shard_map/all_gather | solution.py:11
  150.7 298.7 %all-gather.3.cloned.1.call-done = f32[384,6144]{0,1:T(8,128)} async-done(((f32[384,192]{0,1:T(8,128)}), f32[384,6144]{0,1:T(8,128)}) %all-gather.3.cloned.1.call-update) | async-done | bytes 9437200 | tf_op jit(solution)/shard_map/all_gather | solution.py:14
  449.4 18.3 %fusion = f32[384,192]{1,0:T(8,128)S(1)} fusion(f32[384,6144]{0,1:T(8,128)} %all-gather.3.cloned.1.call-done, f32[6144,192]{1,0:T(8,128)} %all-gather.5.cloned.1.call-done), kind=kOutput, calls=%fused_computation.9 | convolution fusion | flops 5435817984 | bytes 14450688 | tf_op jit(solution)/shard_map/dot_general | solution.py:13
  467.7 0.8 all_to_all.50
  468.6 5.3 %all-to-all-start.2 = ((f32[32,12,192]{2,1,0:T(8,128)}), f32[32,12,192]{2,1,0:T(8,128)S(1)}, u32[]{:S(2)}, u32[]{:S(2)}) async-start(f32[32,12,192]{2,1,0:T(8,128)} %all_to_all.50), calls=%async_computation.2 | async-start | bytes 1048576 | tf_op jit(solution)/shard_map/all_to_all | solution.py:19
  473.9 0.0 copy-done.2
  473.9 0.0 copy-done
  473.9 0.6 gather_fusion
  474.5 0.0 copy-done.3
  474.6 0.6 gather_fusion.1
  475.2 0.0 copy-done.1
  475.2 0.1 broadcast_subtract_fusion.1
  475.3 0.1 dynamic_slice.3
  475.4 30.3 %all-to-all-done.2 = f32[32,12,192]{2,1,0:T(8,128)S(1)} async-done(((f32[32,12,192]{2,1,0:T(8,128)}), f32[32,12,192]{2,1,0:T(8,128)S(1)}, u32[]{:S(2)}, u32[]{:S(2)}) %all-to-all-start.2) | async-done | bytes 294944 | tf_op jit(solution)/shard_map/all_to_all | solution.py:19
  505.7 0.2 copy.19
  505.9 0.2 all_to_all.53
  506.1 0.9 add_divide_fusion
  (8 shorter events, 0.1 us)
Async XLA Ops:
  6.5 467.4 %copy-start = (f32[150]{0:T(256)S(1)}, f32[150]{0:T(256)}, u32[]{:S(2)}) copy-start(f32[150]{0:T(256)} %param.8) | copy-start | bytes 1804
  6.5 144.2 %all-gather.5.cloned.1.call-start = ((), (), s32[]{:S(2)}) async-start(), calls=%async_computation.4 | async-start | bytes 6684672 | tf_op jit(solution)/shard_map/all_gather | solution.py:11
  58.7 390.7 %all-gather.3.cloned.1.call-start = ((), (), s32[]{:S(2)}) async-start(), calls=%async_computation.3 | async-start | bytes 9732096 | tf_op jit(solution)/shard_map/all_gather | solution.py:14
  86.8 387.0 %copy-start.2 = (s32[4]{0:T(128)S(1)}, s32[4]{0:T(128)}, u32[]{:S(2)}) copy-start(s32[4]{0:T(128)} %param.10) | copy-start | bytes 52
  87.7 386.8 %copy-start.3 = (s32[4]{0:T(128)S(1)}, s32[4]{0:T(128)}, u32[]{:S(2)}) copy-start(s32[4]{0:T(128)} %param.11) | copy-start | bytes 52
  87.7 387.5 %copy-start.1 = (f32[1536]{0:T(1024)S(1)}, f32[1536]{0:T(1024)}, u32[]{:S(2)}) copy-start(f32[1536]{0:T(1024)} %param.9) | copy-start | bytes 18436
  468.6 37.1 %all-to-all-start.2 = ((f32[32,12,192]{2,1,0:T(8,128)}), f32[32,12,192]{2,1,0:T(8,128)S(1)}, u32[]{:S(2)}, u32[]{:S(2)}) async-start(f32[32,12,192]{2,1,0:T(8,128)} %all_to_all.50), calls=%async_computation.2 | async-start | bytes 1048576 | tf_op jit(solution)/shard_map/all_to_all | solution.py:19
Sparse Core Ops, SparseCore 0:
  58.8 91.8 all-gather.4
  155.1 294.2 all-gather.2
where the time goes:
time: 514 us
  waiting for transfers between devices  392 us (76%)
  blocking collectives  76.5 us (15%)
  matrix products  18.3 us (4%)
  between operations  13.5 us (3%)
  local copies, waits for them, and re-layouts  7.18 us (1%)
  starting transfers between devices  5.32 us (1%)
    all_gather x1, waiting for transfers between devices, per_device(): lax.all_gather(amp_block, 'col', axis=1, tiled=True)  299 us
    all_gather x1, waiting for transfers between devices, per_device(): column_panel = lax.all_gather(grid_block, 'row', axis=0, tiled=True)  63 us
    all_to_all x1, blocking collectives, per_device(): lax.all_to_all(integrals, 'col', split_axis=1, concat_axis=0, tiled=True)  49.9 us
    all_to_all x1, waiting for transfers between devices, per_device(): lax.all_to_all(cycle_block, 'col', split_axis=0, concat_axis=1, tiled=True)  30.3 us
    all_to_all x1, blocking collectives, per_device(): lax.all_to_all(amplitudes, 'col', split_axis=1, concat_axis=0, tiled=True)  26.6 us
    dot_general x1, matrix products, per_device(): jnp.dot(lax.all_gather(amp_block, 'col', axis=1, tiled=True), column_pane...  18.3 us
  transfers between devices with their start and end apart: 3, of which 3 were waited for; matrix products, arithmetic and copies ran while one was open for 1% of the time, Pallas kernels for 0%

commit v1 on v0

v1 whole, which is shorter than its diff:
```python
import jax
import jax.numpy as jnp
import numpy as np
from jax import lax
from jax.sharding import Mesh, PartitionSpec as P

AXES = ("zlo", "core", "y", "x", "zhi")
SIZES = (8, 2, 4, 4, 2)
PLANE = ("y", "x")
RING = ("zhi", "zlo")


def column_order():
    source = np.arange(768).reshape(2, 16, 2, 12).transpose(2, 0, 1, 3).reshape(-1)
    order = np.zeros((768, 768), np.float32)
    order[source, np.arange(768)] = 1.0
    return order


def per_device(amplitudes, integrals, occupied_energy, virtual_energy, window_i, window_j):
    rows = amplitudes.shape[0]
    blocks = integrals.reshape(rows, 16, 384).transpose(1, 0, 2)
    blocks = lax.all_to_all(blocks, PLANE, split_axis=0, concat_axis=0, tiled=True)
    panel = lax.all_gather(blocks.reshape(16 * rows, 384), RING, axis=0, tiled=True)
    pieces = amplitudes.reshape(rows, 4, 2, 2, 384).transpose(3, 0, 1, 2, 4)
    pieces = jnp.dot(
        pieces.reshape(-1, 768),
        jnp.asarray(column_order()),
        precision=lax.Precision.HIGHEST,
        preferred_element_type=jnp.float32,
    )
    pieces = pieces.reshape(2, rows, 4, 2, 384).transpose(0, 1, 3, 2, 4).reshape(2, rows, 3072)
    pieces = lax.all_to_all(pieces, "core", split_axis=0, concat_axis=0, tiled=True)
    pieces = pieces.reshape(1, 2 * rows, 3072)
    spread = jnp.broadcast_to(pieces, (16, 2 * rows, 3072))
    left = lax.all_to_all(spread, PLANE, split_axis=0, concat_axis=0, tiled=True)
    partial = jnp.dot(
        left.reshape(32 * rows, 3072),
        panel,
        precision=lax.Precision.HIGH,
        preferred_element_type=jnp.float32,
    )
    parts = lax.all_to_all(
        partial.reshape(32, rows, 384), ("y", "x", "core"), split_axis=0, concat_axis=0, tiled=True
    )
    stored = parts.reshape(16, 2, rows, 384).sum(1).transpose(1, 0, 2).reshape(rows, 6144)
    index = lax.axis_index(AXES)
    row_shift = (occupied_energy[window_i][:, None] - virtual_energy[None, :]).reshape(-1)
    col_shift = (occupied_energy[window_j][:, None] - virtual_energy[None, :]).reshape(-1)
    local_shift = lax.dynamic_slice_in_dim(row_shift, index * rows, rows, 0)
    return stored / (local_shift[:, None] + col_shift[None, :])


def solution(mesh):
    fine = Mesh(mesh.devices.reshape(SIZES), AXES)
    split = P(AXES, None)
    return jax.shard_map(
        per_device,
        mesh=fine,
        in_specs=(split, split, P(), P(), P(), P()),
        out_specs=split,
        check_vma=False,
    )
```

time: 514 us -> 160 us (0.31)
  the two profiles are of different devices: /device:TPU:97 before, /device:TPU:1 now
where the time goes in v1:
time: 160 us
  waiting for transfers between devices  83.5 us (52%)
  blocking collectives  22.6 us (14%)
  local copies, waits for them, and re-layouts  15.2 us (10%)
  between operations  13.6 us (8%)
  matrix products  12.7 us (8%)
  starting transfers between devices  11 us (7%)
    all_to_all x1, waiting for transfers between devices, per_device(): lax.all_to_all(spread, PLANE, split_axis=0, concat_axis=0, tiled=True)  70.8 us
    all_to_all x1, blocking collectives, per_device(): lax.all_to_all(blocks, PLANE, split_axis=0, concat_axis=0, tiled=True)  15.9 us
    all_to_all x1, waiting for transfers between devices, per_device(): lax.all_to_all(partial.reshape(32, rows, 384), ('y', 'x', 'core'), split_...  12.7 us
    dot_general x1, matrix products, per_device(): jnp.dot(left.reshape(32 * rows, 3072), panel, precision=lax.Precision.HIG...  10.2 us
    dot_general x2, local copies, waits for them, and re-layouts, per_device(): jnp.dot(left.reshape(32 * rows, 3072), panel, precision=lax.Precision.HIG...  6.75 us
    all_to_all x1, blocking collectives, per_device(): lax.all_to_all(pieces, 'core', split_axis=0, concat_axis=0, tiled=True)  6.67 us
    all_to_all x1, starting transfers between devices, per_device(): lax.all_to_all(partial.reshape(32, rows, 384), ('y', 'x', 'core'), split_...  6.27 us
    all_to_all x1, starting transfers between devices, per_device(): lax.all_to_all(spread, PLANE, split_axis=0, concat_axis=0, tiled=True)  4.7 us
  transfers between devices with their start and end apart: 3, of which 2 were waited for; matrix products, arithmetic and copies ran while one was open for 9% of the time, Pallas kernels for 0%

profile of v1, /device:TPU:1, one launch (start us, length us, event | category | flops | bytes accessed | tf_op | source)
XLA Modules:
  0.0 159.5 jit_solution(5421180476183781436)
XLA Ops:
  6.5 0.0 copy-start
  6.5 0.0 all-gather.2.cloned.1.call-start
  6.5 1.2 copy.41
  7.8 0.1 copy.51
  7.9 15.9 %all_to_all.20 = f32[16,12,384]{2,1,0:T(8,128)S(1)} all-to-all(f32[16,12,384]{2,1,0:T(8,128)S(1)} %bitcast.29), channel_id=1, replica_groups=mesh['zlo'=8,'core'=2,'y'=4,'x'=4,'zhi'=2] {'y','x'}, dimensions={0} | all-to-all | bytes 589824 | tf_op jit(solution)/shard_map/all_to_all | solution.py:23
  23.8 0.7 reshape.54
  24.5 0.0 all-gather.2.cloned.1.call-update
  24.6 1.2 reshape.51
  25.8 0.2 copy.52
  26.0 0.3 dot_general.14
  26.3 0.0 copy-done.1
  26.3 2.5 %convolution_bitcast_fusion = f32[2,12,2,4,384]{4,1,3,0,2:T(8,128)S(1)} fusion(f32[2,384,768,1,1]{2,1,4,3,0:T(8,128)S(1)} %copy-done.1, f32[2,12,4,768]{3,2,1,0:T(4,128)S(1)} %dot_general.14), kind=kOutput, calls=%fused_computation.5 | convolution fusion | flops 679477248 | bytes 2949120 | tf_op jit(solution)/shard_map/dot_general | solution.py:26
  28.8 0.1 copy.39
  28.9 0.1 reshape.78
  29.1 6.7 %all_to_all.21 = f32[2,12,3072]{2,1,0:T(8,128)S(1)} all-to-all(f32[2,12,3072]{2,1,0:T(8,128)S(1)} %reshape.78), channel_id=1, replica_groups=mesh['zlo'=8,'core'=2,'y'=4,'x'=4,'zhi'=2] {'core'}, dimensions={0} | all-to-all | bytes 589824 | tf_op jit(solution)/shard_map/all_to_all | solution.py:33
  35.8 2.7 %broadcast_in_dim.9 = f32[16,24,3072]{2,1,0:T(8,128)} broadcast(f32[24,3072]{1,0:T(8,128)S(1)} %broadcast_in_dim.8), dimensions={1,2} | broadcast | bytes 5013504 | tf_op jit(solution)/shard_map/broadcast_in_dim | solution.py:35
  38.5 4.7 %all-to-all-start.1 = ((f32[16,24,3072]{2,1,0:T(8,128)}), f32[16,24,3072]{2,1,0:T(8,128)}, u32[]{:S(2)}, u32[]{:S(2)}) async-start(f32[16,24,3072]{2,1,0:T(8,128)} %broadcast_in_dim.9), calls=%async_computation.1 | async-start | bytes 9437184 | tf_op jit(solution)/shard_map/all_to_all | solution.py:36
  43.2 0.0 copy-done.3
  43.2 0.0 copy-done.4
  43.2 70.8 %all-to-all-done.1 = f32[16,24,3072]{2,1,0:T(8,128)} async-done(((f32[16,24,3072]{2,1,0:T(8,128)}), f32[16,24,3072]{2,1,0:T(8,128)}, u32[]{:S(2)}, u32[]{:S(2)}) %all-to-all-start.1) | async-done | bytes 4718624 | tf_op jit(solution)/shard_map/all_to_all | solution.py:36
  114.0 5.5 %dot_general.18 = f32[32,12,3072]{2,1,0:T(8,128)} reshape(f32[16,24,3072]{2,1,0:T(8,128)} %all-to-all-done.1) | data formatting | bytes 9437184 | tf_op jit(solution)/shard_map/dot_general | solution.py:37
  119.6 10.2 %fusion = f32[32,12,384]{2,0,1:T(8,128)S(1)} fusion(f32[3072,384]{1,0:T(8,128)} %all-gather.2.cloned.1.call-done, f32[32,12,3072]{2,1,0:T(8,128)} %dot_general.18), kind=kOutput, calls=%fused_computation.2 | convolution fusion | flops 2717908992 | bytes 10027008 | tf_op jit(solution)/shard_map/dot_general | solution.py:37
  129.7 1.2 copy.36
  131.0 6.3 %all-to-all-start.3 = ((f32[32,12,384]{2,1,0:T(8,128)}), f32[32,12,384]{2,1,0:T(8,128)S(1)}, u32[]{:S(2)}, u32[]{:S(2)}) async-start(f32[32,12,384]{2,1,0:T(8,128)} %copy.36), calls=%async_computation.3 | async-start | bytes 1572864 | tf_op jit(solution)/shard_map/all_to_all | solution.py:43
  137.3 0.6 gather_fusion
  137.9 0.6 gather_fusion.1
  138.6 0.1 broadcast_subtract_fusion.1
  138.7 0.1 dynamic_slice.3
  138.8 12.7 %all-to-all-done.3 = f32[32,12,384]{2,1,0:T(8,128)S(1)} async-done(((f32[32,12,384]{2,1,0:T(8,128)}), f32[32,12,384]{2,1,0:T(8,128)S(1)}, u32[]{:S(2)}, u32[]{:S(2)}) %all-to-all-start.3) | async-done | bytes 589856 | tf_op jit(solution)/shard_map/all_to_all | solution.py:43
  151.5 0.1 copy.37
  151.7 0.1 copy.42
  151.8 0.9 add_divide_fusion
  (17 shorter events, 0.2 us)
Async XLA Ops:
  6.5 130.7 %copy-start = (f32[150]{0:T(256)S(1)}, f32[150]{0:T(256)}, u32[]{:S(2)}) copy-start(f32[150]{0:T(256)} %param.9) | copy-start | bytes 1804
  6.5 19.7 %copy-start.1 = (f32[2,384,768,1,1]{2,1,4,3,0:T(8,128)S(1)}, f32[2,384,768,1,1]{2,1,4,3,0:T(8,128)}, u32[]{:S(2)}) copy-start(f32[2,384,768,1,1]{2,1,4,3,0:T(8,128)} %constant.46) | copy-start | bytes 7077892
  6.5 113.0 %all-gather.2.cloned.1.call-start = ((), (), s32[]{:S(2)}) async-start(), calls=%async_computation.4 | async-start | bytes 5013504 | tf_op jit(solution)/shard_map/all_gather | solution.py:24
  38.5 4.7 %copy-start.3 = (s32[4]{0:T(128)S(1)}, s32[4]{0:T(128)}, u32[]{:S(2)}) copy-start(s32[4]{0:T(128)} %param.11) | copy-start | bytes 52
  38.5 4.7 %copy-start.4 = (s32[4]{0:T(128)S(1)}, s32[4]{0:T(128)}, u32[]{:S(2)}) copy-start(s32[4]{0:T(128)} %param.12) | copy-start | bytes 52
  38.5 75.6 %all-to-all-start.1 = ((f32[16,24,3072]{2,1,0:T(8,128)}), f32[16,24,3072]{2,1,0:T(8,128)}, u32[]{:S(2)}, u32[]{:S(2)}) async-start(f32[16,24,3072]{2,1,0:T(8,128)} %broadcast_in_dim.9), calls=%async_computation.1 | async-start | bytes 9437184 | tf_op jit(solution)/shard_map/all_to_all | solution.py:36
  119.6 19.0 %copy-start.2 = (f32[1536]{0:T(1024)S(1)}, f32[1536]{0:T(1024)}, u32[]{:S(2)}) copy-start(f32[1536]{0:T(1024)} %param.10) | copy-start | bytes 18436
  131.0 20.5 %all-to-all-start.3 = ((f32[32,12,384]{2,1,0:T(8,128)}), f32[32,12,384]{2,1,0:T(8,128)S(1)}, u32[]{:S(2)}, u32[]{:S(2)}) async-start(f32[32,12,384]{2,1,0:T(8,128)} %copy.36), calls=%async_computation.3 | async-start | bytes 1572864 | tf_op jit(solution)/shard_map/all_to_all | solution.py:43
Sparse Core Ops, SparseCore 0:
  24.7 74.5 all-gather.1

commit v2 on v1

v2 whole, which is shorter than its diff:
```python
import functools

import jax
import jax.numpy as jnp
import numpy as np
from jax import lax
from jax.experimental import pallas as pl
from jax.experimental.pallas import tpu as pltpu
from jax.sharding import Mesh, PartitionSpec as P

AXES = ("zlo", "core", "y", "x", "zhi")
SIZES = (8, 2, 4, 4, 2)
PLANE = ("y", "x")
RING = ("zhi", "zlo")
ROWS = 12
WIDE = 384
HALF = 3072
STEP = 512
VMEM = pl.BlockSpec(memory_space=pltpu.VMEM)


def params():
    return pltpu.CompilerParams(vmem_limit_bytes=48 * 1024 * 1024)


def cost(flops, moved):
    return pl.CostEstimate(flops=flops, bytes_accessed=moved, transcendentals=0)


def column_order():
    source = np.arange(768).reshape(2, 16, 2, 12).transpose(2, 0, 1, 3).reshape(-1)
    order = np.zeros((768, 768), np.float32)
    order[source, np.arange(768)] = 1
    return order


def prepare_kernel(core_ref, a_ref, b_ref, own_ref, other_ref, blocks_ref):
    core = core_ref[0]
    for z in range(8):
        at = slice(WIDE * z, WIDE * z + WIDE)
        own_ref[:, at] = a_ref[:, pl.ds(pl.multiple_of(768 * z + WIDE * core, 128), WIDE)]
        other_ref[:, at] = a_ref[:, pl.ds(pl.multiple_of(768 * z + WIDE - WIDE * core, 128), WIDE)]
    for i in range(16):
        blocks_ref[i] = b_ref[:, WIDE * i : WIDE * i + WIDE]


def spread_kernel(core_ref, own_ref, other_ref, order_ref, out_ref, rows_ref):
    first = core_ref[0] == 0
    own, other = own_ref[...], other_ref[...]
    upper, lower = jnp.where(first, own, other), jnp.where(first, other, own)
    order = order_ref[...].astype(jnp.bfloat16)
    for q in range(4):
        lanes = slice(768 * q, 768 * q + 768)
        x = jnp.concatenate([upper[:, lanes], lower[:, lanes]], axis=0)
        total = None
        for _ in range(3):
            part = x.astype(jnp.bfloat16)
            x = x - part.astype(jnp.float32)
            moved = jnp.dot(part, order, preferred_element_type=jnp.float32)
            total = moved if total is None else total + moved
        for zhi in range(2):
            at = 1536 * zhi + WIDE * q
            rows_ref[:, at : at + WIDE] = total[:, WIDE * zhi : WIDE * zhi + WIDE]
    for i in range(16):
        out_ref[i] = rows_ref[...]


def split_kernel(x_ref, high_ref, low_ref):
    x = x_ref[...]
    high = x.astype(jnp.bfloat16)
    high_ref[...] = high
    low_ref[...] = (x - high.astype(jnp.float32)).astype(jnp.bfloat16)


def product_kernel(high_ref, low_ref, panel_ref, out_ref, total_ref):
    step = pl.program_id(0)
    b = panel_ref[...]
    b_high = b.astype(jnp.bfloat16)
    b_low = (b - b_high.astype(jnp.float32)).astype(jnp.bfloat16)
    a_high, a_low = high_ref[...], low_ref[...]
    dot = functools.partial(jnp.dot, preferred_element_type=jnp.float32)
    term = dot(a_high, b_high) + (dot(a_low, b_high) + dot(a_high, b_low))

    @pl.when(step == 0)
    def _():
        total_ref[...] = term

    @pl.when(step > 0)
    def _():
        total_ref[...] += term

    @pl.when(step == HALF // STEP - 1)
    def _():
        for d in range(32):
            for g in range(3):
                out_ref[d, ROWS * g : ROWS * g + ROWS, :] = total_ref[
                    ROWS * d : ROWS * d + ROWS, 128 * g : 128 * g + 128
                ]


def divide_kernel(parts_ref, row_ref, col_ref, out_ref):
    row = row_ref[...]
    for i in range(16):
        for g in range(3):
            at = slice(ROWS * g, ROWS * g + ROWS)
            lanes = slice(WIDE * i + 128 * g, WIDE * i + 128 * g + 128)
            cycle = parts_ref[2 * i, at, :] + parts_ref[2 * i + 1, at, :]
            out_ref[:, lanes] = cycle / (row + col_ref[:, lanes])


def per_device(amplitudes, integrals, occupied_energy, virtual_energy, window_i, window_j):
    f32, bf16 = jnp.float32, jnp.bfloat16
    core = lax.axis_index("core").reshape(1)
    own, other, blocks = pl.pallas_call(
        prepare_kernel,
        out_shape=[
            jax.ShapeDtypeStruct((ROWS, HALF), f32),
            jax.ShapeDtypeStruct((ROWS, HALF), f32),
            jax.ShapeDtypeStruct((16, ROWS, WIDE), f32),
        ],
        in_specs=[pl.BlockSpec(memory_space=pltpu.SMEM), VMEM, VMEM],
        out_specs=[VMEM] * 3,
        compiler_params=params(),
        cost_estimate=cost(1, 2 << 20),
        name="prepare",
    )(core, amplitudes, integrals)
    other = lax.ppermute(other, "core", [(0, 1), (1, 0)])
    blocks = lax.all_to_all(blocks, PLANE, split_axis=0, concat_axis=0, tiled=True)
    panel = lax.all_gather(blocks.reshape(16 * ROWS, WIDE), RING, axis=0, tiled=True)

    spread = pl.pallas_call(
        spread_kernel,
        out_shape=jax.ShapeDtypeStruct((16, 2 * ROWS, HALF), f32),
        in_specs=[pl.BlockSpec(memory_space=pltpu.SMEM), VMEM, VMEM, VMEM],
        out_specs=VMEM,
        scratch_shapes=[pltpu.VMEM((2 * ROWS, HALF), f32)],
        compiler_params=params(),
        cost_estimate=cost(2 * 24 * 3 * HALF * 768, 7 << 20),
        name="spread",
    )(core, own, other, jnp.asarray(column_order()))
    spread, occupied_energy, virtual_energy, window_i, window_j = lax.optimization_barrier(
        (spread, occupied_energy, virtual_energy, window_i, window_j)
    )
    left = lax.all_to_all(spread, PLANE, split_axis=0, concat_axis=0, tiled=True)
    left = left.reshape(WIDE, HALF)
    tile = pl.BlockSpec((WIDE, STEP), lambda k: (0, k))
    high, low = pl.pallas_call(
        split_kernel,
        grid=(HALF // STEP,),
        out_shape=[jax.ShapeDtypeStruct((WIDE, HALF), bf16)] * 2,
        in_specs=[tile],
        out_specs=[tile, tile],
        compiler_params=params(),
        cost_estimate=cost(4 * WIDE * HALF, 8 * WIDE * HALF),
        name="split",
    )(left)

    index = lax.axis_index(AXES) * ROWS
    virt = virtual_energy.shape[0]
    row = occupied_energy[window_i[index // virt]] - lax.dynamic_slice_in_dim(
        virtual_energy, index % virt, ROWS, 0
    )
    col = (occupied_energy[window_j][:, None] - virtual_energy[None, :]).reshape(1, -1)
    row = row[:, None]
    high, low, row, col = lax.optimization_barrier((high, low, row, col))

    partial = pl.pallas_call(
        product_kernel,
        grid=(HALF // STEP,),
        out_shape=jax.ShapeDtypeStruct((32, 3 * ROWS, 128), f32),
        in_specs=[tile, tile, pl.BlockSpec((STEP, WIDE), lambda k: (k, 0))],
        out_specs=pl.BlockSpec((32, 3 * ROWS, 128), lambda k: (0, 0, 0)),
        scratch_shapes=[pltpu.VMEM((WIDE, WIDE), f32)],
        compiler_params=params(),
        cost_estimate=cost(6 * WIDE * WIDE * HALF, 8 * WIDE * HALF),
        name="product",
    )(high, low, panel)
    parts = lax.all_to_all(partial, ("y", "x", "core"), split_axis=0, concat_axis=0, tiled=True)
    return pl.pallas_call(
        divide_kernel,
        out_shape=jax.ShapeDtypeStruct((ROWS, 16 * WIDE), f32),
        in_specs=[VMEM] * 3,
        out_specs=VMEM,
        compiler_params=params(),
        cost_estimate=cost(4 * ROWS * 16 * WIDE, 1 << 20),
        name="divide",
    )(parts, row, col)


def solution(mesh):
    fine = Mesh(mesh.devices.reshape(SIZES), AXES)
    split = P(AXES, None)
    return jax.shard_map(
        per_device,
        mesh=fine,
        in_specs=(split, split, P(), P(), P(), P()),
        out_specs=split,
        check_vma=False,
    )
```

time: 160 us -> 157 us (0.981)
  Pallas kernels: 0 us -> 18.4 us
  matrix products: 12.7 us -> 0 us
  blocking collectives: 22.6 us -> 15.9 us
  local copies, waits for them, and re-layouts: 15.2 us -> 9.59 us
  starting transfers between devices: 11 us -> 15.9 us
  waiting for transfers between devices: 83.5 us -> 80 us
  between operations: 13.6 us -> 15.4 us
    pallas_call x0 -> x5, Pallas kernels: none -> 18.4 us  [the longest x1 8 us: per_device(): pl.pallas_call(product_kernel, grid=(HALF // STEP,), out_shape=jax.ShapeD...]
    dot_general x2 -> x0, matrix products: 12.7 us -> none  [the longest x1 10.2 us: per_device(): jnp.dot(left.reshape(32 * rows, 3072), panel, precision=lax.Precision.HIG...]
    dot_general x3 -> x0, local copies, waits for them, and re-layouts: 7.04 us -> none  [the longest x2 6.75 us: per_device(): jnp.dot(left.reshape(32 * rows, 3072), panel, precision=lax.Precision.HIG...]
    all_to_all x1 -> x0, blocking collectives: 6.67 us -> none  [per_device(): lax.all_to_all(pieces, 'core', split_axis=0, concat_axis=0, tiled=True)]
    unnamed x13 -> x19, local copies, waits for them, and re-layouts: 1.39 us -> 6.8 us
    ppermute x0 -> x1, starting transfers between devices: none -> 4.9 us  [per_device(): other = lax.ppermute(other, 'core', [(0, 1), (1, 0)])]
    all_to_all x1, waiting for transfers between devices: 70.8 us -> 66.1 us  [per_device(): lax.all_to_all(spread, PLANE, split_axis=0, concat_axis=0, tiled=True)]
    broadcast_in_dim x2 -> x0, local copies, waits for them, and re-layouts: 2.74 us -> none  [per_device(): spread = jnp.broadcast_to(pieces, (16, 2 * rows, 3072))]
  transfers between devices with their start and end apart: 3 -> 4, of which waited for: 2 -> 3; matrix products, arithmetic and copies ran while one was open for 9% -> 2% of each run, Pallas kernels for 0% -> 6%
where the time goes in v2:
time: 157 us; the launch traced here: 156 us
  waiting for transfers between devices  80 us (51%)
  Pallas kernels  18.4 us (12%)
  starting transfers between devices  15.9 us (10%)
  blocking collectives  15.9 us (10%)
  between operations  15.4 us (10%)
  local copies, waits for them, and re-layouts  9.59 us (6%)
    all_to_all x1, waiting for transfers between devices, per_device(): lax.all_to_all(spread, PLANE, split_axis=0, concat_axis=0, tiled=True)  66.1 us
    all_to_all x1, blocking collectives, per_device(): lax.all_to_all(blocks, PLANE, split_axis=0, concat_axis=0, tiled=True)  15.9 us
    all_to_all x1, waiting for transfers between devices, per_device(): lax.all_to_all(partial, ('y', 'x', 'core'), split_axis=0, concat_axis=0,...  12.8 us
    pallas_call x1, Pallas kernels, per_device(): pl.pallas_call(product_kernel, grid=(HALF // STEP,), out_shape=jax.ShapeD...  8 us
    unnamed x19, local copies, waits for them, and re-layouts  6.8 us
    all_to_all x1, starting transfers between devices, per_device(): lax.all_to_all(partial, ('y', 'x', 'core'), split_axis=0, concat_axis=0,...  6.28 us
    pallas_call x1, Pallas kernels, per_device(): pl.pallas_call(spread_kernel, out_shape=jax.ShapeDtypeStruct((16, 2 * ROW...  5.06 us
    ppermute x1, starting transfers between devices, per_device(): other = lax.ppermute(other, 'core', [(0, 1), (1, 0)])  4.9 us
  transfers between devices with their start and end apart: 4, of which 3 were waited for; matrix products, arithmetic and copies ran while one was open for 2% of the time, Pallas kernels for 6%

profile of v2, /device:TPU:1, one launch (start us, length us, event | category | flops | bytes accessed | tf_op | source)
XLA Modules:
  0.0 155.9 jit_solution(5607735560654163269)
XLA Ops:
  6.5 0.0 all-gather.2.cloned.1.call-start
  6.5 0.0 copy-start.3
  6.5 1.0 copy-done.3
  7.5 1.0 copy-done.4
  8.5 0.1 prepare.1
  8.6 15.9 %all_to_all.15 = f32[16,12,384]{2,1,0:T(8,128)S(1)} all-to-all(f32[16,12,384]{2,1,0:T(8,128)S(1)} %get-tuple-element.30), channel_id=1, replica_groups=mesh['zlo'=8,'core'=2,'y'=4,'x'=4,'zhi'=2] {'y','x'}, dimensions={0} | all-to-all | bytes 589824 | tf_op jit(solution)/shard_map/all_to_all | solution.py:128
  24.5 0.7 reshape.36
  25.2 0.0 all-gather.2.cloned.1.call-update
  25.3 4.9 %collective-permute-start = (f32[12,3072]{1,0:T(8,128)S(1)}, f32[12,3072]{1,0:T(8,128)S(1)}, u32[]{:S(2)}, u32[]{:S(2)}) collective-permute-start(f32[12,3072]{1,0:T(8,128)S(1)} %get-tuple-element.20), channel_id=1, source_target_pairs={{0,32},{32,0},{1,33},{33,1},{2,34},{34,2},{3,35},{35,3},{4,36},{36... | collective-permute-start | bytes 442376 | tf_op jit(solution)/shard_map/ppermute | solution.py:127
  30.2 1.0 collective-permute-done.other_ref
  31.2 1.7 %copy-done.2 = f32[768,768]{1,0:T(8,128)S(1)} copy-done((f32[768,768]{1,0:T(8,128)S(1)}, f32[768,768]{1,0:T(8,128)}, u32[]{:S(2)}) %copy-start.2) | copy-done | bytes 2359320
  32.9 5.1 %spread.1 = f32[16,24,3072]{2,1,0:T(8,128)} custom-call(s32[1]{0:T(128)} %bitcast.core_ref, f32[12,3072]{1,0:T(8,128)S(1)} %get-tuple-element.19.own_ref, f32[12,3072]{1,0:T(8,128)S(1)} %collective-permute-done.other_ref, f32[768,768]{1,0:T(8,128)S(1)} %copy-done.2), custom_call_target="tpu_custom_call" | custom-call | flops 339738624 | bytes 7340032 | tf_op jit(solution)/shard_map/spread/pallas_call | solution.py:131
  37.9 4.7 %all-to-all-start = ((f32[16,24,3072]{2,1,0:T(8,128)}), f32[16,24,3072]{2,1,0:T(8,128)}, u32[]{:S(2)}, u32[]{:S(2)}) async-start(f32[16,24,3072]{2,1,0:T(8,128)} %spread.1), calls=%async_computation | async-start | bytes 9437184 | tf_op jit(solution)/shard_map/all_to_all | solution.py:144
  42.7 0.0 copy-done.7
  42.7 0.7 dynamic_slice.9
  45.3 0.0 copy-done.5
  45.3 0.7 dynamic_slice.10
  46.0 0.0 copy-done.8
  46.0 0.6 gather_fusion
  46.6 0.0 copy-done.6
  46.6 0.1 subtract_bitcast_fusion
  46.7 0.7 subtract_bitcast_fusion.1
  47.5 66.1 %all-to-all-done = f32[16,24,3072]{2,1,0:T(8,128)} async-done(((f32[16,24,3072]{2,1,0:T(8,128)}), f32[16,24,3072]{2,1,0:T(8,128)}, u32[]{:S(2)}, u32[]{:S(2)}) %all-to-all-start) | async-done | bytes 4718624 | tf_op jit(solution)/shard_map/all_to_all | solution.py:144
  113.5 4.4 %split.1 = (bf16[384,3072]{1,0:T(8,128)(2,1)S(1)}, bf16[384,3072]{1,0:T(8,128)(2,1)S(1)}) custom-call(f32[384,3072]{1,0:T(8,128)} %bitcast.1.x_ref), custom_call_target="tpu_custom_call" | custom-call | flops 4718592 | bytes 9437184 | tf_op jit(solution)/shard_map/split/pallas_call | solution.py:147
  117.9 0.0 copy-start
  117.9 1.4 copy-done
  119.3 1.7 %copy-done.1 = bf16[384,3072]{1,0:T(8,128)(2,1)S(1)} copy-done((bf16[384,3072]{1,0:T(8,128)(2,1)S(1)}, bf16[384,3072]{1,0:T(8,128)(2,1)}, u32[]{:S(2)}) %copy-start.1) | copy-done | bytes 2359320
  121.0 8.0 %product.1 = f32[32,36,128]{2,1,0:T(8,128)} custom-call(bf16[384,3072]{1,0:T(8,128)(2,1)S(1)} %get-tuple-element.28.high_ref, bf16[384,3072]{1,0:T(8,128)(2,1)S(1)} %copy-done.1, f32[3072,384]{1,0:T(8,128)} %all-gather.2.cloned.1.call-done.panel_ref), custom_call_target="tpu_custom_call" | custom-call | flops 2717908992 | bytes 9437184 | tf_op jit(solution)/shard_map/product/pallas_call | solution.py:167
  129.0 6.3 %all-to-all-start.2 = ((f32[32,36,128]{2,1,0:T(8,128)}), f32[32,36,128]{2,1,0:T(8,128)S(1)}, u32[]{:S(2)}, u32[]{:S(2)}) async-start(f32[32,36,128]{2,1,0:T(8,128)} %product.1), calls=%async_computation.2 | async-start | bytes 1310720 | tf_op jit(solution)/shard_map/all_to_all | solution.py:178
  135.3 0.1 copy.9.row_ref
  135.4 12.8 %all-to-all-done.2.parts_ref = f32[32,36,128]{2,1,0:T(8,128)S(1)} async-done(((f32[32,36,128]{2,1,0:T(8,128)}), f32[32,36,128]{2,1,0:T(8,128)S(1)}, u32[]{:S(2)}, u32[]{:S(2)}) %all-to-all-start.2) | async-done | bytes 589856 | tf_op jit(solution)/shard_map/all_to_all | solution.py:178
  148.2 0.9 divide.1
  (11 shorter events, 0.1 us)
Async XLA Ops:
  6.5 112.8 %all-gather.2.cloned.1.call-start = ((), (), s32[]{:S(2)}) async-start(), calls=%async_computation.3 | async-start | bytes 5013504 | tf_op jit(solution)/shard_map/all_gather | solution.py:129
  6.5 1.0 copy-start.3
  7.5 1.0 copy-start.4
  25.3 6.0 %collective-permute-start = (f32[12,3072]{1,0:T(8,128)S(1)}, f32[12,3072]{1,0:T(8,128)S(1)}, u32[]{:S(2)}, u32[]{:S(2)}) collective-permute-start(f32[12,3072]{1,0:T(8,128)S(1)} %get-tuple-element.20), channel_id=1, source_target_pairs={{0,32},{32,0},{1,33},{33,1},{2,34},{34,2},{3,35},{35,3},{4,36},{36... | collective-permute-start | bytes 442376 | tf_op jit(solution)/shard_map/ppermute | solution.py:127
  31.2 1.7 %copy-start.2 = (f32[768,768]{1,0:T(8,128)S(1)}, f32[768,768]{1,0:T(8,128)}, u32[]{:S(2)}) copy-start(f32[768,768]{1,0:T(8,128)} %constant.57.clone.order_ref) | copy-start | bytes 7077892
  37.9 4.8 %copy-start.7 = (s32[4]{0:T(128)S(1)}, s32[4]{0:T(128)}, u32[]{:S(2)}) copy-start(s32[4]{0:T(128)} %param.11) | copy-start | bytes 52
  37.9 7.4 %copy-start.5 = (f32[150]{0:T(256)S(1)}, f32[150]{0:T(256)}, u32[]{:S(2)}) copy-start(f32[150]{0:T(256)} %param.9) | copy-start | bytes 1804
  37.9 8.0 %copy-start.8 = (s32[4]{0:T(128)S(1)}, s32[4]{0:T(128)}, u32[]{:S(2)}) copy-start(s32[4]{0:T(128)} %param.12) | copy-start | bytes 52
  37.9 8.7 %copy-start.6 = (f32[1536]{0:T(1024)S(1)}, f32[1536]{0:T(1024)}, u32[]{:S(2)}) copy-start(f32[1536]{0:T(1024)} %param.10) | copy-start | bytes 18436
  37.9 75.6 %all-to-all-start = ((f32[16,24,3072]{2,1,0:T(8,128)}), f32[16,24,3072]{2,1,0:T(8,128)}, u32[]{:S(2)}, u32[]{:S(2)}) async-start(f32[16,24,3072]{2,1,0:T(8,128)} %spread.1), calls=%async_computation | async-start | bytes 9437184 | tf_op jit(solution)/shard_map/all_to_all | solution.py:144
  117.9 1.4 copy-start
  119.3 1.7 %copy-start.1 = (bf16[384,3072]{1,0:T(8,128)(2,1)S(1)}, bf16[384,3072]{1,0:T(8,128)(2,1)}, u32[]{:S(2)}) copy-start(bf16[384,3072]{1,0:T(8,128)(2,1)} %copy-done) | copy-start | bytes 7077892
  129.0 19.2 %all-to-all-start.2 = ((f32[32,36,128]{2,1,0:T(8,128)}), f32[32,36,128]{2,1,0:T(8,128)S(1)}, u32[]{:S(2)}, u32[]{:S(2)}) async-start(f32[32,36,128]{2,1,0:T(8,128)} %product.1), calls=%async_computation.2 | async-start | bytes 1310720 | tf_op jit(solution)/shard_map/all_to_all | solution.py:178
Sparse Core Ops, SparseCore 0:
  25.4 74.5 all-gather.1

commit v3 on v2

v3 whole, which is shorter than its diff:
```python
import jax
import jax.numpy as jnp
import numpy as np
from jax import lax
from jax.experimental import pallas as pl
from jax.experimental.pallas import tpu as pltpu
from jax.sharding import Mesh, PartitionSpec as P

AXES = ("zlo", "core", "y", "x", "zhi")
SIZES = (8, 2, 4, 4, 2)
PLANE = ("y", "x")
RING = ("zhi", "zlo")
VIRT = 1536
OCC_WIN = 4
ROWS = 12
WIDE = 384
HALF = 3072
STEP = 512
VMEM = pl.BlockSpec(memory_space=pltpu.VMEM)


def params(mib):
    return pltpu.CompilerParams(vmem_limit_bytes=mib * 1024 * 1024)


def cost(flops, moved):
    return pl.CostEstimate(flops=flops, bytes_accessed=moved, transcendentals=0)


def column_source():
    return np.arange(768, dtype=np.int32).reshape(2, 16, 2, 12).transpose(2, 0, 1, 3).reshape(1, 768)


def blocks_kernel(b_ref, out_ref, sems):
    copies = [
        pltpu.make_async_copy(b_ref.at[:, WIDE * i : WIDE * i + WIDE], out_ref.at[i], sems.at[i])
        for i in range(16)
    ]
    for copy in copies:
        copy.start()
    for copy in copies:
        copy.wait()


def halves_kernel(core_ref, a_ref, own_ref, other_ref, sems):
    core = core_ref[0]
    copies = []
    for z in range(8):
        at = slice(WIDE * z, WIDE * z + WIDE)
        near = pl.ds(pl.multiple_of(768 * z + WIDE * core, 128), WIDE)
        far = pl.ds(pl.multiple_of(768 * z + WIDE - WIDE * core, 128), WIDE)
        copies.append(pltpu.make_async_copy(a_ref.at[:, far], other_ref.at[:, at], sems.at[z]))
        copies.append(pltpu.make_async_copy(a_ref.at[:, near], own_ref.at[:, at], sems.at[8 + z]))
    for copy in copies:
        copy.start()
    for copy in copies:
        copy.wait()


def spread_kernel(core_ref, own_ref, other_ref, source_ref, out_ref):
    first = core_ref[0] == 0
    own, other = own_ref[...], other_ref[...]
    upper, lower = jnp.where(first, own, other), jnp.where(first, other, own)
    x = jnp.concatenate([upper, lower], axis=0)
    parts = []
    for _ in range(3):
        part = x.astype(jnp.bfloat16)
        x = x - part.astype(jnp.float32)
        parts += [part[:, 768 * q : 768 * q + 768] for q in range(4)]
    parts = jnp.concatenate(parts, axis=0)
    wanted = lax.broadcasted_iota(jnp.int32, (768, 768), 0) == source_ref[...]
    order = jnp.where(wanted, 1.0, 0.0).astype(jnp.bfloat16)
    moved = jnp.dot(parts, order, preferred_element_type=jnp.float32)
    for q in range(4):
        rows = [moved[24 * (4 * p + q) : 24 * (4 * p + q) + 24] for p in range(3)]
        total = (rows[0] + rows[1]) + rows[2]
        for i in range(16):
            for zhi in range(2):
                at = 1536 * zhi + WIDE * q
                out_ref[i, :, at : at + WIDE] = total[:, WIDE * zhi : WIDE * zhi + WIDE]


def in_two(x):
    high = x.astype(jnp.bfloat16)
    return high, (x - high.astype(jnp.float32)).astype(jnp.bfloat16)


def split_kernel(x_ref, high_ref, low_ref):
    high_ref[...], low_ref[...] = in_two(x_ref[...])


def product_kernel(high_ref, low_ref, panel_ref, out_ref, highs, lows, panels, total_ref, sems):
    steps = HALF // STEP
    copies = []
    for k in range(steps):
        at = pl.ds(STEP * k, STEP)
        copies.append(
            [
                pltpu.make_async_copy(panel_ref.at[at], panels.at[k], sems.at[0, k]),
                pltpu.make_async_copy(high_ref.at[:, at], highs.at[k], sems.at[1, k]),
                pltpu.make_async_copy(low_ref.at[:, at], lows.at[k], sems.at[2, k]),
            ]
        )
        for copy in copies[k]:
            copy.start()
    for k in range(steps):
        for copy in copies[k]:
            copy.wait()
        a_high, a_low = highs[k], lows[k]
        b_high, b_low = in_two(panels[k])
        term = jnp.dot(
            jnp.concatenate([a_high, a_low, a_high], axis=1),
            jnp.concatenate([b_high, b_high, b_low], axis=0),
            preferred_element_type=jnp.float32,
        )
        if k == 0:
            total_ref[...] = term
        else:
            total_ref[...] += term
    for d in range(32):
        for g in range(3):
            out_ref[d, ROWS * g : ROWS * g + ROWS, :] = total_ref[
                ROWS * d : ROWS * d + ROWS, 128 * g : 128 * g + 128
            ]


def shifts_kernel(place_ref, wi_ref, wj_ref, occ_ref, virt_ref, lanes_ref, row_ref, col_ref):
    place = place_ref[0]
    per_orbital = VIRT // ROWS
    occ_i = occ_ref[wi_ref[place // per_orbital]]
    start = lax.rem(place, per_orbital) * ROWS
    at = lax.broadcasted_iota(jnp.int32, (ROWS, 128), 0)
    row = jnp.zeros((ROWS, 128), jnp.float32)
    for r in range(ROWS):
        row = jnp.where(at == r, occ_i - virt_ref[start + r], row)
    row_ref[...] = row
    for j in range(OCC_WIN):
        col_ref[:, VIRT * j : VIRT * j + VIRT] = occ_ref[wj_ref[j]] - lanes_ref[...]


def divide_kernel(parts_ref, row_ref, col_ref, out_ref):
    row = row_ref[...]
    for i in range(16):
        for g in range(3):
            at = slice(ROWS * g, ROWS * g + ROWS)
            lanes = slice(WIDE * i + 128 * g, WIDE * i + 128 * g + 128)
            cycle = parts_ref[2 * i, at, :] + parts_ref[2 * i + 1, at, :]
            out_ref[:, lanes] = cycle / (row + col_ref[:, lanes])


def per_device(amplitudes, integrals, occupied_energy, virtual_energy, window_i, window_j):
    f32 = jnp.float32
    place = lax.axis_index(AXES).reshape(1)
    core = lax.axis_index("core").reshape(1)
    place, core, integrals = lax.optimization_barrier((place, core, integrals))
    smem = pl.BlockSpec(memory_space=pltpu.SMEM)
    hbm = pl.BlockSpec(memory_space=pltpu.HBM)
    blocks = pl.pallas_call(
        blocks_kernel,
        out_shape=jax.ShapeDtypeStruct((16, ROWS, WIDE), f32),
        in_specs=[hbm],
        out_specs=VMEM,
        scratch_shapes=[pltpu.SemaphoreType.DMA((16,))],
        compiler_params=params(4),
        cost_estimate=cost(1, 1 << 20),
        name="blocks",
    )(integrals)
    blocks = lax.all_to_all(blocks, PLANE, split_axis=0, concat_axis=0, tiled=True)
    panel = lax.all_gather(blocks.reshape(16 * ROWS, WIDE), RING, axis=0, tiled=True)

    own, other = pl.pallas_call(
        halves_kernel,
        out_shape=[jax.ShapeDtypeStruct((ROWS, HALF), f32)] * 2,
        in_specs=[smem, hbm],
        out_specs=[VMEM] * 2,
        scratch_shapes=[pltpu.SemaphoreType.DMA((16,))],
        compiler_params=params(4),
        cost_estimate=cost(1, 1 << 20),
        name="halves",
    )(core, amplitudes)
    other = lax.ppermute(other, "core", [(0, 1), (1, 0)])
    spread = pl.pallas_call(
        spread_kernel,
        out_shape=jax.ShapeDtypeStruct((16, 2 * ROWS, HALF), f32),
        in_specs=[smem, VMEM, VMEM, VMEM],
        out_specs=VMEM,
        compiler_params=params(12),
        cost_estimate=cost(2 * 24 * 3 * HALF * 768, 7 << 20),
        name="spread",
    )(core, own, other, jnp.asarray(column_source()))
    left = lax.all_to_all(spread, PLANE, split_axis=0, concat_axis=0, tiled=True)
    left = left.reshape(WIDE, HALF)

    left, place, window_i, window_j, occupied_energy, virtual_energy = lax.optimization_barrier(
        (left, place, window_i, window_j, occupied_energy, virtual_energy)
    )
    row, col = pl.pallas_call(
        shifts_kernel,
        out_shape=[
            jax.ShapeDtypeStruct((ROWS, 128), f32),
            jax.ShapeDtypeStruct((1, OCC_WIN * VIRT), f32),
        ],
        in_specs=[smem] * 5 + [VMEM],
        out_specs=[VMEM] * 2,
        compiler_params=params(2),
        cost_estimate=cost(1, 1 << 16),
        name="shifts",
    )(place, window_i, window_j, occupied_energy, virtual_energy, virtual_energy[None, :])
    tile = pl.BlockSpec((WIDE, STEP), lambda k: (0, k))
    high, low = pl.pallas_call(
        split_kernel,
        grid=(HALF // STEP,),
        out_shape=[jax.ShapeDtypeStruct((WIDE, HALF), jnp.bfloat16)] * 2,
        in_specs=[tile],
        out_specs=[tile, tile],
        compiler_params=params(8),
        cost_estimate=cost(4 * WIDE * HALF, 8 * WIDE * HALF),
        name="split",
    )(left)
    high, low, row, col = lax.optimization_barrier((high, low, row, col))
    steps = HALF // STEP
    partial = pl.pallas_call(
        product_kernel,
        out_shape=jax.ShapeDtypeStruct((32, 3 * ROWS, 128), f32),
        in_specs=[hbm] * 3,
        out_specs=VMEM,
        scratch_shapes=[
            pltpu.VMEM((steps, WIDE, STEP), jnp.bfloat16),
            pltpu.VMEM((steps, WIDE, STEP), jnp.bfloat16),
            pltpu.VMEM((steps, STEP, WIDE), f32),
            pltpu.VMEM((WIDE, WIDE), f32),
            pltpu.SemaphoreType.DMA((3, steps)),
        ],
        compiler_params=params(56),
        cost_estimate=cost(6 * WIDE * WIDE * HALF, 8 * WIDE * HALF),
        name="product",
    )(high, low, panel)
    parts = lax.all_to_all(partial, ("y", "x", "core"), split_axis=0, concat_axis=0, tiled=True)
    return pl.pallas_call(
        divide_kernel,
        out_shape=jax.ShapeDtypeStruct((ROWS, 16 * WIDE), f32),
        in_specs=[VMEM] * 3,
        out_specs=VMEM,
        compiler_params=params(6),
        cost_estimate=cost(4 * ROWS * 16 * WIDE, 1 << 20),
        name="divide",
    )(parts, row, col)


def solution(mesh):
    fine = Mesh(mesh.devices.reshape(SIZES), AXES)
    split = P(AXES, None)
    return jax.shard_map(
        per_device,
        mesh=fine,
        in_specs=(split, split, P(), P(), P(), P()),
        out_specs=split,
        check_vma=False,
    )
```

time: 157 us -> 142 us (0.904)
  blocking collectives: 15.9 us -> 103 us
  waiting for transfers between devices: 80 us -> 2.86 us
  starting transfers between devices: 15.9 us -> 4.9 us
  Pallas kernels: 18.4 us -> 11.4 us
  local copies, waits for them, and re-layouts: 9.59 us -> 6.36 us
  between operations: 15.4 us -> 13.5 us
    all_to_all x0 -> x2, blocking collectives: none -> 86.9 us  [the longest x1 58.5 us: per_device(): lax.all_to_all(spread, PLANE, split_axis=0, concat_axis=0, tiled=True)]
    all_to_all x2 -> x0, waiting for transfers between devices: 78.9 us -> none  [the longest x1 66.1 us: per_device(): lax.all_to_all(spread, PLANE, split_axis=0, concat_axis=0, tiled=True)]
    all_to_all x2 -> x0, starting transfers between devices: 11 us -> none  [the longest x1 6.28 us: per_device(): lax.all_to_all(partial, ('y', 'x', 'core'), split_axis=0, concat_axis=0,...]
    pallas_call x1, Pallas kernels: 5.06 us -> 1 us  [per_device(): pl.pallas_call(spread_kernel, out_shape=jax.ShapeDtypeStruct((16, 2 * ROW...]
    pallas_call x1, Pallas kernels: 4.36 us -> 1.58 us  [per_device(): pl.pallas_call(split_kernel, grid=(HALF // STEP,), out_shape=[jax.ShapeDt...]
    all_gather x1, waiting for transfers between devices: 0.01 us -> 1.8 us  [per_device(): lax.all_gather(blocks.reshape(16 * ROWS, WIDE), RING, axis=0, tiled=True)]
    unnamed x19 -> x18, local copies, waits for them, and re-layouts: 6.8 us -> 5.61 us
    pallas_call x2 -> x4, Pallas kernels: 8.05 us -> 7.99 us  [the longest x1 6.48 us: per_device(): pl.pallas_call(product_kernel, out_shape=jax.ShapeDtypeStruct((32, 3 * RO...]
  transfers between devices with their start and end apart: 4 -> 2, of which waited for: 3 -> 2; matrix products, arithmetic and copies ran while one was open for 2% -> 0% of each run, Pallas kernels for 6% -> 3%
where the time goes in v3:
time: 142 us
  blocking collectives  103 us (73%)
  between operations  13.5 us (10%)
  Pallas kernels  11.4 us (8%)
  local copies, waits for them, and re-layouts  6.36 us (4%)
  starting transfers between devices  4.9 us (3%)
  waiting for transfers between devices  2.86 us (2%)
    all_to_all x1, blocking collectives, per_device(): lax.all_to_all(spread, PLANE, split_axis=0, concat_axis=0, tiled=True)  58.5 us
    all_to_all x1, blocking collectives, per_device(): lax.all_to_all(partial, ('y', 'x', 'core'), split_axis=0, concat_axis=0,...  28.4 us
    all_to_all x1, blocking collectives, per_device(): lax.all_to_all(blocks, PLANE, split_axis=0, concat_axis=0, tiled=True)  15.9 us
    pallas_call x1, Pallas kernels, per_device(): pl.pallas_call(product_kernel, out_shape=jax.ShapeDtypeStruct((32, 3 * RO...  6.48 us
    unnamed x18, local copies, waits for them, and re-layouts  5.61 us
    ppermute x1, starting transfers between devices, per_device(): other = lax.ppermute(other, 'core', [(0, 1), (1, 0)])  4.9 us
  transfers between devices with their start and end apart: 2, of which 2 were waited for; matrix products, arithmetic and copies ran while one was open for 0% of the time, Pallas kernels for 3%

profile of v3, /device:TPU:1, one launch (start us, length us, event | category | flops | bytes accessed | tf_op | source)
XLA Modules:
  0.0 141.8 jit_solution(13044505964574956175)
XLA Ops:
  6.5 0.0 all-gather.2.cloned.1.call-start
  6.5 0.0 copy-start.2
  6.5 1.0 copy-done.2
  7.5 0.4 blocks.1
  8.0 15.9 %all_to_all.15 = f32[16,12,384]{2,1,0:T(8,128)S(1)} all-to-all(f32[16,12,384]{2,1,0:T(8,128)S(1)} %blocks.1), channel_id=1, replica_groups=mesh['zlo'=8,'core'=2,'y'=4,'x'=4,'zhi'=2] {'y','x'}, dimensions={0} | all-to-all | bytes 589824 | tf_op jit(solution)/shard_map/all_to_all | solution.py:168
  23.8 0.7 reshape.15
  24.6 0.0 all-gather.2.cloned.1.call-update
  24.6 0.0 copy-start.3
  24.6 1.0 copy-done.3
  25.6 0.4 halves.1
  26.0 4.9 %collective-permute-start = (f32[12,3072]{1,0:T(8,128)S(1)}, f32[12,3072]{1,0:T(8,128)S(1)}, u32[]{:S(2)}, u32[]{:S(2)}) collective-permute-start(f32[12,3072]{1,0:T(8,128)S(1)} %get-tuple-element.26), channel_id=1, source_target_pairs={{0,32},{32,0},{1,33},{33,1},{2,34},{34,2},{3,35},{35,3},{4,36},{36... | collective-permute-start | bytes 442376 | tf_op jit(solution)/shard_map/ppermute | solution.py:181
  30.9 1.0 collective-permute-done.other_ref
  32.0 0.7 copy-done.5
  32.7 1.0 spread.1
  33.7 0.0 copy-start.4
  33.7 0.0 copy-start.6
  33.7 0.0 copy-start.7
  33.7 0.0 copy-start.8
  33.7 58.5 %all_to_all.16 = f32[16,24,3072]{2,1,0:T(8,128)S(1)} all-to-all(f32[16,24,3072]{2,1,0:T(8,128)S(1)} %spread.1), channel_id=1, replica_groups=mesh['zlo'=8,'core'=2,'y'=4,'x'=4,'zhi'=2] {'y','x'}, dimensions={0} | all-to-all | bytes 9437184 | tf_op jit(solution)/shard_map/all_to_all | solution.py:191
  92.2 0.0 copy-done.4
  92.3 0.0 copy-done.6
  92.3 0.0 copy-done.7
  92.3 0.0 copy-done.8
  92.3 0.7 shifts.1
  93.0 1.6 %split.1 = (bf16[384,3072]{1,0:T(8,128)(2,1)S(1)}, bf16[384,3072]{1,0:T(8,128)(2,1)S(1)}) custom-call(f32[384,3072]{1,0:T(8,128)S(1)} %bitcast.3), custom_call_target="tpu_custom_call" | custom-call | flops 4718592 | bytes 9437184 | tf_op jit(solution)/shard_map/split/pallas_call | solution.py:210
  94.6 0.0 copy-start
  94.6 1.4 %copy-done = bf16[384,3072]{1,0:T(8,128)(2,1)} copy-done((bf16[384,3072]{1,0:T(8,128)(2,1)}, bf16[384,3072]{1,0:T(8,128)(2,1)S(1)}, u32[]{:S(2)}) %copy-start) | copy-done | bytes 2359320
  96.0 1.5 %copy-done.1 = bf16[384,3072]{1,0:T(8,128)(2,1)} copy-done((bf16[384,3072]{1,0:T(8,128)(2,1)}, bf16[384,3072]{1,0:T(8,128)(2,1)S(1)}, u32[]{:S(2)}) %copy-start.1) | copy-done | bytes 2359320
  97.5 1.8 %all-gather.2.cloned.1.call-done.panel_ref = f32[3072,384]{1,0:T(8,128)} async-done(((f32[192,384]{1,0:T(8,128)}), f32[3072,384]{1,0:T(8,128)}) %all-gather.2.cloned.1.call-update) | async-done | bytes 4718608 | tf_op jit(solution)/shard_map/all_gather | solution.py:169
  99.3 6.5 %product.1 = f32[32,36,128]{2,1,0:T(8,128)} custom-call(bf16[384,3072]{1,0:T(8,128)(2,1)} %copy-done, bf16[384,3072]{1,0:T(8,128)(2,1)} %copy-done.1, f32[3072,384]{1,0:T(8,128)} %all-gather.2.cloned.1.call-done.panel_ref), custom_call_target="tpu_custom_call" | custom-call | flops 2717908992 | bytes 9437184 | tf_op jit(solution)/shard_map/product/pallas_call | solution.py:222
  105.8 28.4 %all_to_all.17.parts_ref = f32[32,36,128]{2,1,0:T(8,128)S(1)} all-to-all(f32[32,36,128]{2,1,0:T(8,128)} %product.1), channel_id=1, replica_groups=mesh['zlo'=8,'core'=2,'y'=4,'x'=4,'zhi'=2] {'y','x','core'}, dimensions={0} | all-to-all | bytes 1179648 | tf_op jit(solution)/shard_map/all_to_all | solution.py:238
  134.2 0.8 divide.1
  (3 shorter events, 0.0 us)
Async XLA Ops:
  6.5 92.7 %all-gather.2.cloned.1.call-start = ((), (), s32[]{:S(2)}) async-start(), calls=%async_computation.3 | async-start | bytes 5013504 | tf_op jit(solution)/shard_map/all_gather | solution.py:169
  6.5 1.0 copy-start.2
  24.6 1.0 copy-start.3
  26.0 6.0 %collective-permute-start = (f32[12,3072]{1,0:T(8,128)S(1)}, f32[12,3072]{1,0:T(8,128)S(1)}, u32[]{:S(2)}, u32[]{:S(2)}) collective-permute-start(f32[12,3072]{1,0:T(8,128)S(1)} %get-tuple-element.26), channel_id=1, source_target_pairs={{0,32},{32,0},{1,33},{33,1},{2,34},{34,2},{3,35},{35,3},{4,36},{36... | collective-permute-start | bytes 442376 | tf_op jit(solution)/shard_map/ppermute | solution.py:181
  32.0 0.7 copy-start.5
  33.7 58.6 %copy-start.4 = (f32[1536]{0:T(1024)S(1)}, f32[1536]{0:T(1024)}, u32[]{:S(2)}) copy-start(f32[1536]{0:T(1024)} %virt_ref) | copy-start | bytes 18436
  33.7 58.6 %copy-start.6 = (f32[150]{0:T(256)S(1)}, f32[150]{0:T(256)}, u32[]{:S(2)}) copy-start(f32[150]{0:T(256)} %occ_ref) | copy-start | bytes 1804
  33.7 58.5 %copy-start.7 = (s32[4]{0:T(128)S(1)}, s32[4]{0:T(128)}, u32[]{:S(2)}) copy-start(s32[4]{0:T(128)} %wi_ref) | copy-start | bytes 52
  33.7 58.5 %copy-start.8 = (s32[4]{0:T(128)S(1)}, s32[4]{0:T(128)}, u32[]{:S(2)}) copy-start(s32[4]{0:T(128)} %wj_ref) | copy-start | bytes 52
  94.6 1.4 %copy-start = (bf16[384,3072]{1,0:T(8,128)(2,1)}, bf16[384,3072]{1,0:T(8,128)(2,1)S(1)}, u32[]{:S(2)}) copy-start(bf16[384,3072]{1,0:T(8,128)(2,1)S(1)} %get-tuple-element.38.high_ref) | copy-start | bytes 7077892
  96.0 1.5 %copy-start.1 = (bf16[384,3072]{1,0:T(8,128)(2,1)}, bf16[384,3072]{1,0:T(8,128)(2,1)S(1)}, u32[]{:S(2)}) copy-start(bf16[384,3072]{1,0:T(8,128)(2,1)S(1)} %get-tuple-element.39.low_ref) | copy-start | bytes 7077892
Sparse Core Ops, SparseCore 0:
  24.7 74.5 all-gather.1

commit v4 on v0

v4 whole, which is shorter than its diff:
```python
import jax
import jax.numpy as jnp
import numpy as np
from jax import lax
from jax.experimental import pallas as pl
from jax.experimental.pallas import tpu as pltpu
from jax.sharding import Mesh, PartitionSpec as P

AXES = ("zl4", "zb", "core", "y", "x", "zhi")
SIZES = (4, 2, 2, 4, 4, 2)
PLANE = ("y", "x")
VIRT = 1536
OCC_WIN = 4
ROWS = 12
WIDE = 384
SHARD = 16 * ROWS
DEEP = 8 * SHARD
STEP = 512
VMEM = pl.BlockSpec(memory_space=pltpu.VMEM)
SMEM = pl.BlockSpec(memory_space=pltpu.SMEM)
HBM = pl.BlockSpec(memory_space=pltpu.HBM)
F32 = jnp.float32
BF16 = jnp.bfloat16


def call(body, name, out, ins, outs, mib, flops, moved, scratch=(), grid=None):
    return pl.pallas_call(
        body,
        out_shape=out,
        in_specs=ins,
        out_specs=outs,
        scratch_shapes=scratch,
        compiler_params=pltpu.CompilerParams(vmem_limit_bytes=mib * 1024 * 1024),
        cost_estimate=pl.CostEstimate(flops=flops, bytes_accessed=moved, transcendentals=0),
        name=name,
    )


def shape(*dims, dtype=F32):
    return jax.ShapeDtypeStruct(dims, dtype)


def column_source():
    return np.arange(WIDE, dtype=np.int32).reshape(16, 2, ROWS).transpose(1, 0, 2).reshape(1, WIDE)


def in_two(x):
    high = x.astype(BF16)
    return high, (x - high.astype(F32)).astype(BF16)


def first_kernel(where_ref, a_ref, b_ref, own_ref, other_ref, blocks_ref):
    zb = where_ref[0]
    for z in range(4):
        at = slice(768 * z, 768 * z + 768)
        other_ref[:, at] = a_ref[:, pl.ds(pl.multiple_of(1536 * z + 768 - 768 * zb, 128), 768)]
        own_ref[:, at] = a_ref[:, pl.ds(pl.multiple_of(1536 * z + 768 * zb, 128), 768)]
    for i in range(16):
        blocks_ref[i] = b_ref[:, WIDE * i : WIDE * i + WIDE]


def spread_kernel(where_ref, own_ref, other_ref, source_ref, out_ref):
    first = where_ref[0] == 0
    own, other = own_ref[...], other_ref[...]
    upper, lower = jnp.where(first, own, other), jnp.where(first, other, own)
    x = jnp.concatenate([upper, lower], axis=0)
    parts = []
    for _ in range(3):
        part = x.astype(BF16)
        x = x - part.astype(F32)
        parts += [part[:, WIDE * q : WIDE * q + WIDE] for q in range(8)]
    parts = jnp.concatenate(parts, axis=0)
    wanted = lax.broadcasted_iota(jnp.int32, (WIDE, WIDE), 0) == source_ref[...]
    order = jnp.where(wanted, 1.0, 0.0).astype(BF16)
    moved = jnp.dot(parts, order, preferred_element_type=F32)
    for q in range(8):
        rows = [moved[24 * (8 * p + q) : 24 * (8 * p + q) + 24] for p in range(3)]
        total = (rows[0] + rows[1]) + rows[2]
        z, core = divmod(q, 2)
        for i in range(16):
            out_ref[16 * core + i, :, WIDE * z : WIDE * z + WIDE] = total


def place_kernel(where_ref, *refs):
    shards, high_ref, low_ref = refs[:-2], refs[-2], refs[-1]
    ring = where_ref[2]
    steps = [0, -1, 1, -2, 2, -3, 3, 4, 4]
    for i, step in enumerate(steps):
        at = lax.rem(ring + 8 + step, 8)
        row = (lax.rem(at, 4) * 2 + at // 4) * SHARD + (SHARD // 2 if i == 8 else 0)
        rows = pl.ds(pl.multiple_of(row, 32), shards[i].shape[0])
        high_ref[rows, :], low_ref[rows, :] = in_two(shards[i][...])


def product_kernel(mine, where_ref, left_ref, high_ref, low_ref, out_ref, chunks_ref, sems):
    half = where_ref[1] if mine else 1 - where_ref[1]
    copies = []
    for k in range(DEEP // STEP):
        source = left_ref.at[half, :, pl.ds(STEP * k, STEP)]
        copies.append(pltpu.make_async_copy(source, chunks_ref.at[k], sems.at[k]))
        copies[k].start()
    total = None
    for k, copy in enumerate(copies):
        copy.wait()
        a_high, a_low = in_two(chunks_ref[k])
        at = slice(STEP * k, STEP * k + STEP)
        b_high, b_low = high_ref[at, :], low_ref[at, :]
        term = jnp.dot(
            jnp.concatenate([a_high, a_low, a_high], axis=1),
            jnp.concatenate([b_high, b_high, b_low], axis=0),
            preferred_element_type=F32,
        )
        total = term if total is None else total + term
    out_ref[...] = total


def pack_kernel(own_ref, other_ref, out_ref):
    for i in range(16):
        for zb in range(2):
            rows = slice(24 * i + ROWS * zb, 24 * i + ROWS * zb + ROWS)
            total = own_ref[rows, :] + other_ref[rows, :]
            for g in range(3):
                at = slice(ROWS * g, ROWS * g + ROWS)
                out_ref[16 * zb + i, at, :] = total[:, 128 * g : 128 * g + 128]


def shifts_kernel(where_ref, wi_ref, wj_ref, occ_ref, virt_ref, lanes_ref, row_ref, col_ref):
    place = where_ref[3]
    per_orbital = VIRT // ROWS
    occ_i = occ_ref[wi_ref[place // per_orbital]]
    start = lax.rem(place, per_orbital) * ROWS
    at = lax.broadcasted_iota(jnp.int32, (ROWS, 128), 0)
    row = jnp.zeros((ROWS, 128), F32)
    for r in range(ROWS):
        row = jnp.where(at == r, occ_i - virt_ref[start + r], row)
    row_ref[...] = row
    for j in range(OCC_WIN):
        col_ref[:, VIRT * j : VIRT * j + VIRT] = occ_ref[wj_ref[j]] - lanes_ref[...]


def divide_kernel(parts_ref, row_ref, col_ref, out_ref):
    row = row_ref[...]
    for i in range(16):
        for g in range(3):
            at = slice(ROWS * g, ROWS * g + ROWS)
            lanes = slice(WIDE * i + 128 * g, WIDE * i + 128 * g + 128)
            cycle = parts_ref[i, at, :] + parts_ref[16 + i, at, :]
            out_ref[:, lanes] = cycle / (row + col_ref[:, lanes])


def turn(x, step):
    index = lambda a: (a % 8 % 4) * 2 + a % 8 // 4
    return lax.ppermute(x, ("zl4", "zhi"), [(index(a), index(a + step)) for a in range(8)])


def per_device(amplitudes, integrals, occupied_energy, virtual_energy, window_i, window_j):
    swap = [(0, 1), (1, 0)]
    axis = lax.axis_index
    where = jnp.stack([axis("zb"), axis("core"), axis("zhi") * 4 + axis("zl4"), axis(AXES)])
    own, other, blocks = call(
        first_kernel,
        "first",
        [shape(ROWS, 3072), shape(ROWS, 3072), shape(16, ROWS, WIDE)],
        [SMEM, VMEM, VMEM],
        [VMEM] * 3,
        4,
        1,
        2 << 20,
    )(where, amplitudes, integrals)
    other = lax.ppermute(other, "zb", swap)
    blocks = lax.all_to_all(blocks, PLANE, split_axis=0, concat_axis=0, tiled=True)
    shard = blocks.reshape(SHARD, WIDE)

    shards, right, left = [shard], shard, shard
    for _ in range(3):
        right, left = turn(right, 1), turn(left, -1)
        shards += [right, left]
    shards += [turn(right[: SHARD // 2], 1), turn(left[SHARD // 2 :], -1)]

    spread = call(
        spread_kernel,
        "spread",
        shape(32, 2 * ROWS, DEEP),
        [SMEM, VMEM, VMEM, VMEM],
        VMEM,
        14,
        2 * 576 * WIDE * WIDE,
        6 << 20,
    )(where, own, other, jnp.asarray(column_source()))
    rows = lax.all_to_all(spread, ("core", "y", "x"), split_axis=0, concat_axis=0, tiled=True)
    rows = rows.reshape(2, WIDE, DEEP)

    row, col = call(
        shifts_kernel,
        "shifts",
        [shape(ROWS, 128), shape(1, OCC_WIN * VIRT)],
        [SMEM] * 5 + [VMEM],
        [VMEM] * 2,
        2,
        1,
        1 << 16,
    )(where, window_i, window_j, occupied_energy, virtual_energy, virtual_energy[None, :])
    high, low = call(
        place_kernel,
        "place",
        [shape(DEEP, WIDE, dtype=BF16)] * 2,
        [SMEM] + [VMEM] * 9,
        [VMEM] * 2,
        10,
        4 * DEEP * WIDE,
        8 * DEEP * WIDE,
    )(where, *shards)
    high, low, row, col = lax.optimization_barrier((high, low, row, col))

    def product(mine):
        return call(
            lambda *refs: product_kernel(mine, *refs),
            "product_own" if mine else "product_other",
            shape(WIDE, WIDE),
            [SMEM, HBM, VMEM, VMEM],
            VMEM,
            16,
            6 * WIDE * WIDE * DEEP,
            8 * WIDE * DEEP,
            [pltpu.VMEM((DEEP // STEP, WIDE, STEP), F32), pltpu.SemaphoreType.DMA((DEEP // STEP,))],
        )(where, rows, high, low)

    theirs = lax.ppermute(product(False), "core", swap)
    packed = call(
        pack_kernel,
        "pack",
        shape(32, 3 * ROWS, 128),
        [VMEM] * 2,
        VMEM,
        6,
        WIDE * WIDE,
        12 * WIDE * WIDE,
    )(product(True), theirs)
    parts = lax.all_to_all(packed, ("zb", "y", "x"), split_axis=0, concat_axis=0, tiled=True)
    return call(
        divide_kernel,
        "divide",
        shape(ROWS, 16 * WIDE),
        [VMEM] * 3,
        VMEM,
        6,
        4 * ROWS * 16 * WIDE,
        1 << 20,
    )(parts, row, col)


def solution(mesh):
    fine = Mesh(mesh.devices.reshape(SIZES), AXES)
    split = P(AXES, None)
    return jax.shard_map(
        per_device,
        mesh=fine,
        in_specs=(split, split, P(), P(), P(), P()),
        out_specs=split,
        check_vma=False,
    )
```

time: 514 us -> 136 us (0.26)
  the two profiles are of different devices: /device:TPU:97 before, /device:TPU:1 now
where the time goes in v4:
time: 136 us; the launch traced here: 135 us
  starting transfers between devices  69.5 us (51%)
  waiting for transfers between devices  28.9 us (21%)
  blocking collectives  18.3 us (13%)
  Pallas kernels  13.3 us (10%)
  local copies, waits for them, and re-layouts  4.92 us (4%)
    ppermute x8, starting transfers between devices, turn(): lax.ppermute(x, ('zl4', 'zhi'), [(index(a), index(a + step)) for a in ran...  45 us
    ppermute x8, waiting for transfers between devices, turn(): lax.ppermute(x, ('zl4', 'zhi'), [(index(a), index(a + step)) for a in ran...  25.6 us
    all_to_all x1, blocking collectives, per_device(): lax.all_to_all(packed, ('zb', 'y', 'x'), split_axis=0, concat_axis=0, til...  18.3 us
    all_to_all x1, starting transfers between devices, per_device(): lax.all_to_all(spread, ('core', 'y', 'x'), split_axis=0, concat_axis=0, t...  10.9 us
    pallas_call x2, Pallas kernels, product(): call(lambda *refs: product_kernel(mine, *refs), 'product_own' if mine els...  7.97 us
    all_to_all x1, starting transfers between devices, per_device(): lax.all_to_all(blocks, PLANE, split_axis=0, concat_axis=0, tiled=True)  7.58 us
    unnamed x16, local copies, waits for them, and re-layouts  4.86 us
    ppermute x1, starting transfers between devices, per_device(): other = lax.ppermute(other, 'zb', swap)  3.55 us
  transfers between devices with their start and end apart: 12, of which 7 were waited for; matrix products, arithmetic and copies ran while one was open for 0% of the time, Pallas kernels for 5%

profile of v4, /device:TPU:1, one launch (start us, length us, event | category | flops | bytes accessed | tf_op | source)
XLA Modules:
  0.0 135.3 jit_solution(930504133917061854)
XLA Ops:
  0.1 1.0 copy-done.1
  1.1 1.0 copy-done.2
  2.1 1.3 first.1
  3.4 7.6 %all-to-all-start.1 = ((f32[16,12,384]{2,1,0:T(8,128)}), f32[16,12,384]{2,1,0:T(8,128)S(1)}, u32[]{:S(2)}, u32[]{:S(2)}) async-start(f32[16,12,384]{2,1,0:T(8,128)} %get-tuple-element.18), calls=%async_computation.1 | async-start | bytes 786432 | tf_op jit(solution)/shard_map/all_to_all | solution.py:171
  11.0 3.5 %collective-permute-start = (f32[12,3072]{1,0:T(8,128)S(1)}, f32[12,3072]{1,0:T(8,128)S(1)}, u32[]{:S(2)}, u32[]{:S(2)}) collective-permute-start(f32[12,3072]{1,0:T(8,128)S(1)} %get-tuple-element.17), channel_id=1, source_target_pairs={{0,64},{64,0},{1,65},{65,1},{2,66},{66,2},{3,67},{67,3},{4,68},{68... | collective-permute-start | bytes 442376 | tf_op jit(solution)/shard_map/ppermute | solution.py:170
  14.6 3.3 %collective-permute-done.other_ref = f32[12,3072]{1,0:T(8,128)S(1)} collective-permute-done((f32[12,3072]{1,0:T(8,128)S(1)}, f32[12,3072]{1,0:T(8,128)S(1)}, u32[]{:S(2)}, u32[]{:S(2)}) %collective-permute-start) | collective-permute-done | bytes 147488 | tf_op jit(solution)/shard_map/ppermute | solution.py:170
  17.9 0.7 copy-done.4
  18.6 1.4 %spread.1 = f32[32,24,1536]{2,1,0:T(8,128)S(1)} custom-call(s32[4]{0:T(128)S(1)} %pad_add_fusion.where_ref.refs_0_, f32[12,3072]{1,0:T(8,128)S(1)} %get-tuple-element.16.own_ref, f32[12,3072]{1,0:T(8,128)S(1)} %collective-permute-done.other_ref, s32[1,384]{1,0:T(1,128)S(1)} %copy-done.4), custom_call_target="tpu_custom_call" | custom-call | flops 169869312 | bytes 6291456 | tf_op jit(solution)/shard_map/spread/pallas_call | solution.py:180
  20.0 2.2 %copy-done = f32[32,24,1536]{2,1,0:T(8,128)} copy-done((f32[32,24,1536]{2,1,0:T(8,128)}, f32[32,24,1536]{2,1,0:T(8,128)S(1)}, u32[]{:S(2)}) %copy-start) | copy-done | bytes 4718616
  22.2 10.9 %all-to-all-start = ((f32[32,24,1536]{2,1,0:T(8,128)}), f32[32,24,1536]{2,1,0:T(8,128)}, u32[]{:S(2)}, u32[]{:S(2)}) async-start(f32[32,24,1536]{2,1,0:T(8,128)} %copy-done), calls=%async_computation | async-start | bytes 9437184 | tf_op jit(solution)/shard_map/all_to_all | solution.py:190
  33.2 3.7 %collective-permute-start.1 = (f32[192,384]{1,0:T(8,128)S(1)}, f32[192,384]{1,0:T(8,128)S(1)}, u32[]{:S(2)}, u32[]{:S(2)}) collective-permute-start(f32[192,384]{1,0:T(8,128)S(1)} %reshape.7.refs_0_), channel_id=1, source_target_pairs={{0,128},{128,256},{256,384},{384,1},{1,129},{129,257},{257,385},{3... | collective-permute-start | bytes 884744 | tf_op jit(solution)/shard_map/ppermute | solution.py:153
  36.8 8.4 %collective-permute-start.2 = (f32[192,384]{1,0:T(8,128)S(1)}, f32[192,384]{1,0:T(8,128)S(1)}, u32[]{:S(2)}, u32[]{:S(2)}) collective-permute-start(f32[192,384]{1,0:T(8,128)S(1)} %reshape.7.refs_0_), channel_id=1, source_target_pairs={{0,385},{128,0},{256,128},{384,256},{1,384},{129,1},{257,129},{385... | collective-permute-start | bytes 884744 | tf_op jit(solution)/shard_map/ppermute | solution.py:153
  45.2 7.4 %collective-permute-done.1.refs_1_ = f32[192,384]{1,0:T(8,128)S(1)} collective-permute-done((f32[192,384]{1,0:T(8,128)S(1)}, f32[192,384]{1,0:T(8,128)S(1)}, u32[]{:S(2)}, u32[]{:S(2)}) %collective-permute-start.1) | collective-permute-done | bytes 294944 | tf_op jit(solution)/shard_map/ppermute | solution.py:153
  52.7 2.6 %collective-permute-start.3 = (f32[192,384]{1,0:T(8,128)S(1)}, f32[192,384]{1,0:T(8,128)S(1)}, u32[]{:S(2)}, u32[]{:S(2)}) collective-permute-start(f32[192,384]{1,0:T(8,128)S(1)} %collective-permute-done.1.refs_1_), channel_id=1, source_target_pairs={{0,128},{128,256},{256,384},{384,1},{1,129},{129,257},{257,385},{3... | collective-permute-start | bytes 884744 | tf_op jit(solution)/shard_map/ppermute | solution.py:153
  55.3 1.0 collective-permute-done.2.refs_2_
  56.3 7.8 %collective-permute-start.4 = (f32[192,384]{1,0:T(8,128)S(1)}, f32[192,384]{1,0:T(8,128)S(1)}, u32[]{:S(2)}, u32[]{:S(2)}) collective-permute-start(f32[192,384]{1,0:T(8,128)S(1)} %collective-permute-done.2.refs_2_), channel_id=1, source_target_pairs={{0,385},{128,0},{256,128},{384,256},{1,384},{129,1},{257,129},{385... | collective-permute-start | bytes 884744 | tf_op jit(solution)/shard_map/ppermute | solution.py:153
  64.1 8.8 %collective-permute-start.5 = (f32[192,384]{1,0:T(8,128)S(1)}, f32[192,384]{1,0:T(8,128)S(1)}, u32[]{:S(2)}, u32[]{:S(2)}) collective-permute-start(f32[192,384]{1,0:T(8,128)S(1)} %collective-permute-done.3.refs_3_), channel_id=1, source_target_pairs={{0,128},{128,256},{256,384},{384,1},{1,129},{129,257},{257,385},{3... | collective-permute-start | bytes 884744 | tf_op jit(solution)/shard_map/ppermute | solution.py:153
  72.9 3.3 %collective-permute-done.4.refs_4_ = f32[192,384]{1,0:T(8,128)S(1)} collective-permute-done((f32[192,384]{1,0:T(8,128)S(1)}, f32[192,384]{1,0:T(8,128)S(1)}, u32[]{:S(2)}, u32[]{:S(2)}) %collective-permute-start.4) | collective-permute-done | bytes 294944 | tf_op jit(solution)/shard_map/ppermute | solution.py:153
  76.2 6.5 %collective-permute-start.6 = (f32[192,384]{1,0:T(8,128)S(1)}, f32[192,384]{1,0:T(8,128)S(1)}, u32[]{:S(2)}, u32[]{:S(2)}) collective-permute-start(f32[192,384]{1,0:T(8,128)S(1)} %collective-permute-done.4.refs_4_), channel_id=1, source_target_pairs={{0,385},{128,0},{256,128},{384,256},{1,384},{129,1},{257,129},{385... | collective-permute-start | bytes 884744 | tf_op jit(solution)/shard_map/ppermute | solution.py:153
  82.7 6.0 %collective-permute-done.5.refs_5_ = f32[192,384]{1,0:T(8,128)S(1)} collective-permute-done((f32[192,384]{1,0:T(8,128)S(1)}, f32[192,384]{1,0:T(8,128)S(1)}, u32[]{:S(2)}, u32[]{:S(2)}) %collective-permute-start.5) | collective-permute-done | bytes 294944 | tf_op jit(solution)/shard_map/ppermute | solution.py:153
  88.7 1.9 %collective-permute-start.7 = (f32[96,384]{1,0:T(8,128)S(1)}, f32[96,384]{1,0:T(8,128)S(1)}, u32[]{:S(2)}, u32[]{:S(2)}) collective-permute-start(f32[96,384]{1,0:T(8,128)S(1)} %slice.8), channel_id=1, source_target_pairs={{0,128},{128,256},{256,384},{384,1},{1,129},{129,257},{257,385},{3... | collective-permute-start | bytes 442376 | tf_op jit(solution)/shard_map/ppermute | solution.py:153
  90.6 2.6 %collective-permute-done.6.refs_6_ = f32[192,384]{1,0:T(8,128)S(1)} collective-permute-done((f32[192,384]{1,0:T(8,128)S(1)}, f32[192,384]{1,0:T(8,128)S(1)}, u32[]{:S(2)}, u32[]{:S(2)}) %collective-permute-start.6) | collective-permute-done | bytes 294944 | tf_op jit(solution)/shard_map/ppermute | solution.py:153
  93.2 5.4 %collective-permute-start.8 = (f32[96,384]{1,0:T(8,128)S(1)}, f32[96,384]{1,0:T(8,128)S(1)}, u32[]{:S(2)}, u32[]{:S(2)}) collective-permute-start(f32[96,384]{1,0:T(8,128)S(1)} %slice.9), channel_id=1, source_target_pairs={{0,385},{128,0},{256,128},{384,256},{1,384},{129,1},{257,129},{385... | collective-permute-start | bytes 442376 | tf_op jit(solution)/shard_map/ppermute | solution.py:153
  98.6 0.7 shifts.1
  99.4 5.3 %collective-permute-done.8.refs_8_ = f32[96,384]{1,0:T(8,128)S(1)} collective-permute-done((f32[96,384]{1,0:T(8,128)S(1)}, f32[96,384]{1,0:T(8,128)S(1)}, u32[]{:S(2)}, u32[]{:S(2)}) %collective-permute-start.8) | collective-permute-done | bytes 147488 | tf_op jit(solution)/shard_map/ppermute | solution.py:153
  104.6 1.0 place.1
  105.6 4.0 %product_other.1 = f32[384,384]{1,0:T(8,128)S(1)} custom-call(s32[4]{0:T(128)S(1)} %pad_add_fusion.where_ref.refs_0_, f32[2,384,1536]{2,1,0:T(8,128)} %bitcast.4.refs_1_, bf16[1536,384]{1,0:T(8,128)(2,1)S(1)} %get-tuple-element.23.refs_2_, bf16[1536,384]{1,0:T(8,128)(2,1)S(1)} %get-tuple-element.24.refs_3_), custom_call_target="tpu_custom_call" | custom-call | flops 1358954496 | bytes 4718592 | tf_op jit(solution)/shard_map/product_other/pallas_call | solution.py:216
  109.6 2.5 %collective-permute-start.9 = (f32[384,384]{1,0:T(8,128)S(1)}, f32[384,384]{1,0:T(8,128)S(1)}, u32[]{:S(2)}, u32[]{:S(2)}) collective-permute-start(f32[384,384]{1,0:T(8,128)S(1)} %product_other.1), channel_id=1, source_target_pairs={{0,32},{32,0},{1,33},{33,1},{2,34},{34,2},{3,35},{35,3},{4,36},{36... | collective-permute-start | bytes 1769480 | tf_op jit(solution)/shard_map/ppermute | solution.py:228
  112.1 4.0 %product_own.1.own_ref = f32[384,384]{1,0:T(8,128)S(1)} custom-call(s32[4]{0:T(128)S(1)} %pad_add_fusion.where_ref.refs_0_, f32[2,384,1536]{2,1,0:T(8,128)} %bitcast.4.refs_1_, bf16[1536,384]{1,0:T(8,128)(2,1)S(1)} %get-tuple-element.23.refs_2_, bf16[1536,384]{1,0:T(8,128)(2,1)S(1)} %get-tuple-element.24.refs_3_), custom_call_target="tpu_custom_call" | custom-call | flops 1358954496 | bytes 4718592 | tf_op jit(solution)/shard_map/product_own/pallas_call | solution.py:216
  116.1 0.1 pack.1
  116.2 18.3 %all_to_all.15.parts_ref = f32[32,36,128]{2,1,0:T(8,128)S(1)} all-to-all(f32[32,36,128]{2,1,0:T(8,128)S(1)} %pack.1), channel_id=1, replica_groups=mesh['zl4'=4,'zb'=2,'core'=2,'y'=4,'x'=4,'zhi'=2] {'zb','y','x'}, dimensions={0} | all-to-all | bytes 1179648 | tf_op jit(solution)/shard_map/all_to_all | solution.py:239
  134.5 0.8 divide.1
  (22 shorter events, 0.2 us)
Async XLA Ops:
  0.1 1.0 copy-start.1
  1.1 1.0 copy-start.2
  3.4 18.8 %all-to-all-start.1 = ((f32[16,12,384]{2,1,0:T(8,128)}), f32[16,12,384]{2,1,0:T(8,128)S(1)}, u32[]{:S(2)}, u32[]{:S(2)}) async-start(f32[16,12,384]{2,1,0:T(8,128)} %get-tuple-element.18), calls=%async_computation.1 | async-start | bytes 786432 | tf_op jit(solution)/shard_map/all_to_all | solution.py:171
  11.0 6.9 %collective-permute-start = (f32[12,3072]{1,0:T(8,128)S(1)}, f32[12,3072]{1,0:T(8,128)S(1)}, u32[]{:S(2)}, u32[]{:S(2)}) collective-permute-start(f32[12,3072]{1,0:T(8,128)S(1)} %get-tuple-element.17), channel_id=1, source_target_pairs={{0,64},{64,0},{1,65},{65,1},{2,66},{66,2},{3,67},{67,3},{4,68},{68... | collective-permute-start | bytes 442376 | tf_op jit(solution)/shard_map/ppermute | solution.py:170
  17.9 0.7 copy-start.4
  20.0 2.2 %copy-start = (f32[32,24,1536]{2,1,0:T(8,128)}, f32[32,24,1536]{2,1,0:T(8,128)S(1)}, u32[]{:S(2)}) copy-start(f32[32,24,1536]{2,1,0:T(8,128)S(1)} %spread.1) | copy-start | bytes 14155780
  22.2 76.4 %copy-start.3 = (f32[1536]{0:T(1024)S(1)}, f32[1536]{0:T(1024)}, u32[]{:S(2)}) copy-start(f32[1536]{0:T(1024)} %virt_ref.1) | copy-start | bytes 18436
  22.2 76.4 %copy-start.5 = (f32[150]{0:T(256)S(1)}, f32[150]{0:T(256)}, u32[]{:S(2)}) copy-start(f32[150]{0:T(256)} %occ_ref.1) | copy-start | bytes 1804
  22.2 76.4 %copy-start.6 = (s32[4]{0:T(128)S(1)}, s32[4]{0:T(128)}, u32[]{:S(2)}) copy-start(s32[4]{0:T(128)} %wi_ref.1) | copy-start | bytes 52
  22.2 76.5 %copy-start.7 = (s32[4]{0:T(128)S(1)}, s32[4]{0:T(128)}, u32[]{:S(2)}) copy-start(s32[4]{0:T(128)} %wj_ref.1) | copy-start | bytes 52
  22.2 83.4 %all-to-all-start = ((f32[32,24,1536]{2,1,0:T(8,128)}), f32[32,24,1536]{2,1,0:T(8,128)}, u32[]{:S(2)}, u32[]{:S(2)}) async-start(f32[32,24,1536]{2,1,0:T(8,128)} %copy-done), calls=%async_computation | async-start | bytes 9437184 | tf_op jit(solution)/shard_map/all_to_all | solution.py:190
  33.2 19.5 %collective-permute-start.1 = (f32[192,384]{1,0:T(8,128)S(1)}, f32[192,384]{1,0:T(8,128)S(1)}, u32[]{:S(2)}, u32[]{:S(2)}) collective-permute-start(f32[192,384]{1,0:T(8,128)S(1)} %reshape.7.refs_0_), channel_id=1, source_target_pairs={{0,128},{128,256},{256,384},{384,1},{1,129},{129,257},{257,385},{3... | collective-permute-start | bytes 884744 | tf_op jit(solution)/shard_map/ppermute | solution.py:153
  36.8 19.5 %collective-permute-start.2 = (f32[192,384]{1,0:T(8,128)S(1)}, f32[192,384]{1,0:T(8,128)S(1)}, u32[]{:S(2)}, u32[]{:S(2)}) collective-permute-start(f32[192,384]{1,0:T(8,128)S(1)} %reshape.7.refs_0_), channel_id=1, source_target_pairs={{0,385},{128,0},{256,128},{384,256},{1,384},{129,1},{257,129},{385... | collective-permute-start | bytes 884744 | tf_op jit(solution)/shard_map/ppermute | solution.py:153
  52.7 11.4 %collective-permute-start.3 = (f32[192,384]{1,0:T(8,128)S(1)}, f32[192,384]{1,0:T(8,128)S(1)}, u32[]{:S(2)}, u32[]{:S(2)}) collective-permute-start(f32[192,384]{1,0:T(8,128)S(1)} %collective-permute-done.1.refs_1_), channel_id=1, source_target_pairs={{0,128},{128,256},{256,384},{384,1},{1,129},{129,257},{257,385},{3... | collective-permute-start | bytes 884744 | tf_op jit(solution)/shard_map/ppermute | solution.py:153
  56.3 19.9 %collective-permute-start.4 = (f32[192,384]{1,0:T(8,128)S(1)}, f32[192,384]{1,0:T(8,128)S(1)}, u32[]{:S(2)}, u32[]{:S(2)}) collective-permute-start(f32[192,384]{1,0:T(8,128)S(1)} %collective-permute-done.2.refs_2_), channel_id=1, source_target_pairs={{0,385},{128,0},{256,128},{384,256},{1,384},{129,1},{257,129},{385... | collective-permute-start | bytes 884744 | tf_op jit(solution)/shard_map/ppermute | solution.py:153
  64.1 24.6 %collective-permute-start.5 = (f32[192,384]{1,0:T(8,128)S(1)}, f32[192,384]{1,0:T(8,128)S(1)}, u32[]{:S(2)}, u32[]{:S(2)}) collective-permute-start(f32[192,384]{1,0:T(8,128)S(1)} %collective-permute-done.3.refs_3_), channel_id=1, source_target_pairs={{0,128},{128,256},{256,384},{384,1},{1,129},{129,257},{257,385},{3... | collective-permute-start | bytes 884744 | tf_op jit(solution)/shard_map/ppermute | solution.py:153
  76.2 17.0 %collective-permute-start.6 = (f32[192,384]{1,0:T(8,128)S(1)}, f32[192,384]{1,0:T(8,128)S(1)}, u32[]{:S(2)}, u32[]{:S(2)}) collective-permute-start(f32[192,384]{1,0:T(8,128)S(1)} %collective-permute-done.4.refs_4_), channel_id=1, source_target_pairs={{0,385},{128,0},{256,128},{384,256},{1,384},{129,1},{257,129},{385... | collective-permute-start | bytes 884744 | tf_op jit(solution)/shard_map/ppermute | solution.py:153
  88.7 10.7 %collective-permute-start.7 = (f32[96,384]{1,0:T(8,128)S(1)}, f32[96,384]{1,0:T(8,128)S(1)}, u32[]{:S(2)}, u32[]{:S(2)}) collective-permute-start(f32[96,384]{1,0:T(8,128)S(1)} %slice.8), channel_id=1, source_target_pairs={{0,128},{128,256},{256,384},{384,1},{1,129},{129,257},{257,385},{3... | collective-permute-start | bytes 442376 | tf_op jit(solution)/shard_map/ppermute | solution.py:153
  93.2 11.4 %collective-permute-start.8 = (f32[96,384]{1,0:T(8,128)S(1)}, f32[96,384]{1,0:T(8,128)S(1)}, u32[]{:S(2)}, u32[]{:S(2)}) collective-permute-start(f32[96,384]{1,0:T(8,128)S(1)} %slice.9), channel_id=1, source_target_pairs={{0,385},{128,0},{256,128},{384,256},{1,384},{129,1},{257,129},{385... | collective-permute-start | bytes 442376 | tf_op jit(solution)/shard_map/ppermute | solution.py:153
  109.6 6.5 %collective-permute-start.9 = (f32[384,384]{1,0:T(8,128)S(1)}, f32[384,384]{1,0:T(8,128)S(1)}, u32[]{:S(2)}, u32[]{:S(2)}) collective-permute-start(f32[384,384]{1,0:T(8,128)S(1)} %product_other.1), channel_id=1, source_target_pairs={{0,32},{32,0},{1,33},{33,1},{2,34},{34,2},{3,35},{35,3},{4,36},{36... | collective-permute-start | bytes 1769480 | tf_op jit(solution)/shard_map/ppermute | solution.py:228

commit v5 on v4

v5 whole, which is shorter than its diff:
```python
import jax
import jax.numpy as jnp
import numpy as np
from jax import lax
from jax.experimental import pallas as pl
from jax.experimental.pallas import tpu as pltpu
from jax.sharding import Mesh, PartitionSpec as P

AXES = ("zl4", "zb", "core", "y", "x", "zhi")
SIZES = (4, 2, 2, 4, 4, 2)
PLANE = ("y", "x")
VIRT = 1536
OCC_WIN = 4
ROWS = 12
WIDE = 384
SHARD = 16 * ROWS
DEEP = 8 * SHARD
STEP = 512
TALL = 62
SPREAD = 52
VMEM = pl.BlockSpec(memory_space=pltpu.VMEM)
SMEM = pl.BlockSpec(memory_space=pltpu.SMEM)
HBM = pl.BlockSpec(memory_space=pltpu.HBM)
F32 = jnp.float32
BF16 = jnp.bfloat16


def call(body, name, out, ins, outs, mib, flops, moved, scratch=()):
    return pl.pallas_call(
        body,
        out_shape=out,
        in_specs=ins,
        out_specs=outs,
        scratch_shapes=scratch,
        compiler_params=pltpu.CompilerParams(vmem_limit_bytes=mib * 1024 * 1024),
        cost_estimate=pl.CostEstimate(flops=flops, bytes_accessed=moved, transcendentals=0),
        name=name,
    )


def shape(*dims, dtype=F32):
    return jax.ShapeDtypeStruct(dims, dtype)


def column_source():
    return np.arange(WIDE, dtype=np.int32).reshape(16, 2, ROWS).transpose(1, 0, 2).reshape(1, WIDE)


def in_two(x):
    high = x.astype(BF16)
    return high, (x - high.astype(F32)).astype(BF16)


def run(copies):
    for copy in copies:
        copy.start()
    for copy in copies:
        copy.wait()


def halves_kernel(where_ref, a_ref, own_ref, other_ref, sems):
    zb = where_ref[0]
    copies = []
    for z in range(4):
        at = slice(768 * z, 768 * z + 768)
        far = pl.ds(pl.multiple_of(1536 * z + 768 - 768 * zb, 128), 768)
        near = pl.ds(pl.multiple_of(1536 * z + 768 * zb, 128), 768)
        copies.append(pltpu.make_async_copy(a_ref.at[:, far], other_ref.at[:, at], sems.at[z]))
        copies.append(pltpu.make_async_copy(a_ref.at[:, near], own_ref.at[:, at], sems.at[4 + z]))
    run(copies)


def blocks_kernel(b_ref, out_ref, sems):
    run(
        [
            pltpu.make_async_copy(
                b_ref.at[:, WIDE * i : WIDE * i + WIDE], out_ref.at[i], sems.at[i]
            )
            for i in range(16)
        ]
    )


def stack_kernel(blocks_ref, out_ref):
    for i in range(16):
        out_ref[ROWS * i : ROWS * i + ROWS, :] = blocks_ref[i]


def half_kernel(lower, x_ref, out_ref):
    out_ref[...] = x_ref[SHARD // 2 :, :] if lower else x_ref[: SHARD // 2, :]


def spread_kernel(own_ref, pair_ref, source_ref, out_ref, rows_ref, sems):
    x = jnp.concatenate([own_ref[...], pair_ref[...]], axis=0)
    parts = []
    for _ in range(3):
        part = x.astype(BF16)
        x = x - part.astype(F32)
        parts += [part[:, WIDE * q : WIDE * q + WIDE] for q in range(8)]
    parts = jnp.concatenate(parts, axis=0)
    wanted = lax.broadcasted_iota(jnp.int32, (WIDE, WIDE), 0) == source_ref[...]
    order = jnp.where(wanted, 1.0, 0.0).astype(BF16)
    moved = jnp.dot(parts, order, preferred_element_type=F32)
    for q in range(8):
        rows = [moved[24 * (8 * p + q) : 24 * (8 * p + q) + 24] for p in range(3)]
        z, core = divmod(q, 2)
        rows_ref[core, :, WIDE * z : WIDE * z + WIDE] = (rows[0] + rows[1]) + rows[2]
    run([pltpu.make_async_copy(rows_ref.at[i // 16], out_ref.at[i], sems.at[i]) for i in range(32)])


def block_of(ring, step):
    at = lax.rem(ring + 8 + step, 8)
    return lax.rem(at, 4), at // 4


def place_kernel(where_ref, *refs):
    shards, high_ref, low_ref = refs[:7], refs[7], refs[8]
    ring = where_ref[2]
    for shard, step in zip(shards, [0, -1, 1, -2, 2, -3, 3]):
        z, zhi = block_of(ring, step)
        at = pl.ds(pl.multiple_of((2 * z + zhi) * SHARD, 64), SHARD)
        high_ref[at, :], low_ref[at, :] = in_two(shard[...])
    z, zhi = block_of(ring, 4)
    at = pl.ds(pl.multiple_of((2 * z + zhi) * SHARD, 64), SHARD)
    high_ref[at, :] = jnp.zeros((SHARD, WIDE), BF16)
    low_ref[at, :] = jnp.zeros((SHARD, WIDE), BF16)


def seven_kernel(where_ref, rows_ref, high_ref, low_ref, part_ref, run_high_ref, run_low_ref, left_ref, sems):
    copies = []
    for k in range(DEEP // STEP):
        at = pl.ds(STEP * k, STEP)
        for core in range(2):
            first = 16 * (1 - where_ref[1] if core else where_ref[1])
            source = rows_ref.at[pl.ds(first, 16), :, at]
            copies.append(pltpu.make_async_copy(source, left_ref.at[core, :, :, at], sems.at[core, k]))
            copies[-1].start()
    for k in range(DEEP // STEP):
        copies[2 * k].wait()
        copies[2 * k + 1].wait()
        at = slice(STEP * k, STEP * k + STEP)
        a_high, a_low = in_two(left_ref[:, :, :, at].reshape(2 * WIDE, STEP))
        b_high, b_low = high_ref[at, :], low_ref[at, :]
        term = jnp.dot(
            jnp.concatenate([a_high, a_low, a_high], axis=1),
            jnp.concatenate([b_high, b_high, b_low], axis=0),
            preferred_element_type=F32,
        )
        if k == 0:
            part_ref[...] = term
        else:
            part_ref[...] += term
    z, _ = block_of(where_ref[2], 4)
    last = left_ref[:, :, :, pl.ds(pl.multiple_of(z * WIDE, 128), WIDE)]
    run_high_ref[...], run_low_ref[...] = in_two(last.reshape(2 * WIDE, WIDE))


def eighth_kernel(where_ref, part_ref, a_high_ref, a_low_ref, up_ref, down_ref, own_ref, other_ref, high_ref, low_ref):
    _, zhi = block_of(where_ref[2], 4)
    high_ref[...] = jnp.zeros((WIDE, WIDE), BF16)
    low_ref[...] = jnp.zeros((WIDE, WIDE), BF16)
    for i, half in enumerate([up_ref, down_ref]):
        at = pl.ds(pl.multiple_of(zhi * SHARD + SHARD // 2 * i, 32), SHARD // 2)
        high_ref[at, :], low_ref[at, :] = in_two(half[...])
    a_high, a_low, b_high, b_low = a_high_ref[...], a_low_ref[...], high_ref[...], low_ref[...]
    total = part_ref[...] + jnp.dot(
        jnp.concatenate([a_high, a_low, a_high], axis=1),
        jnp.concatenate([b_high, b_high, b_low], axis=0),
        preferred_element_type=F32,
    )
    own_ref[...] = total[:WIDE]
    other_ref[...] = total[WIDE:]


def pack_kernel(where_ref, own_ref, other_ref, out_ref):
    for pair in range(2):
        zb = 1 - where_ref[0] if pair else where_ref[0]
        for i in range(16):
            rows = slice(24 * i + ROWS * pair, 24 * i + ROWS * pair + ROWS)
            total = own_ref[rows, :] + other_ref[rows, :]
            for g in range(3):
                at = slice(ROWS * g, ROWS * g + ROWS)
                out_ref[16 * zb + i, at, :] = total[:, 128 * g : 128 * g + 128]


def shifts_kernel(where_ref, wi_ref, wj_ref, occ_ref, virt_ref, lanes_ref, row_ref, col_ref):
    place = where_ref[3]
    per_orbital = VIRT // ROWS
    occ_i = occ_ref[wi_ref[place // per_orbital]]
    start = lax.rem(place, per_orbital) * ROWS
    at = lax.broadcasted_iota(jnp.int32, (ROWS, 128), 0)
    row = jnp.zeros((ROWS, 128), F32)
    for r in range(ROWS):
        row = jnp.where(at == r, occ_i - virt_ref[start + r], row)
    row_ref[...] = row
    for j in range(OCC_WIN):
        col_ref[:, VIRT * j : VIRT * j + VIRT] = occ_ref[wj_ref[j]] - lanes_ref[...].reshape(1, VIRT)


def divide_kernel(parts_ref, row_ref, col_ref, out_ref):
    row = row_ref[...]
    for i in range(16):
        for g in range(3):
            at = slice(ROWS * g, ROWS * g + ROWS)
            lanes = slice(WIDE * i + 128 * g, WIDE * i + 128 * g + 128)
            cycle = parts_ref[i, at, :] + parts_ref[16 + i, at, :]
            out_ref[:, lanes] = cycle / (row + col_ref[:, lanes])


def turn(x, step):
    index = lambda a: (a % 8 % 4) * 2 + a % 8 // 4
    return lax.ppermute(x, ("zl4", "zhi"), [(index(a), index(a + step)) for a in range(8)])


def per_device(amplitudes, integrals, occupied_energy, virtual_energy, window_i, window_j):
    swap = [(0, 1), (1, 0)]
    axis = lax.axis_index
    where = jnp.stack([axis("zb"), axis("core"), axis("zhi") * 4 + axis("zl4"), axis(AXES)])
    own, pair = call(
        halves_kernel,
        "halves",
        [shape(ROWS, 3072)] * 2,
        [SMEM, HBM],
        [VMEM] * 2,
        4,
        1,
        1 << 20,
        [pltpu.SemaphoreType.DMA((8,))],
    )(where, amplitudes)
    pair = lax.ppermute(pair, "zb", swap)
    blocks = call(
        blocks_kernel,
        "blocks",
        shape(16, ROWS, WIDE),
        [HBM],
        VMEM,
        TALL,
        1,
        1 << 20,
        [pltpu.SemaphoreType.DMA((16,))],
    )(integrals)
    blocks = lax.all_to_all(blocks, PLANE, split_axis=0, concat_axis=0, tiled=True)
    shard = call(
        stack_kernel,
        "stack",
        shape(SHARD, WIDE),
        [VMEM],
        VMEM,
        4,
        1,
        1 << 20,
    )(blocks)

    shards, right, left = [shard], shard, shard
    for _ in range(3):
        right, left = turn(right, 1), turn(left, -1)
        shards += [right, left]
    def half(x, lower):
        return call(
            lambda *refs: half_kernel(lower, *refs),
            "lower_half" if lower else "upper_half",
            shape(SHARD // 2, WIDE),
            [VMEM],
            VMEM,
            2,
            1,
            1 << 19,
        )(x)

    up, down = turn(half(right, False), 1), turn(half(left, True), -1)


    spread = call(
        spread_kernel,
        "spread",
        shape(32, 2 * ROWS, DEEP),
        [VMEM] * 3,
        HBM,
        SPREAD,
        2 * 576 * WIDE * WIDE,
        6 << 20,
        [pltpu.VMEM((2, 2 * ROWS, DEEP), F32), pltpu.SemaphoreType.DMA((32,))],
    )(own, pair, jnp.asarray(column_source()))
    rows = lax.all_to_all(spread, ("core", "y", "x"), split_axis=0, concat_axis=0, tiled=True)

    row, col = call(
        shifts_kernel,
        "shifts",
        [shape(ROWS, 128), shape(1, OCC_WIN * VIRT)],
        [SMEM] * 5 + [VMEM],
        [VMEM] * 2,
        2,
        1,
        1 << 16,
    )(where, window_i, window_j, occupied_energy, virtual_energy, virtual_energy)
    high, low = call(
        place_kernel,
        "place",
        [shape(DEEP, WIDE, dtype=BF16)] * 2,
        [SMEM] + [VMEM] * 7,
        [VMEM] * 2,
        10,
        4 * DEEP * WIDE,
        8 * DEEP * WIDE,
    )(where, *shards)
    part, run_high, run_low = call(
        seven_kernel,
        "seven",
        [shape(2 * WIDE, WIDE)] + [shape(2 * WIDE, WIDE, dtype=BF16)] * 2,
        [SMEM, HBM] + [VMEM] * 2,
        [VMEM] * 3,
        24,
        12 * WIDE * WIDE * DEEP,
        12 * WIDE * DEEP,
        [pltpu.VMEM((2, 16, 2 * ROWS, DEEP), F32), pltpu.SemaphoreType.DMA((2, DEEP // STEP))],
    )(where, rows, high, low)
    part, run_high, run_low, row, col = lax.optimization_barrier(
        (part, run_high, run_low, row, col)
    )
    mine, theirs = call(
        eighth_kernel,
        "eighth",
        [shape(WIDE, WIDE)] * 2,
        [SMEM] + [VMEM] * 5,
        [VMEM] * 2,
        14,
        12 * WIDE * WIDE * WIDE,
        6 << 20,
        [pltpu.VMEM((WIDE, WIDE), BF16)] * 2,
    )(where, part, run_high, run_low, up, down)
    theirs = lax.ppermute(theirs, "core", swap)
    packed = call(
        pack_kernel,
        "pack",
        shape(32, 3 * ROWS, 128),
        [SMEM] + [VMEM] * 2,
        VMEM,
        6,
        WIDE * WIDE,
        12 * WIDE * WIDE,
    )(where, mine, theirs)
    parts = lax.all_to_all(packed, ("zb", "y", "x"), split_axis=0, concat_axis=0, tiled=True)
    return call(
        divide_kernel,
        "divide",
        shape(ROWS, 16 * WIDE),
        [VMEM] * 3,
        VMEM,
        6,
        4 * ROWS * 16 * WIDE,
        1 << 20,
    )(parts, row, col)


def solution(mesh):
    fine = Mesh(mesh.devices.reshape(SIZES), AXES)
    split = P(AXES, None)
    return jax.shard_map(
        per_device,
        mesh=fine,
        in_specs=(split, split, P(), P(), P(), P()),
        out_specs=split,
        check_vma=False,
    )
```

time: 136 us -> 130 us (0.956)
  local copies, waits for them, and re-layouts: 4.92 us -> 0.03 us
  waiting for transfers between devices: 28.9 us -> 24.5 us
  Pallas kernels: 13.3 us -> 16.8 us
    ppermute x8, waiting for transfers between devices: 25.6 us -> 19.6 us  [turn(): lax.ppermute(x, ('zl4', 'zhi'), [(index(a), index(a + step)) for a in ran...]
    unnamed x16 -> x12, local copies, waits for them, and re-layouts: 4.86 us -> 0.03 us
    pallas_call x5 -> x9, Pallas kernels: 10.8 us -> 14.3 us  [the longest x1 6.23 us: per_device(): call(seven_kernel, 'seven', [shape(2 * WIDE, WIDE)] + [shape(2 * WIDE, WI...]
    ppermute x2, waiting for transfers between devices: 3.34 us -> 4.95 us  [the longest x1 3.34 us: per_device(): pair = lax.ppermute(pair, 'zb', swap)]
  transfers between devices with their start and end apart: 12 -> 12, of which waited for: 7 -> 7; matrix products, arithmetic and copies ran while one was open for 0% -> 0% of each run, Pallas kernels for 5% -> 9%
where the time goes in v5:
time: 130 us
  starting transfers between devices  69.5 us (53%)
  waiting for transfers between devices  24.5 us (19%)
  blocking collectives  18.4 us (14%)
  Pallas kernels  16.8 us (13%)
    ppermute x8, starting transfers between devices, turn(): lax.ppermute(x, ('zl4', 'zhi'), [(index(a), index(a + step)) for a in ran...  45 us
    ppermute x8, waiting for transfers between devices, turn(): lax.ppermute(x, ('zl4', 'zhi'), [(index(a), index(a + step)) for a in ran...  19.6 us
    all_to_all x1, blocking collectives, per_device(): lax.all_to_all(packed, ('zb', 'y', 'x'), split_axis=0, concat_axis=0, til...  18.4 us
    all_to_all x1, starting transfers between devices, per_device(): lax.all_to_all(spread, ('core', 'y', 'x'), split_axis=0, concat_axis=0, t...  10.8 us
    all_to_all x1, starting transfers between devices, per_device(): lax.all_to_all(blocks, PLANE, split_axis=0, concat_axis=0, tiled=True)  7.6 us
    pallas_call x1, Pallas kernels, per_device(): call(seven_kernel, 'seven', [shape(2 * WIDE, WIDE)] + [shape(2 * WIDE, WI...  6.23 us
    ppermute x1, starting transfers between devices, per_device(): pair = lax.ppermute(pair, 'zb', swap)  3.55 us
    ppermute x1, waiting for transfers between devices, per_device(): pair = lax.ppermute(pair, 'zb', swap)  3.34 us
  transfers between devices with their start and end apart: 12, of which 7 were waited for; matrix products, arithmetic and copies ran while one was open for 0% of the time, Pallas kernels for 9%

profile of v5, /device:TPU:1, one launch (start us, length us, event | category | flops | bytes accessed | tf_op | source)
XLA Modules:
  0.0 129.6 jit_solution(1703654903043335715)
XLA Ops:
  0.0 1.9 %blocks.1 = f32[16,12,384]{2,1,0:T(8,128)} custom-call(f32[12,6144]{1,0:T(8,128)} %b_ref.1), custom_call_target="tpu_custom_call" | custom-call | flops 1 | bytes 1048576 | tf_op jit(solution)/shard_map/blocks/pallas_call | solution.py:231
  1.9 7.6 %all-to-all-start.1 = ((f32[16,12,384]{2,1,0:T(8,128)}), f32[16,12,384]{2,1,0:T(8,128)S(1)}, u32[]{:S(2)}, u32[]{:S(2)}) async-start(f32[16,12,384]{2,1,0:T(8,128)} %blocks.1), calls=%async_computation.1 | async-start | bytes 786432 | tf_op jit(solution)/shard_map/all_to_all | solution.py:242
  9.5 0.1 pad_add_fusion.where_ref
  9.6 0.9 halves.1
  10.5 3.5 %collective-permute-start = (f32[12,3072]{1,0:T(8,128)S(1)}, f32[12,3072]{1,0:T(8,128)S(1)}, u32[]{:S(2)}, u32[]{:S(2)}) collective-permute-start(f32[12,3072]{1,0:T(8,128)S(1)} %get-tuple-element.22), channel_id=1, source_target_pairs={{0,64},{64,0},{1,65},{65,1},{2,66},{66,2},{3,67},{67,3},{4,68},{68... | collective-permute-start | bytes 442376 | tf_op jit(solution)/shard_map/ppermute | solution.py:230
  14.0 3.3 %collective-permute-done.pair_ref = f32[12,3072]{1,0:T(8,128)S(1)} collective-permute-done((f32[12,3072]{1,0:T(8,128)S(1)}, f32[12,3072]{1,0:T(8,128)S(1)}, u32[]{:S(2)}, u32[]{:S(2)}) %collective-permute-start) | collective-permute-done | bytes 147488 | tf_op jit(solution)/shard_map/ppermute | solution.py:230
  17.4 2.9 %spread.1 = f32[32,24,1536]{2,1,0:T(8,128)} custom-call(f32[12,3072]{1,0:T(8,128)S(1)} %get-tuple-element.21.own_ref, f32[12,3072]{1,0:T(8,128)S(1)} %collective-permute-done.pair_ref, s32[1,384]{1,0:T(1,128)S(1)} %copy-done.2), custom_call_target="tpu_custom_call" | custom-call | flops 169869312 | bytes 6291456 | tf_op jit(solution)/shard_map/spread/pallas_call | solution.py:273
  20.3 0.0 copy-start.1
  20.3 0.0 copy-start.3
  20.3 10.8 %all-to-all-start = ((f32[32,24,1536]{2,1,0:T(8,128)}), f32[32,24,1536]{2,1,0:T(8,128)}, u32[]{:S(2)}, u32[]{:S(2)}) async-start(f32[32,24,1536]{2,1,0:T(8,128)} %spread.1), calls=%async_computation | async-start | bytes 9437184 | tf_op jit(solution)/shard_map/all_to_all | solution.py:284
  31.2 3.7 %collective-permute-start.1 = (f32[192,384]{1,0:T(8,128)S(1)}, f32[192,384]{1,0:T(8,128)S(1)}, u32[]{:S(2)}, u32[]{:S(2)}) collective-permute-start(f32[192,384]{1,0:T(8,128)S(1)} %stack.21.refs_0_), channel_id=1, source_target_pairs={{0,128},{128,256},{256,384},{384,1},{1,129},{129,257},{257,385},{3... | collective-permute-start | bytes 884744 | tf_op jit(solution)/shard_map/ppermute | solution.py:212
  34.8 8.4 %collective-permute-start.2 = (f32[192,384]{1,0:T(8,128)S(1)}, f32[192,384]{1,0:T(8,128)S(1)}, u32[]{:S(2)}, u32[]{:S(2)}) collective-permute-start(f32[192,384]{1,0:T(8,128)S(1)} %stack.21.refs_0_), channel_id=1, source_target_pairs={{0,385},{128,0},{256,128},{384,256},{1,384},{129,1},{257,129},{385... | collective-permute-start | bytes 884744 | tf_op jit(solution)/shard_map/ppermute | solution.py:212
  43.3 7.4 %collective-permute-done.1.refs_1_ = f32[192,384]{1,0:T(8,128)S(1)} collective-permute-done((f32[192,384]{1,0:T(8,128)S(1)}, f32[192,384]{1,0:T(8,128)S(1)}, u32[]{:S(2)}, u32[]{:S(2)}) %collective-permute-start.1) | collective-permute-done | bytes 294944 | tf_op jit(solution)/shard_map/ppermute | solution.py:212
  50.7 2.6 %collective-permute-start.3 = (f32[192,384]{1,0:T(8,128)S(1)}, f32[192,384]{1,0:T(8,128)S(1)}, u32[]{:S(2)}, u32[]{:S(2)}) collective-permute-start(f32[192,384]{1,0:T(8,128)S(1)} %collective-permute-done.1.refs_1_), channel_id=1, source_target_pairs={{0,128},{128,256},{256,384},{384,1},{1,129},{129,257},{257,385},{3... | collective-permute-start | bytes 884744 | tf_op jit(solution)/shard_map/ppermute | solution.py:212
  53.3 1.0 collective-permute-done.2.refs_2_
  54.3 7.8 %collective-permute-start.4 = (f32[192,384]{1,0:T(8,128)S(1)}, f32[192,384]{1,0:T(8,128)S(1)}, u32[]{:S(2)}, u32[]{:S(2)}) collective-permute-start(f32[192,384]{1,0:T(8,128)S(1)} %collective-permute-done.2.refs_2_), channel_id=1, source_target_pairs={{0,385},{128,0},{256,128},{384,256},{1,384},{129,1},{257,129},{385... | collective-permute-start | bytes 884744 | tf_op jit(solution)/shard_map/ppermute | solution.py:212
  62.1 8.8 %collective-permute-start.5 = (f32[192,384]{1,0:T(8,128)S(1)}, f32[192,384]{1,0:T(8,128)S(1)}, u32[]{:S(2)}, u32[]{:S(2)}) collective-permute-start(f32[192,384]{1,0:T(8,128)S(1)} %collective-permute-done.3.refs_3_), channel_id=1, source_target_pairs={{0,128},{128,256},{256,384},{384,1},{1,129},{129,257},{257,385},{3... | collective-permute-start | bytes 884744 | tf_op jit(solution)/shard_map/ppermute | solution.py:212
  70.9 3.3 %collective-permute-done.4.refs_4_ = f32[192,384]{1,0:T(8,128)S(1)} collective-permute-done((f32[192,384]{1,0:T(8,128)S(1)}, f32[192,384]{1,0:T(8,128)S(1)}, u32[]{:S(2)}, u32[]{:S(2)}) %collective-permute-start.4) | collective-permute-done | bytes 294944 | tf_op jit(solution)/shard_map/ppermute | solution.py:212
  74.2 6.5 %collective-permute-start.6 = (f32[192,384]{1,0:T(8,128)S(1)}, f32[192,384]{1,0:T(8,128)S(1)}, u32[]{:S(2)}, u32[]{:S(2)}) collective-permute-start(f32[192,384]{1,0:T(8,128)S(1)} %collective-permute-done.4.refs_4_), channel_id=1, source_target_pairs={{0,385},{128,0},{256,128},{384,256},{1,384},{129,1},{257,129},{385... | collective-permute-start | bytes 884744 | tf_op jit(solution)/shard_map/ppermute | solution.py:212
  80.7 0.7 shifts.1
  81.4 5.3 %collective-permute-done.5.refs_5_.refs_0_ = f32[192,384]{1,0:T(8,128)S(1)} collective-permute-done((f32[192,384]{1,0:T(8,128)S(1)}, f32[192,384]{1,0:T(8,128)S(1)}, u32[]{:S(2)}, u32[]{:S(2)}) %collective-permute-start.5) | collective-permute-done | bytes 294944 | tf_op jit(solution)/shard_map/ppermute | solution.py:212
  86.7 1.9 %collective-permute-start.7 = (f32[96,384]{1,0:T(8,128)S(1)}, f32[96,384]{1,0:T(8,128)S(1)}, u32[]{:S(2)}, u32[]{:S(2)}) collective-permute-start(f32[96,384]{1,0:T(8,128)S(1)} %upper_half.1), channel_id=1, source_target_pairs={{0,128},{128,256},{256,384},{384,1},{1,129},{129,257},{257,385},{3... | collective-permute-start | bytes 442376 | tf_op jit(solution)/shard_map/ppermute | solution.py:212
  88.6 2.6 %collective-permute-done.6.refs_6_.refs_0_ = f32[192,384]{1,0:T(8,128)S(1)} collective-permute-done((f32[192,384]{1,0:T(8,128)S(1)}, f32[192,384]{1,0:T(8,128)S(1)}, u32[]{:S(2)}, u32[]{:S(2)}) %collective-permute-start.6) | collective-permute-done | bytes 294944 | tf_op jit(solution)/shard_map/ppermute | solution.py:212
  91.2 5.4 %collective-permute-start.8 = (f32[96,384]{1,0:T(8,128)S(1)}, f32[96,384]{1,0:T(8,128)S(1)}, u32[]{:S(2)}, u32[]{:S(2)}) collective-permute-start(f32[96,384]{1,0:T(8,128)S(1)} %lower_half.1), channel_id=1, source_target_pairs={{0,385},{128,0},{256,128},{384,256},{1,384},{129,1},{257,129},{385... | collective-permute-start | bytes 442376 | tf_op jit(solution)/shard_map/ppermute | solution.py:212
  96.6 1.0 place.1
  97.6 6.2 %seven.1 = (f32[768,384]{1,0:T(8,128)S(1)}, bf16[768,384]{1,0:T(8,128)(2,1)S(1)}, bf16[768,384]{1,0:T(8,128)(2,1)S(1)}) custom-call(s32[4]{0:T(128)S(1)} %pad_add_fusion.where_ref, f32[32,24,1536]{2,1,0:T(8,128)} %all-to-all-done.rows_ref, bf16[1536,384]{1,0:T(8,128)(2,1)S(1)} %get-tuple-element.23.high_ref, bf16[1536,384]{1,0:T(8,128)(2,1)S(1)} %get-tuple-element.24.low_ref), custom_call_target="tpu_custom_call" | custom-call | flops 2717908992 | bytes 7077888 | tf_op jit(solution)/shard_map/seven/pallas_call | solution.py:306
  103.8 1.8 %eighth.1 = (f32[384,384]{1,0:T(8,128)S(1)}, f32[384,384]{1,0:T(8,128)S(1)}) custom-call(s32[4]{0:T(128)S(1)} %pad_add_fusion.where_ref, f32[768,384]{1,0:T(8,128)S(1)} %get-tuple-element.30.part_ref, bf16[768,384]{1,0:T(8,128)(2,1)S(1)} %get-tuple-element.31.a_high_ref, bf16[768,384]{1,0:T(8,128)(2,1)S(1)} %get-tuple-element.32.a_low_ref, ...), custom_call_target="tpu_custom_call" | custom-call | flops 679477248 | bytes 6291456 | tf_op jit(solution)/shard_map/eighth/pallas_call | solution.py:320
  105.6 2.6 %collective-permute-start.9 = (f32[384,384]{1,0:T(8,128)S(1)}, f32[384,384]{1,0:T(8,128)S(1)}, u32[]{:S(2)}, u32[]{:S(2)}) collective-permute-start(f32[384,384]{1,0:T(8,128)S(1)} %get-tuple-element.34), channel_id=1, source_target_pairs={{0,32},{32,0},{1,33},{33,1},{2,34},{34,2},{3,35},{35,3},{4,36},{36... | collective-permute-start | bytes 1769480 | tf_op jit(solution)/shard_map/ppermute | solution.py:331
  108.2 1.6 %collective-permute-done.9.other_ref = f32[384,384]{1,0:T(8,128)S(1)} collective-permute-done((f32[384,384]{1,0:T(8,128)S(1)}, f32[384,384]{1,0:T(8,128)S(1)}, u32[]{:S(2)}, u32[]{:S(2)}) %collective-permute-start.9) | collective-permute-done | bytes 589856 | tf_op jit(solution)/shard_map/ppermute | solution.py:331
  109.8 0.6 pack.1
  110.5 18.4 %all_to_all.15.parts_ref = f32[32,36,128]{2,1,0:T(8,128)S(1)} all-to-all(f32[32,36,128]{2,1,0:T(8,128)S(1)} %pack.1), channel_id=1, replica_groups=mesh['zl4'=4,'zb'=2,'core'=2,'y'=4,'x'=4,'zhi'=2] {'zb','y','x'}, dimensions={0} | all-to-all | bytes 1179648 | tf_op jit(solution)/shard_map/all_to_all | solution.py:342
  128.8 0.8 divide.1
  (18 shorter events, 0.1 us)
Async XLA Ops:
  0.0 17.4 %copy-start.2 = (s32[1,384]{1,0:T(1,128)S(1)}, s32[1,384]{1,0:T(1,128)}, u32[]{:S(2)}) copy-start(s32[1,384]{1,0:T(1,128)} %constant.37.clone.source_ref) | copy-start | bytes 4612
  0.0 9.6 %copy-start = (f32[12,6144]{1,0:T(8,128)S(1)}, f32[12,6144]{1,0:T(8,128)}, u32[]{:S(2)}) copy-start(f32[12,6144]{1,0:T(8,128)} %a_ref.1) | copy-start | bytes 884740
  1.9 18.5 %all-to-all-start.1 = ((f32[16,12,384]{2,1,0:T(8,128)}), f32[16,12,384]{2,1,0:T(8,128)S(1)}, u32[]{:S(2)}, u32[]{:S(2)}) async-start(f32[16,12,384]{2,1,0:T(8,128)} %blocks.1), calls=%async_computation.1 | async-start | bytes 786432 | tf_op jit(solution)/shard_map/all_to_all | solution.py:242
  10.5 6.9 %collective-permute-start = (f32[12,3072]{1,0:T(8,128)S(1)}, f32[12,3072]{1,0:T(8,128)S(1)}, u32[]{:S(2)}, u32[]{:S(2)}) collective-permute-start(f32[12,3072]{1,0:T(8,128)S(1)} %get-tuple-element.22), channel_id=1, source_target_pairs={{0,64},{64,0},{1,65},{65,1},{2,66},{66,2},{3,67},{67,3},{4,68},{68... | collective-permute-start | bytes 442376 | tf_op jit(solution)/shard_map/ppermute | solution.py:230
  20.3 60.4 %copy-start.1 = (f32[1536]{0:T(1024)S(1)}, f32[1536]{0:T(1024)}, u32[]{:S(2)}) copy-start(f32[1536]{0:T(1024)} %lanes_ref.1) | copy-start | bytes 18436
  20.3 60.4 %copy-start.3 = (f32[150]{0:T(256)S(1)}, f32[150]{0:T(256)}, u32[]{:S(2)}) copy-start(f32[150]{0:T(256)} %occ_ref.1) | copy-start | bytes 1804
  20.3 60.4 %copy-start.4 = (s32[4]{0:T(128)S(1)}, s32[4]{0:T(128)}, u32[]{:S(2)}) copy-start(s32[4]{0:T(128)} %wi_ref.1) | copy-start | bytes 52
  20.3 60.4 %copy-start.5 = (s32[4]{0:T(128)S(1)}, s32[4]{0:T(128)}, u32[]{:S(2)}) copy-start(s32[4]{0:T(128)} %wj_ref.1) | copy-start | bytes 52
  20.3 77.2 %all-to-all-start = ((f32[32,24,1536]{2,1,0:T(8,128)}), f32[32,24,1536]{2,1,0:T(8,128)}, u32[]{:S(2)}, u32[]{:S(2)}) async-start(f32[32,24,1536]{2,1,0:T(8,128)} %spread.1), calls=%async_computation | async-start | bytes 9437184 | tf_op jit(solution)/shard_map/all_to_all | solution.py:284
  31.2 19.5 %collective-permute-start.1 = (f32[192,384]{1,0:T(8,128)S(1)}, f32[192,384]{1,0:T(8,128)S(1)}, u32[]{:S(2)}, u32[]{:S(2)}) collective-permute-start(f32[192,384]{1,0:T(8,128)S(1)} %stack.21.refs_0_), channel_id=1, source_target_pairs={{0,128},{128,256},{256,384},{384,1},{1,129},{129,257},{257,385},{3... | collective-permute-start | bytes 884744 | tf_op jit(solution)/shard_map/ppermute | solution.py:212
  34.8 19.5 %collective-permute-start.2 = (f32[192,384]{1,0:T(8,128)S(1)}, f32[192,384]{1,0:T(8,128)S(1)}, u32[]{:S(2)}, u32[]{:S(2)}) collective-permute-start(f32[192,384]{1,0:T(8,128)S(1)} %stack.21.refs_0_), channel_id=1, source_target_pairs={{0,385},{128,0},{256,128},{384,256},{1,384},{129,1},{257,129},{385... | collective-permute-start | bytes 884744 | tf_op jit(solution)/shard_map/ppermute | solution.py:212
  50.7 11.4 %collective-permute-start.3 = (f32[192,384]{1,0:T(8,128)S(1)}, f32[192,384]{1,0:T(8,128)S(1)}, u32[]{:S(2)}, u32[]{:S(2)}) collective-permute-start(f32[192,384]{1,0:T(8,128)S(1)} %collective-permute-done.1.refs_1_), channel_id=1, source_target_pairs={{0,128},{128,256},{256,384},{384,1},{1,129},{129,257},{257,385},{3... | collective-permute-start | bytes 884744 | tf_op jit(solution)/shard_map/ppermute | solution.py:212
  54.3 19.9 %collective-permute-start.4 = (f32[192,384]{1,0:T(8,128)S(1)}, f32[192,384]{1,0:T(8,128)S(1)}, u32[]{:S(2)}, u32[]{:S(2)}) collective-permute-start(f32[192,384]{1,0:T(8,128)S(1)} %collective-permute-done.2.refs_2_), channel_id=1, source_target_pairs={{0,385},{128,0},{256,128},{384,256},{1,384},{129,1},{257,129},{385... | collective-permute-start | bytes 884744 | tf_op jit(solution)/shard_map/ppermute | solution.py:212
  62.1 24.6 %collective-permute-start.5 = (f32[192,384]{1,0:T(8,128)S(1)}, f32[192,384]{1,0:T(8,128)S(1)}, u32[]{:S(2)}, u32[]{:S(2)}) collective-permute-start(f32[192,384]{1,0:T(8,128)S(1)} %collective-permute-done.3.refs_3_), channel_id=1, source_target_pairs={{0,128},{128,256},{256,384},{384,1},{1,129},{129,257},{257,385},{3... | collective-permute-start | bytes 884744 | tf_op jit(solution)/shard_map/ppermute | solution.py:212
  74.2 17.0 %collective-permute-start.6 = (f32[192,384]{1,0:T(8,128)S(1)}, f32[192,384]{1,0:T(8,128)S(1)}, u32[]{:S(2)}, u32[]{:S(2)}) collective-permute-start(f32[192,384]{1,0:T(8,128)S(1)} %collective-permute-done.4.refs_4_), channel_id=1, source_target_pairs={{0,385},{128,0},{256,128},{384,256},{1,384},{129,1},{257,129},{385... | collective-permute-start | bytes 884744 | tf_op jit(solution)/shard_map/ppermute | solution.py:212
  86.7 17.1 %collective-permute-start.7 = (f32[96,384]{1,0:T(8,128)S(1)}, f32[96,384]{1,0:T(8,128)S(1)}, u32[]{:S(2)}, u32[]{:S(2)}) collective-permute-start(f32[96,384]{1,0:T(8,128)S(1)} %upper_half.1), channel_id=1, source_target_pairs={{0,128},{128,256},{256,384},{384,1},{1,129},{129,257},{257,385},{3... | collective-permute-start | bytes 442376 | tf_op jit(solution)/shard_map/ppermute | solution.py:212
  91.2 12.6 %collective-permute-start.8 = (f32[96,384]{1,0:T(8,128)S(1)}, f32[96,384]{1,0:T(8,128)S(1)}, u32[]{:S(2)}, u32[]{:S(2)}) collective-permute-start(f32[96,384]{1,0:T(8,128)S(1)} %lower_half.1), channel_id=1, source_target_pairs={{0,385},{128,0},{256,128},{384,256},{1,384},{129,1},{257,129},{385... | collective-permute-start | bytes 442376 | tf_op jit(solution)/shard_map/ppermute | solution.py:212
  105.6 4.2 %collective-permute-start.9 = (f32[384,384]{1,0:T(8,128)S(1)}, f32[384,384]{1,0:T(8,128)S(1)}, u32[]{:S(2)}, u32[]{:S(2)}) collective-permute-start(f32[384,384]{1,0:T(8,128)S(1)} %get-tuple-element.34), channel_id=1, source_target_pairs={{0,32},{32,0},{1,33},{33,1},{2,34},{34,2},{3,35},{35,3},{4,36},{36... | collective-permute-start | bytes 1769480 | tf_op jit(solution)/shard_map/ppermute | solution.py:331

commit v6 on v5

--- a/solution.py
+++ b/solution.py
@@ -105,7 +105,7 @@
         rows = [moved[24 * (8 * p + q) : 24 * (8 * p + q) + 24] for p in range(3)]
         z, core = divmod(q, 2)
         rows_ref[core, :, WIDE * z : WIDE * z + WIDE] = (rows[0] + rows[1]) + rows[2]
-    run([pltpu.make_async_copy(rows_ref.at[i // 16], out_ref.at[i], sems.at[i]) for i in range(32)])
+    run([pltpu.make_async_copy(rows_ref.at[i % 2], out_ref.at[i], sems.at[i]) for i in range(32)])
 
 
 def block_of(ring, step):
@@ -131,8 +131,8 @@
     for k in range(DEEP // STEP):
         at = pl.ds(STEP * k, STEP)
         for core in range(2):
-            first = 16 * (1 - where_ref[1] if core else where_ref[1])
-            source = rows_ref.at[pl.ds(first, 16), :, at]
+            which = 1 - where_ref[1] if core else where_ref[1]
+            source = rows_ref.at[:, which, :, at]
             copies.append(pltpu.make_async_copy(source, left_ref.at[core, :, :, at], sems.at[core, k]))
             copies[-1].start()
     for k in range(DEEP // STEP):
@@ -155,21 +155,19 @@
     run_high_ref[...], run_low_ref[...] = in_two(last.reshape(2 * WIDE, WIDE))
 
 
-def eighth_kernel(where_ref, part_ref, a_high_ref, a_low_ref, up_ref, down_ref, own_ref, other_ref, high_ref, low_ref):
+def eighth_kernel(mine, where_ref, part_ref, a_high_ref, a_low_ref, last_ref, out_ref, high_ref, low_ref):
     _, zhi = block_of(where_ref[2], 4)
     high_ref[...] = jnp.zeros((WIDE, WIDE), BF16)
     low_ref[...] = jnp.zeros((WIDE, WIDE), BF16)
-    for i, half in enumerate([up_ref, down_ref]):
-        at = pl.ds(pl.multiple_of(zhi * SHARD + SHARD // 2 * i, 32), SHARD // 2)
-        high_ref[at, :], low_ref[at, :] = in_two(half[...])
-    a_high, a_low, b_high, b_low = a_high_ref[...], a_low_ref[...], high_ref[...], low_ref[...]
-    total = part_ref[...] + jnp.dot(
+    at = pl.ds(pl.multiple_of(zhi * SHARD, 64), SHARD)
+    high_ref[at, :], low_ref[at, :] = in_two(last_ref[...])
+    rows = slice(0, WIDE) if mine else slice(WIDE, 2 * WIDE)
+    a_high, a_low, b_high, b_low = a_high_ref[rows, :], a_low_ref[rows, :], high_ref[...], low_ref[...]
+    out_ref[...] = part_ref[rows, :] + jnp.dot(
         jnp.concatenate([a_high, a_low, a_high], axis=1),
         jnp.concatenate([b_high, b_high, b_low], axis=0),
         preferred_element_type=F32,
     )
-    own_ref[...] = total[:WIDE]
-    other_ref[...] = total[WIDE:]
 
 
 def pack_kernel(where_ref, own_ref, other_ref, out_ref):
@@ -255,19 +253,7 @@
     for _ in range(3):
         right, left = turn(right, 1), turn(left, -1)
         shards += [right, left]
-    def half(x, lower):
-        return call(
-            lambda *refs: half_kernel(lower, *refs),
-            "lower_half" if lower else "upper_half",
-            shape(SHARD // 2, WIDE),
-            [VMEM],
-            VMEM,
-            2,
-            1,
-            1 << 19,
-        )(x)
-
-    up, down = turn(half(right, False), 1), turn(half(left, True), -1)
+    last = turn(right, 1)
 
 
     spread = call(
@@ -281,7 +267,7 @@
         6 << 20,
         [pltpu.VMEM((2, 2 * ROWS, DEEP), F32), pltpu.SemaphoreType.DMA((32,))],
     )(own, pair, jnp.asarray(column_source()))
-    rows = lax.all_to_all(spread, ("core", "y", "x"), split_axis=0, concat_axis=0, tiled=True)
+    rows = lax.all_to_all(spread, ("y", "x", "core"), split_axis=0, concat_axis=0, tiled=True)
 
     row, col = call(
         shifts_kernel,
@@ -313,22 +299,25 @@
         12 * WIDE * WIDE * DEEP,
         12 * WIDE * DEEP,
         [pltpu.VMEM((2, 16, 2 * ROWS, DEEP), F32), pltpu.SemaphoreType.DMA((2, DEEP // STEP))],
-    )(where, rows, high, low)
+    )(where, rows.reshape(16, 2, 2 * ROWS, DEEP), high, low)
     part, run_high, run_low, row, col = lax.optimization_barrier(
         (part, run_high, run_low, row, col)
     )
-    mine, theirs = call(
-        eighth_kernel,
-        "eighth",
-        [shape(WIDE, WIDE)] * 2,
-        [SMEM] + [VMEM] * 5,
-        [VMEM] * 2,
-        14,
-        12 * WIDE * WIDE * WIDE,
-        6 << 20,
-        [pltpu.VMEM((WIDE, WIDE), BF16)] * 2,
-    )(where, part, run_high, run_low, up, down)
-    theirs = lax.ppermute(theirs, "core", swap)
+    def eighth(mine):
+        return call(
+            lambda *refs: eighth_kernel(mine, *refs),
+            "eighth_mine" if mine else "eighth_theirs",
+            shape(WIDE, WIDE),
+            [SMEM] + [VMEM] * 4,
+            VMEM,
+            14,
+            6 * WIDE * WIDE * WIDE,
+            3 << 20,
+            [pltpu.VMEM((WIDE, WIDE), BF16)] * 2,
+        )(where, part, run_high, run_low, last)
+
+    theirs = lax.ppermute(eighth(False), "core", swap)
+    mine = eighth(True)
     packed = call(
         pack_kernel,
         "pack",

time: 130 us -> 130 us (level)
  waiting for transfers between devices: 24.5 us -> 19.1 us
  blocking collectives: 18.4 us -> 22.9 us
    all_to_all x1, blocking collectives: 18.4 us -> 22.9 us  [per_device(): lax.all_to_all(packed, ('zb', 'y', 'x'), split_axis=0, concat_axis=0, til...]
    ppermute x8 -> x7, waiting for transfers between devices: 19.6 us -> 15.5 us  [turn(): lax.ppermute(x, ('zl4', 'zhi'), [(index(a), index(a + step)) for a in ran...]
    ppermute x1, waiting for transfers between devices: 1.61 us -> 0.29 us  [per_device(): theirs = lax.ppermute(eighth(False), 'core', swap)]
    pallas_call x3 -> x2, Pallas kernels: 1.8 us -> 2.61 us  [eighth(): call(lambda *refs: eighth_kernel(mine, *refs), 'eighth_mine' if mine else...]
    ppermute x8 -> x7, starting transfers between devices: 45 us -> 44.3 us  [turn(): lax.ppermute(x, ('zl4', 'zhi'), [(index(a), index(a + step)) for a in ran...]
  transfers between devices with their start and end apart: 12 -> 11, of which waited for: 7 -> 7; matrix products, arithmetic and copies ran while one was open for 0% -> 0% of each run, Pallas kernels for 9% -> 10%
where the time goes in v6:
time: 130 us; the launch traced here: 129 us
  starting transfers between devices  69.1 us (53%)
  blocking collectives  22.9 us (18%)
  waiting for transfers between devices  19.1 us (15%)
  Pallas kernels  17.6 us (14%)
    ppermute x7, starting transfers between devices, turn(): lax.ppermute(x, ('zl4', 'zhi'), [(index(a), index(a + step)) for a in ran...  44.3 us
    all_to_all x1, blocking collectives, per_device(): lax.all_to_all(packed, ('zb', 'y', 'x'), split_axis=0, concat_axis=0, til...  22.9 us
    ppermute x7, waiting for transfers between devices, turn(): lax.ppermute(x, ('zl4', 'zhi'), [(index(a), index(a + step)) for a in ran...  15.5 us
    all_to_all x1, starting transfers between devices, per_device(): lax.all_to_all(spread, ('y', 'x', 'core'), split_axis=0, concat_axis=0, t...  10.8 us
    all_to_all x1, starting transfers between devices, per_device(): lax.all_to_all(blocks, PLANE, split_axis=0, concat_axis=0, tiled=True)  7.6 us
    pallas_call x1, Pallas kernels, per_device(): call(seven_kernel, 'seven', [shape(2 * WIDE, WIDE)] + [shape(2 * WIDE, WI...  6.24 us
    ppermute x1, starting transfers between devices, per_device(): pair = lax.ppermute(pair, 'zb', swap)  3.55 us
    ppermute x1, waiting for transfers between devices, per_device(): pair = lax.ppermute(pair, 'zb', swap)  3.34 us
  transfers between devices with their start and end apart: 11, of which 7 were waited for; matrix products, arithmetic and copies ran while one was open for 0% of the time, Pallas kernels for 10%

profile of v6, /device:TPU:1, one launch (start us, length us, event | category | flops | bytes accessed | tf_op | source)
XLA Modules:
  0.0 129.1 jit_solution(14679879356686713128)
XLA Ops:
  0.0 1.9 %blocks.1 = f32[16,12,384]{2,1,0:T(8,128)} custom-call(f32[12,6144]{1,0:T(8,128)} %b_ref.1), custom_call_target="tpu_custom_call" | custom-call | flops 1 | bytes 1048576 | tf_op jit(solution)/shard_map/blocks/pallas_call | solution.py:229
  1.9 7.6 %all-to-all-start.1 = ((f32[16,12,384]{2,1,0:T(8,128)}), f32[16,12,384]{2,1,0:T(8,128)S(1)}, u32[]{:S(2)}, u32[]{:S(2)}) async-start(f32[16,12,384]{2,1,0:T(8,128)} %blocks.1), calls=%async_computation.1 | async-start | bytes 786432 | tf_op jit(solution)/shard_map/all_to_all | solution.py:240
  9.5 0.1 pad_add_fusion.where_ref.refs_0_
  9.6 0.9 halves.1
  10.5 3.5 %collective-permute-start = (f32[12,3072]{1,0:T(8,128)S(1)}, f32[12,3072]{1,0:T(8,128)S(1)}, u32[]{:S(2)}, u32[]{:S(2)}) collective-permute-start(f32[12,3072]{1,0:T(8,128)S(1)} %get-tuple-element.20), channel_id=1, source_target_pairs={{0,64},{64,0},{1,65},{65,1},{2,66},{66,2},{3,67},{67,3},{4,68},{68... | collective-permute-start | bytes 442376 | tf_op jit(solution)/shard_map/ppermute | solution.py:228
  14.0 3.3 %collective-permute-done.pair_ref = f32[12,3072]{1,0:T(8,128)S(1)} collective-permute-done((f32[12,3072]{1,0:T(8,128)S(1)}, f32[12,3072]{1,0:T(8,128)S(1)}, u32[]{:S(2)}, u32[]{:S(2)}) %collective-permute-start) | collective-permute-done | bytes 147488 | tf_op jit(solution)/shard_map/ppermute | solution.py:228
  17.4 2.9 %spread.1 = f32[32,24,1536]{2,1,0:T(8,128)} custom-call(f32[12,3072]{1,0:T(8,128)S(1)} %get-tuple-element.19.own_ref, f32[12,3072]{1,0:T(8,128)S(1)} %collective-permute-done.pair_ref, s32[1,384]{1,0:T(1,128)S(1)} %copy-done.2), custom_call_target="tpu_custom_call" | custom-call | flops 169869312 | bytes 6291456 | tf_op jit(solution)/shard_map/spread/pallas_call | solution.py:259
  20.3 0.0 copy-start.3
  20.3 0.0 copy-start.4
  20.4 10.8 %all-to-all-start = ((f32[32,24,1536]{2,1,0:T(8,128)}), f32[32,24,1536]{2,1,0:T(8,128)}, u32[]{:S(2)}, u32[]{:S(2)}) async-start(f32[32,24,1536]{2,1,0:T(8,128)} %spread.1), calls=%async_computation | async-start | bytes 9437184 | tf_op jit(solution)/shard_map/all_to_all | solution.py:270
  31.2 3.7 %collective-permute-start.1 = (f32[192,384]{1,0:T(8,128)S(1)}, f32[192,384]{1,0:T(8,128)S(1)}, u32[]{:S(2)}, u32[]{:S(2)}) collective-permute-start(f32[192,384]{1,0:T(8,128)S(1)} %stack.21.refs_0_), channel_id=1, source_target_pairs={{0,128},{128,256},{256,384},{384,1},{1,129},{129,257},{257,385},{3... | collective-permute-start | bytes 884744 | tf_op jit(solution)/shard_map/ppermute | solution.py:210
  34.8 8.4 %collective-permute-start.2 = (f32[192,384]{1,0:T(8,128)S(1)}, f32[192,384]{1,0:T(8,128)S(1)}, u32[]{:S(2)}, u32[]{:S(2)}) collective-permute-start(f32[192,384]{1,0:T(8,128)S(1)} %stack.21.refs_0_), channel_id=1, source_target_pairs={{0,385},{128,0},{256,128},{384,256},{1,384},{129,1},{257,129},{385... | collective-permute-start | bytes 884744 | tf_op jit(solution)/shard_map/ppermute | solution.py:210
  43.3 7.5 %collective-permute-done.1.refs_1_ = f32[192,384]{1,0:T(8,128)S(1)} collective-permute-done((f32[192,384]{1,0:T(8,128)S(1)}, f32[192,384]{1,0:T(8,128)S(1)}, u32[]{:S(2)}, u32[]{:S(2)}) %collective-permute-start.1) | collective-permute-done | bytes 294944 | tf_op jit(solution)/shard_map/ppermute | solution.py:210
  50.8 2.5 %collective-permute-start.3 = (f32[192,384]{1,0:T(8,128)S(1)}, f32[192,384]{1,0:T(8,128)S(1)}, u32[]{:S(2)}, u32[]{:S(2)}) collective-permute-start(f32[192,384]{1,0:T(8,128)S(1)} %collective-permute-done.1.refs_1_), channel_id=1, source_target_pairs={{0,128},{128,256},{256,384},{384,1},{1,129},{129,257},{257,385},{3... | collective-permute-start | bytes 884744 | tf_op jit(solution)/shard_map/ppermute | solution.py:210
  53.3 1.0 collective-permute-done.2.refs_2_
  54.3 7.9 %collective-permute-start.4 = (f32[192,384]{1,0:T(8,128)S(1)}, f32[192,384]{1,0:T(8,128)S(1)}, u32[]{:S(2)}, u32[]{:S(2)}) collective-permute-start(f32[192,384]{1,0:T(8,128)S(1)} %collective-permute-done.2.refs_2_), channel_id=1, source_target_pairs={{0,385},{128,0},{256,128},{384,256},{1,384},{129,1},{257,129},{385... | collective-permute-start | bytes 884744 | tf_op jit(solution)/shard_map/ppermute | solution.py:210
  62.2 8.9 %collective-permute-start.5 = (f32[192,384]{1,0:T(8,128)S(1)}, f32[192,384]{1,0:T(8,128)S(1)}, u32[]{:S(2)}, u32[]{:S(2)}) collective-permute-start(f32[192,384]{1,0:T(8,128)S(1)} %collective-permute-done.3.refs_3_), channel_id=1, source_target_pairs={{0,128},{128,256},{256,384},{384,1},{1,129},{129,257},{257,385},{3... | collective-permute-start | bytes 884744 | tf_op jit(solution)/shard_map/ppermute | solution.py:210
  71.1 3.3 %collective-permute-done.4.refs_4_ = f32[192,384]{1,0:T(8,128)S(1)} collective-permute-done((f32[192,384]{1,0:T(8,128)S(1)}, f32[192,384]{1,0:T(8,128)S(1)}, u32[]{:S(2)}, u32[]{:S(2)}) %collective-permute-start.4) | collective-permute-done | bytes 294944 | tf_op jit(solution)/shard_map/ppermute | solution.py:210
  74.5 6.5 %collective-permute-start.6 = (f32[192,384]{1,0:T(8,128)S(1)}, f32[192,384]{1,0:T(8,128)S(1)}, u32[]{:S(2)}, u32[]{:S(2)}) collective-permute-start(f32[192,384]{1,0:T(8,128)S(1)} %collective-permute-done.4.refs_4_), channel_id=1, source_target_pairs={{0,385},{128,0},{256,128},{384,256},{1,384},{129,1},{257,129},{385... | collective-permute-start | bytes 884744 | tf_op jit(solution)/shard_map/ppermute | solution.py:210
  80.9 2.4 %collective-permute-done.5.refs_5_ = f32[192,384]{1,0:T(8,128)S(1)} collective-permute-done((f32[192,384]{1,0:T(8,128)S(1)}, f32[192,384]{1,0:T(8,128)S(1)}, u32[]{:S(2)}, u32[]{:S(2)}) %collective-permute-start.5) | collective-permute-done | bytes 294944 | tf_op jit(solution)/shard_map/ppermute | solution.py:210
  83.3 6.5 %collective-permute-start.7 = (f32[192,384]{1,0:T(8,128)S(1)}, f32[192,384]{1,0:T(8,128)S(1)}, u32[]{:S(2)}, u32[]{:S(2)}) collective-permute-start(f32[192,384]{1,0:T(8,128)S(1)} %collective-permute-done.5.refs_5_), channel_id=1, source_target_pairs={{0,128},{128,256},{256,384},{384,1},{1,129},{129,257},{257,385},{3... | collective-permute-start | bytes 884744 | tf_op jit(solution)/shard_map/ppermute | solution.py:210
  89.9 0.7 shifts.1
  90.6 1.0 place.1
  91.6 6.2 %seven.1 = (f32[768,384]{1,0:T(8,128)S(1)}, bf16[768,384]{1,0:T(8,128)(2,1)S(1)}, bf16[768,384]{1,0:T(8,128)(2,1)S(1)}) custom-call(s32[4]{0:T(128)S(1)} %pad_add_fusion.where_ref.refs_0_, f32[16,2,24,1536]{3,2,1,0:T(8,128)} %bitcast.4.rows_ref, bf16[1536,384]{1,0:T(8,128)(2,1)S(1)} %get-tuple-element.21.high_ref, ...), custom_call_target="tpu_custom_call" | custom-call | flops 2717908992 | bytes 7077888 | tf_op jit(solution)/shard_map/seven/pallas_call | solution.py:292
  97.8 1.2 collective-permute-done.7.refs_4_
  99.0 1.3 %eighth_theirs.1 = f32[384,384]{1,0:T(8,128)S(1)} custom-call(s32[4]{0:T(128)S(1)} %pad_add_fusion.where_ref.refs_0_, f32[768,384]{1,0:T(8,128)S(1)} %get-tuple-element.28.refs_1_, bf16[768,384]{1,0:T(8,128)(2,1)S(1)} %get-tuple-element.29.refs_2_, bf16[768,384]{1,0:T(8,128)(2,1)S(1)} %get-tuple-element.30.refs_3_, f32[192,384]{1,0:T(8,128)S(1)} %collective-permute-done.7.refs_4_), custom_call_target="tpu_custom_call" | custom-call | flops 339738624 | bytes 3145728 | tf_op jit(solution)/shard_map/eighth_theirs/pallas_call | solution.py:307
  100.3 2.9 %collective-permute-start.8 = (f32[384,384]{1,0:T(8,128)S(1)}, f32[384,384]{1,0:T(8,128)S(1)}, u32[]{:S(2)}, u32[]{:S(2)}) collective-permute-start(f32[384,384]{1,0:T(8,128)S(1)} %eighth_theirs.1), channel_id=1, source_target_pairs={{0,32},{32,0},{1,33},{33,1},{2,34},{34,2},{3,35},{35,3},{4,36},{36... | collective-permute-start | bytes 1769480 | tf_op jit(solution)/shard_map/ppermute | solution.py:319
  103.2 1.3 %eighth_mine.1.own_ref = f32[384,384]{1,0:T(8,128)S(1)} custom-call(s32[4]{0:T(128)S(1)} %pad_add_fusion.where_ref.refs_0_, f32[768,384]{1,0:T(8,128)S(1)} %get-tuple-element.28.refs_1_, bf16[768,384]{1,0:T(8,128)(2,1)S(1)} %get-tuple-element.29.refs_2_, bf16[768,384]{1,0:T(8,128)(2,1)S(1)} %get-tuple-element.30.refs_3_, ...), custom_call_target="tpu_custom_call" | custom-call | flops 339738624 | bytes 3145728 | tf_op jit(solution)/shard_map/eighth_mine/pallas_call | solution.py:307
  104.5 0.3 collective-permute-done.8.other_ref
  104.8 0.6 pack.1
  105.5 22.9 %all_to_all.15.parts_ref = f32[32,36,128]{2,1,0:T(8,128)S(1)} all-to-all(f32[32,36,128]{2,1,0:T(8,128)S(1)} %pack.1), channel_id=1, replica_groups=mesh['zl4'=4,'zb'=2,'core'=2,'y'=4,'x'=4,'zhi'=2] {'zb','y','x'}, dimensions={0} | all-to-all | bytes 1179648 | tf_op jit(solution)/shard_map/all_to_all | solution.py:331
  128.3 0.8 divide.1
  (15 shorter events, 0.1 us)
Async XLA Ops:
  0.0 17.4 %copy-start.2 = (s32[1,384]{1,0:T(1,128)S(1)}, s32[1,384]{1,0:T(1,128)}, u32[]{:S(2)}) copy-start(s32[1,384]{1,0:T(1,128)} %constant.37.clone.source_ref) | copy-start | bytes 4612
  0.0 9.6 %copy-start = (f32[12,6144]{1,0:T(8,128)S(1)}, f32[12,6144]{1,0:T(8,128)}, u32[]{:S(2)}) copy-start(f32[12,6144]{1,0:T(8,128)} %a_ref.1) | copy-start | bytes 884740
  1.9 18.5 %all-to-all-start.1 = ((f32[16,12,384]{2,1,0:T(8,128)}), f32[16,12,384]{2,1,0:T(8,128)S(1)}, u32[]{:S(2)}, u32[]{:S(2)}) async-start(f32[16,12,384]{2,1,0:T(8,128)} %blocks.1), calls=%async_computation.1 | async-start | bytes 786432 | tf_op jit(solution)/shard_map/all_to_all | solution.py:240
  10.5 6.9 %collective-permute-start = (f32[12,3072]{1,0:T(8,128)S(1)}, f32[12,3072]{1,0:T(8,128)S(1)}, u32[]{:S(2)}, u32[]{:S(2)}) collective-permute-start(f32[12,3072]{1,0:T(8,128)S(1)} %get-tuple-element.20), channel_id=1, source_target_pairs={{0,64},{64,0},{1,65},{65,1},{2,66},{66,2},{3,67},{67,3},{4,68},{68... | collective-permute-start | bytes 442376 | tf_op jit(solution)/shard_map/ppermute | solution.py:228
  20.3 69.6 %copy-start.1 = (f32[1536]{0:T(1024)S(1)}, f32[1536]{0:T(1024)}, u32[]{:S(2)}) copy-start(f32[1536]{0:T(1024)} %lanes_ref.1) | copy-start | bytes 18436
  20.3 69.6 %copy-start.3 = (f32[150]{0:T(256)S(1)}, f32[150]{0:T(256)}, u32[]{:S(2)}) copy-start(f32[150]{0:T(256)} %occ_ref.1) | copy-start | bytes 1804
  20.3 69.6 %copy-start.4 = (s32[4]{0:T(128)S(1)}, s32[4]{0:T(128)}, u32[]{:S(2)}) copy-start(s32[4]{0:T(128)} %wi_ref.1) | copy-start | bytes 52
  20.3 69.6 %copy-start.5 = (s32[4]{0:T(128)S(1)}, s32[4]{0:T(128)}, u32[]{:S(2)}) copy-start(s32[4]{0:T(128)} %wj_ref.1) | copy-start | bytes 52
  20.4 71.2 %all-to-all-start = ((f32[32,24,1536]{2,1,0:T(8,128)}), f32[32,24,1536]{2,1,0:T(8,128)}, u32[]{:S(2)}, u32[]{:S(2)}) async-start(f32[32,24,1536]{2,1,0:T(8,128)} %spread.1), calls=%async_computation | async-start | bytes 9437184 | tf_op jit(solution)/shard_map/all_to_all | solution.py:270
  31.2 19.6 %collective-permute-start.1 = (f32[192,384]{1,0:T(8,128)S(1)}, f32[192,384]{1,0:T(8,128)S(1)}, u32[]{:S(2)}, u32[]{:S(2)}) collective-permute-start(f32[192,384]{1,0:T(8,128)S(1)} %stack.21.refs_0_), channel_id=1, source_target_pairs={{0,128},{128,256},{256,384},{384,1},{1,129},{129,257},{257,385},{3... | collective-permute-start | bytes 884744 | tf_op jit(solution)/shard_map/ppermute | solution.py:210
  34.8 19.5 %collective-permute-start.2 = (f32[192,384]{1,0:T(8,128)S(1)}, f32[192,384]{1,0:T(8,128)S(1)}, u32[]{:S(2)}, u32[]{:S(2)}) collective-permute-start(f32[192,384]{1,0:T(8,128)S(1)} %stack.21.refs_0_), channel_id=1, source_target_pairs={{0,385},{128,0},{256,128},{384,256},{1,384},{129,1},{257,129},{385... | collective-permute-start | bytes 884744 | tf_op jit(solution)/shard_map/ppermute | solution.py:210
  50.8 11.4 %collective-permute-start.3 = (f32[192,384]{1,0:T(8,128)S(1)}, f32[192,384]{1,0:T(8,128)S(1)}, u32[]{:S(2)}, u32[]{:S(2)}) collective-permute-start(f32[192,384]{1,0:T(8,128)S(1)} %collective-permute-done.1.refs_1_), channel_id=1, source_target_pairs={{0,128},{128,256},{256,384},{384,1},{1,129},{129,257},{257,385},{3... | collective-permute-start | bytes 884744 | tf_op jit(solution)/shard_map/ppermute | solution.py:210
  54.3 20.1 %collective-permute-start.4 = (f32[192,384]{1,0:T(8,128)S(1)}, f32[192,384]{1,0:T(8,128)S(1)}, u32[]{:S(2)}, u32[]{:S(2)}) collective-permute-start(f32[192,384]{1,0:T(8,128)S(1)} %collective-permute-done.2.refs_2_), channel_id=1, source_target_pairs={{0,385},{128,0},{256,128},{384,256},{1,384},{129,1},{257,129},{385... | collective-permute-start | bytes 884744 | tf_op jit(solution)/shard_map/ppermute | solution.py:210
  62.2 21.1 %collective-permute-start.5 = (f32[192,384]{1,0:T(8,128)S(1)}, f32[192,384]{1,0:T(8,128)S(1)}, u32[]{:S(2)}, u32[]{:S(2)}) collective-permute-start(f32[192,384]{1,0:T(8,128)S(1)} %collective-permute-done.3.refs_3_), channel_id=1, source_target_pairs={{0,128},{128,256},{256,384},{384,1},{1,129},{129,257},{257,385},{3... | collective-permute-start | bytes 884744 | tf_op jit(solution)/shard_map/ppermute | solution.py:210
  74.5 16.2 %collective-permute-start.6 = (f32[192,384]{1,0:T(8,128)S(1)}, f32[192,384]{1,0:T(8,128)S(1)}, u32[]{:S(2)}, u32[]{:S(2)}) collective-permute-start(f32[192,384]{1,0:T(8,128)S(1)} %collective-permute-done.4.refs_4_), channel_id=1, source_target_pairs={{0,385},{128,0},{256,128},{384,256},{1,384},{129,1},{257,129},{385... | collective-permute-start | bytes 884744 | tf_op jit(solution)/shard_map/ppermute | solution.py:210
  83.3 15.7 %collective-permute-start.7 = (f32[192,384]{1,0:T(8,128)S(1)}, f32[192,384]{1,0:T(8,128)S(1)}, u32[]{:S(2)}, u32[]{:S(2)}) collective-permute-start(f32[192,384]{1,0:T(8,128)S(1)} %collective-permute-done.5.refs_5_), channel_id=1, source_target_pairs={{0,128},{128,256},{256,384},{384,1},{1,129},{129,257},{257,385},{3... | collective-permute-start | bytes 884744 | tf_op jit(solution)/shard_map/ppermute | solution.py:210
  100.3 4.5 %collective-permute-start.8 = (f32[384,384]{1,0:T(8,128)S(1)}, f32[384,384]{1,0:T(8,128)S(1)}, u32[]{:S(2)}, u32[]{:S(2)}) collective-permute-start(f32[384,384]{1,0:T(8,128)S(1)} %eighth_theirs.1), channel_id=1, source_target_pairs={{0,32},{32,0},{1,33},{33,1},{2,34},{34,2},{3,35},{35,3},{4,36},{36... | collective-permute-start | bytes 1769480 | tf_op jit(solution)/shard_map/ppermute | solution.py:319

commit v7 on v6

--- a/solution.py
+++ b/solution.py
@@ -92,20 +92,26 @@
 
 def spread_kernel(own_ref, pair_ref, source_ref, out_ref, rows_ref, sems):
     x = jnp.concatenate([own_ref[...], pair_ref[...]], axis=0)
-    parts = []
-    for _ in range(3):
-        part = x.astype(BF16)
-        x = x - part.astype(F32)
-        parts += [part[:, WIDE * q : WIDE * q + WIDE] for q in range(8)]
-    parts = jnp.concatenate(parts, axis=0)
     wanted = lax.broadcasted_iota(jnp.int32, (WIDE, WIDE), 0) == source_ref[...]
     order = jnp.where(wanted, 1.0, 0.0).astype(BF16)
-    moved = jnp.dot(parts, order, preferred_element_type=F32)
-    for q in range(8):
-        rows = [moved[24 * (8 * p + q) : 24 * (8 * p + q) + 24] for p in range(3)]
-        z, core = divmod(q, 2)
-        rows_ref[core, :, WIDE * z : WIDE * z + WIDE] = (rows[0] + rows[1]) + rows[2]
-    run([pltpu.make_async_copy(rows_ref.at[i % 2], out_ref.at[i], sems.at[i]) for i in range(32)])
+    copies = []
+    for core in range(2):
+        rest = jnp.concatenate(
+            [x[:, 768 * z + WIDE * core : 768 * z + WIDE * core + WIDE] for z in range(4)], axis=0
+        )
+        total = None
+        for _ in range(3):
+            part = rest.astype(BF16)
+            rest = rest - part.astype(F32)
+            moved = jnp.dot(part, order, preferred_element_type=F32)
+            total = moved if total is None else total + moved
+        for z in range(4):
+            rows_ref[core, :, WIDE * z : WIDE * z + WIDE] = total[24 * z : 24 * z + 24]
+        for i in range(core, 32, 2):
+            copies.append(pltpu.make_async_copy(rows_ref.at[core], out_ref.at[i], sems.at[i]))
+            copies[-1].start()
+    for copy in copies:
+        copy.wait()
 
 
 def block_of(ring, step):

time: 130 us -> 130 us (level)
    ppermute x7, starting transfers between devices: 44.3 us -> 42.8 us  [turn(): lax.ppermute(x, ('zl4', 'zhi'), [(index(a), index(a + step)) for a in ran...]
    ppermute x1, starting transfers between devices: 2.91 us -> 4.45 us  [per_device(): theirs = lax.ppermute(eighth(False), 'core', swap)]
  transfers between devices with their start and end apart: 11 -> 11, of which waited for: 7 -> 8; matrix products, arithmetic and copies ran while one was open for 0% -> 0% of each run, Pallas kernels for 10% -> 10%
where the time goes in v7:
time: 130 us; the launch traced here: 129 us
  starting transfers between devices  69.1 us (53%)
  blocking collectives  21.6 us (17%)
  waiting for transfers between devices  20.4 us (16%)
  Pallas kernels  17.5 us (13%)
    ppermute x7, starting transfers between devices, turn(): lax.ppermute(x, ('zl4', 'zhi'), [(index(a), index(a + step)) for a in ran...  42.8 us
    all_to_all x1, blocking collectives, per_device(): lax.all_to_all(packed, ('zb', 'y', 'x'), split_axis=0, concat_axis=0, til...  21.6 us
    ppermute x7, waiting for transfers between devices, turn(): lax.ppermute(x, ('zl4', 'zhi'), [(index(a), index(a + step)) for a in ran...  16.7 us
    all_to_all x1, starting transfers between devices, per_device(): lax.all_to_all(spread, ('y', 'x', 'core'), split_axis=0, concat_axis=0, t...  10.8 us
    all_to_all x1, starting transfers between devices, per_device(): lax.all_to_all(blocks, PLANE, split_axis=0, concat_axis=0, tiled=True)  7.6 us
    pallas_call x1, Pallas kernels, per_device(): call(seven_kernel, 'seven', [shape(2 * WIDE, WIDE)] + [shape(2 * WIDE, WI...  6.24 us
    ppermute x1, starting transfers between devices, per_device(): theirs = lax.ppermute(eighth(False), 'core', swap)  4.45 us
    ppermute x1, starting transfers between devices, per_device(): pair = lax.ppermute(pair, 'zb', swap)  3.55 us
  transfers between devices with their start and end apart: 11, of which 8 were waited for; matrix products, arithmetic and copies ran while one was open for 0% of the time, Pallas kernels for 10%

profile of v7, /device:TPU:1, one launch (start us, length us, event | category | flops | bytes accessed | tf_op | source)
XLA Modules:
  0.0 129.0 jit_solution(2071579477259580606)
XLA Ops:
  0.0 1.9 %blocks.1 = f32[16,12,384]{2,1,0:T(8,128)} custom-call(f32[12,6144]{1,0:T(8,128)} %b_ref.1), custom_call_target="tpu_custom_call" | custom-call | flops 1 | bytes 1048576 | tf_op jit(solution)/shard_map/blocks/pallas_call | solution.py:235
  1.9 7.6 %all-to-all-start.1 = ((f32[16,12,384]{2,1,0:T(8,128)}), f32[16,12,384]{2,1,0:T(8,128)S(1)}, u32[]{:S(2)}, u32[]{:S(2)}) async-start(f32[16,12,384]{2,1,0:T(8,128)} %blocks.1), calls=%async_computation.1 | async-start | bytes 786432 | tf_op jit(solution)/shard_map/all_to_all | solution.py:246
  9.5 0.1 pad_add_fusion.where_ref.refs_0_
  9.6 0.9 halves.1
  10.5 3.5 %collective-permute-start = (f32[12,3072]{1,0:T(8,128)S(1)}, f32[12,3072]{1,0:T(8,128)S(1)}, u32[]{:S(2)}, u32[]{:S(2)}) collective-permute-start(f32[12,3072]{1,0:T(8,128)S(1)} %get-tuple-element.20), channel_id=1, source_target_pairs={{0,64},{64,0},{1,65},{65,1},{2,66},{66,2},{3,67},{67,3},{4,68},{68... | collective-permute-start | bytes 442376 | tf_op jit(solution)/shard_map/ppermute | solution.py:234
  14.0 3.3 %collective-permute-done.pair_ref = f32[12,3072]{1,0:T(8,128)S(1)} collective-permute-done((f32[12,3072]{1,0:T(8,128)S(1)}, f32[12,3072]{1,0:T(8,128)S(1)}, u32[]{:S(2)}, u32[]{:S(2)}) %collective-permute-start) | collective-permute-done | bytes 147488 | tf_op jit(solution)/shard_map/ppermute | solution.py:234
  17.4 2.8 %spread.1 = f32[32,24,1536]{2,1,0:T(8,128)} custom-call(f32[12,3072]{1,0:T(8,128)S(1)} %get-tuple-element.19.own_ref, f32[12,3072]{1,0:T(8,128)S(1)} %collective-permute-done.pair_ref, s32[1,384]{1,0:T(1,128)S(1)} %copy-done.2), custom_call_target="tpu_custom_call" | custom-call | flops 169869312 | bytes 6291456 | tf_op jit(solution)/shard_map/spread/pallas_call | solution.py:265
  20.2 0.0 copy-start.1
  20.3 10.8 %all-to-all-start = ((f32[32,24,1536]{2,1,0:T(8,128)}), f32[32,24,1536]{2,1,0:T(8,128)}, u32[]{:S(2)}, u32[]{:S(2)}) async-start(f32[32,24,1536]{2,1,0:T(8,128)} %spread.1), calls=%async_computation | async-start | bytes 9437184 | tf_op jit(solution)/shard_map/all_to_all | solution.py:276
  31.1 3.7 %collective-permute-start.1 = (f32[192,384]{1,0:T(8,128)S(1)}, f32[192,384]{1,0:T(8,128)S(1)}, u32[]{:S(2)}, u32[]{:S(2)}) collective-permute-start(f32[192,384]{1,0:T(8,128)S(1)} %stack.21.refs_0_), channel_id=1, source_target_pairs={{0,128},{128,256},{256,384},{384,1},{1,129},{129,257},{257,385},{3... | collective-permute-start | bytes 884744 | tf_op jit(solution)/shard_map/ppermute | solution.py:216
  34.8 8.4 %collective-permute-start.2 = (f32[192,384]{1,0:T(8,128)S(1)}, f32[192,384]{1,0:T(8,128)S(1)}, u32[]{:S(2)}, u32[]{:S(2)}) collective-permute-start(f32[192,384]{1,0:T(8,128)S(1)} %stack.21.refs_0_), channel_id=1, source_target_pairs={{0,385},{128,0},{256,128},{384,256},{1,384},{129,1},{257,129},{385... | collective-permute-start | bytes 884744 | tf_op jit(solution)/shard_map/ppermute | solution.py:216
  43.2 7.5 %collective-permute-done.1.refs_1_ = f32[192,384]{1,0:T(8,128)S(1)} collective-permute-done((f32[192,384]{1,0:T(8,128)S(1)}, f32[192,384]{1,0:T(8,128)S(1)}, u32[]{:S(2)}, u32[]{:S(2)}) %collective-permute-start.1) | collective-permute-done | bytes 294944 | tf_op jit(solution)/shard_map/ppermute | solution.py:216
  50.7 2.5 %collective-permute-start.3 = (f32[192,384]{1,0:T(8,128)S(1)}, f32[192,384]{1,0:T(8,128)S(1)}, u32[]{:S(2)}, u32[]{:S(2)}) collective-permute-start(f32[192,384]{1,0:T(8,128)S(1)} %collective-permute-done.1.refs_1_), channel_id=1, source_target_pairs={{0,128},{128,256},{256,384},{384,1},{1,129},{129,257},{257,385},{3... | collective-permute-start | bytes 884744 | tf_op jit(solution)/shard_map/ppermute | solution.py:216
  53.2 1.0 collective-permute-done.2.refs_2_
  54.2 7.9 %collective-permute-start.4 = (f32[192,384]{1,0:T(8,128)S(1)}, f32[192,384]{1,0:T(8,128)S(1)}, u32[]{:S(2)}, u32[]{:S(2)}) collective-permute-start(f32[192,384]{1,0:T(8,128)S(1)} %collective-permute-done.2.refs_2_), channel_id=1, source_target_pairs={{0,385},{128,0},{256,128},{384,256},{1,384},{129,1},{257,129},{385... | collective-permute-start | bytes 884744 | tf_op jit(solution)/shard_map/ppermute | solution.py:216
  62.1 8.9 %collective-permute-start.5 = (f32[192,384]{1,0:T(8,128)S(1)}, f32[192,384]{1,0:T(8,128)S(1)}, u32[]{:S(2)}, u32[]{:S(2)}) collective-permute-start(f32[192,384]{1,0:T(8,128)S(1)} %collective-permute-done.3.refs_3_), channel_id=1, source_target_pairs={{0,128},{128,256},{256,384},{384,1},{1,129},{129,257},{257,385},{3... | collective-permute-start | bytes 884744 | tf_op jit(solution)/shard_map/ppermute | solution.py:216
  71.0 3.3 %collective-permute-done.4.refs_4_ = f32[192,384]{1,0:T(8,128)S(1)} collective-permute-done((f32[192,384]{1,0:T(8,128)S(1)}, f32[192,384]{1,0:T(8,128)S(1)}, u32[]{:S(2)}, u32[]{:S(2)}) %collective-permute-start.4) | collective-permute-done | bytes 294944 | tf_op jit(solution)/shard_map/ppermute | solution.py:216
  74.4 6.5 %collective-permute-start.6 = (f32[192,384]{1,0:T(8,128)S(1)}, f32[192,384]{1,0:T(8,128)S(1)}, u32[]{:S(2)}, u32[]{:S(2)}) collective-permute-start(f32[192,384]{1,0:T(8,128)S(1)} %collective-permute-done.4.refs_4_), channel_id=1, source_target_pairs={{0,385},{128,0},{256,128},{384,256},{1,384},{129,1},{257,129},{385... | collective-permute-start | bytes 884744 | tf_op jit(solution)/shard_map/ppermute | solution.py:216
  80.8 3.6 %collective-permute-done.5.refs_5_ = f32[192,384]{1,0:T(8,128)S(1)} collective-permute-done((f32[192,384]{1,0:T(8,128)S(1)}, f32[192,384]{1,0:T(8,128)S(1)}, u32[]{:S(2)}, u32[]{:S(2)}) %collective-permute-start.5) | collective-permute-done | bytes 294944 | tf_op jit(solution)/shard_map/ppermute | solution.py:216
  84.4 4.9 %collective-permute-start.7 = (f32[192,384]{1,0:T(8,128)S(1)}, f32[192,384]{1,0:T(8,128)S(1)}, u32[]{:S(2)}, u32[]{:S(2)}) collective-permute-start(f32[192,384]{1,0:T(8,128)S(1)} %collective-permute-done.5.refs_5_), channel_id=1, source_target_pairs={{0,128},{128,256},{256,384},{384,1},{1,129},{129,257},{257,385},{3... | collective-permute-start | bytes 884744 | tf_op jit(solution)/shard_map/ppermute | solution.py:216
  89.4 0.7 shifts.1
  90.1 0.4 collective-permute-done.6.refs_6_
  90.5 1.0 place.1
  91.5 6.2 %seven.1 = (f32[768,384]{1,0:T(8,128)S(1)}, bf16[768,384]{1,0:T(8,128)(2,1)S(1)}, bf16[768,384]{1,0:T(8,128)(2,1)S(1)}) custom-call(s32[4]{0:T(128)S(1)} %pad_add_fusion.where_ref.refs_0_, f32[16,2,24,1536]{3,2,1,0:T(8,128)} %bitcast.4.rows_ref, bf16[1536,384]{1,0:T(8,128)(2,1)S(1)} %get-tuple-element.21.high_ref, ...), custom_call_target="tpu_custom_call" | custom-call | flops 2717908992 | bytes 7077888 | tf_op jit(solution)/shard_map/seven/pallas_call | solution.py:298
  97.7 0.9 collective-permute-done.7.refs_4_
  98.6 1.3 %eighth_theirs.1 = f32[384,384]{1,0:T(8,128)S(1)} custom-call(s32[4]{0:T(128)S(1)} %pad_add_fusion.where_ref.refs_0_, f32[768,384]{1,0:T(8,128)S(1)} %get-tuple-element.28.refs_1_, bf16[768,384]{1,0:T(8,128)(2,1)S(1)} %get-tuple-element.29.refs_2_, bf16[768,384]{1,0:T(8,128)(2,1)S(1)} %get-tuple-element.30.refs_3_, f32[192,384]{1,0:T(8,128)S(1)} %collective-permute-done.7.refs_4_), custom_call_target="tpu_custom_call" | custom-call | flops 339738624 | bytes 3145728 | tf_op jit(solution)/shard_map/eighth_theirs/pallas_call | solution.py:313
  99.9 4.5 %collective-permute-start.8 = (f32[384,384]{1,0:T(8,128)S(1)}, f32[384,384]{1,0:T(8,128)S(1)}, u32[]{:S(2)}, u32[]{:S(2)}) collective-permute-start(f32[384,384]{1,0:T(8,128)S(1)} %eighth_theirs.1), channel_id=1, source_target_pairs={{0,32},{32,0},{1,33},{33,1},{2,34},{34,2},{3,35},{35,3},{4,36},{36... | collective-permute-start | bytes 1769480 | tf_op jit(solution)/shard_map/ppermute | solution.py:325
  104.4 1.3 %eighth_mine.1.own_ref = f32[384,384]{1,0:T(8,128)S(1)} custom-call(s32[4]{0:T(128)S(1)} %pad_add_fusion.where_ref.refs_0_, f32[768,384]{1,0:T(8,128)S(1)} %get-tuple-element.28.refs_1_, bf16[768,384]{1,0:T(8,128)(2,1)S(1)} %get-tuple-element.29.refs_2_, bf16[768,384]{1,0:T(8,128)(2,1)S(1)} %get-tuple-element.30.refs_3_, ...), custom_call_target="tpu_custom_call" | custom-call | flops 339738624 | bytes 3145728 | tf_op jit(solution)/shard_map/eighth_mine/pallas_call | solution.py:313
  105.7 0.3 collective-permute-done.8.other_ref
  106.0 0.6 pack.1
  106.6 21.6 %all_to_all.15.parts_ref = f32[32,36,128]{2,1,0:T(8,128)S(1)} all-to-all(f32[32,36,128]{2,1,0:T(8,128)S(1)} %pack.1), channel_id=1, replica_groups=mesh['zl4'=4,'zb'=2,'core'=2,'y'=4,'x'=4,'zhi'=2] {'zb','y','x'}, dimensions={0} | all-to-all | bytes 1179648 | tf_op jit(solution)/shard_map/all_to_all | solution.py:337
  128.2 0.8 divide.1
  (15 shorter events, 0.1 us)
Async XLA Ops:
  0.0 17.4 %copy-start.2 = (s32[1,384]{1,0:T(1,128)S(1)}, s32[1,384]{1,0:T(1,128)}, u32[]{:S(2)}) copy-start(s32[1,384]{1,0:T(1,128)} %constant.37.clone.source_ref) | copy-start | bytes 4612
  0.0 9.6 %copy-start = (f32[12,6144]{1,0:T(8,128)S(1)}, f32[12,6144]{1,0:T(8,128)}, u32[]{:S(2)}) copy-start(f32[12,6144]{1,0:T(8,128)} %a_ref.1) | copy-start | bytes 884740
  1.9 18.4 %all-to-all-start.1 = ((f32[16,12,384]{2,1,0:T(8,128)}), f32[16,12,384]{2,1,0:T(8,128)S(1)}, u32[]{:S(2)}, u32[]{:S(2)}) async-start(f32[16,12,384]{2,1,0:T(8,128)} %blocks.1), calls=%async_computation.1 | async-start | bytes 786432 | tf_op jit(solution)/shard_map/all_to_all | solution.py:246
  10.5 6.9 %collective-permute-start = (f32[12,3072]{1,0:T(8,128)S(1)}, f32[12,3072]{1,0:T(8,128)S(1)}, u32[]{:S(2)}, u32[]{:S(2)}) collective-permute-start(f32[12,3072]{1,0:T(8,128)S(1)} %get-tuple-element.20), channel_id=1, source_target_pairs={{0,64},{64,0},{1,65},{65,1},{2,66},{66,2},{3,67},{67,3},{4,68},{68... | collective-permute-start | bytes 442376 | tf_op jit(solution)/shard_map/ppermute | solution.py:234
  20.2 69.2 %copy-start.1 = (f32[1536]{0:T(1024)S(1)}, f32[1536]{0:T(1024)}, u32[]{:S(2)}) copy-start(f32[1536]{0:T(1024)} %lanes_ref.1) | copy-start | bytes 18436
  20.2 69.2 %copy-start.3 = (f32[150]{0:T(256)S(1)}, f32[150]{0:T(256)}, u32[]{:S(2)}) copy-start(f32[150]{0:T(256)} %occ_ref.1) | copy-start | bytes 1804
  20.2 69.2 %copy-start.4 = (s32[4]{0:T(128)S(1)}, s32[4]{0:T(128)}, u32[]{:S(2)}) copy-start(s32[4]{0:T(128)} %wi_ref.1) | copy-start | bytes 52
  20.2 69.2 %copy-start.5 = (s32[4]{0:T(128)S(1)}, s32[4]{0:T(128)}, u32[]{:S(2)}) copy-start(s32[4]{0:T(128)} %wj_ref.1) | copy-start | bytes 52
  20.3 71.2 %all-to-all-start = ((f32[32,24,1536]{2,1,0:T(8,128)}), f32[32,24,1536]{2,1,0:T(8,128)}, u32[]{:S(2)}, u32[]{:S(2)}) async-start(f32[32,24,1536]{2,1,0:T(8,128)} %spread.1), calls=%async_computation | async-start | bytes 9437184 | tf_op jit(solution)/shard_map/all_to_all | solution.py:276
  31.1 19.6 %collective-permute-start.1 = (f32[192,384]{1,0:T(8,128)S(1)}, f32[192,384]{1,0:T(8,128)S(1)}, u32[]{:S(2)}, u32[]{:S(2)}) collective-permute-start(f32[192,384]{1,0:T(8,128)S(1)} %stack.21.refs_0_), channel_id=1, source_target_pairs={{0,128},{128,256},{256,384},{384,1},{1,129},{129,257},{257,385},{3... | collective-permute-start | bytes 884744 | tf_op jit(solution)/shard_map/ppermute | solution.py:216
  34.8 19.5 %collective-permute-start.2 = (f32[192,384]{1,0:T(8,128)S(1)}, f32[192,384]{1,0:T(8,128)S(1)}, u32[]{:S(2)}, u32[]{:S(2)}) collective-permute-start(f32[192,384]{1,0:T(8,128)S(1)} %stack.21.refs_0_), channel_id=1, source_target_pairs={{0,385},{128,0},{256,128},{384,256},{1,384},{129,1},{257,129},{385... | collective-permute-start | bytes 884744 | tf_op jit(solution)/shard_map/ppermute | solution.py:216
  50.7 11.4 %collective-permute-start.3 = (f32[192,384]{1,0:T(8,128)S(1)}, f32[192,384]{1,0:T(8,128)S(1)}, u32[]{:S(2)}, u32[]{:S(2)}) collective-permute-start(f32[192,384]{1,0:T(8,128)S(1)} %collective-permute-done.1.refs_1_), channel_id=1, source_target_pairs={{0,128},{128,256},{256,384},{384,1},{1,129},{129,257},{257,385},{3... | collective-permute-start | bytes 884744 | tf_op jit(solution)/shard_map/ppermute | solution.py:216
  54.2 20.1 %collective-permute-start.4 = (f32[192,384]{1,0:T(8,128)S(1)}, f32[192,384]{1,0:T(8,128)S(1)}, u32[]{:S(2)}, u32[]{:S(2)}) collective-permute-start(f32[192,384]{1,0:T(8,128)S(1)} %collective-permute-done.2.refs_2_), channel_id=1, source_target_pairs={{0,385},{128,0},{256,128},{384,256},{1,384},{129,1},{257,129},{385... | collective-permute-start | bytes 884744 | tf_op jit(solution)/shard_map/ppermute | solution.py:216
  62.1 22.3 %collective-permute-start.5 = (f32[192,384]{1,0:T(8,128)S(1)}, f32[192,384]{1,0:T(8,128)S(1)}, u32[]{:S(2)}, u32[]{:S(2)}) collective-permute-start(f32[192,384]{1,0:T(8,128)S(1)} %collective-permute-done.3.refs_3_), channel_id=1, source_target_pairs={{0,128},{128,256},{256,384},{384,1},{1,129},{129,257},{257,385},{3... | collective-permute-start | bytes 884744 | tf_op jit(solution)/shard_map/ppermute | solution.py:216
  74.4 16.1 %collective-permute-start.6 = (f32[192,384]{1,0:T(8,128)S(1)}, f32[192,384]{1,0:T(8,128)S(1)}, u32[]{:S(2)}, u32[]{:S(2)}) collective-permute-start(f32[192,384]{1,0:T(8,128)S(1)} %collective-permute-done.4.refs_4_), channel_id=1, source_target_pairs={{0,385},{128,0},{256,128},{384,256},{1,384},{129,1},{257,129},{385... | collective-permute-start | bytes 884744 | tf_op jit(solution)/shard_map/ppermute | solution.py:216
  84.4 14.2 %collective-permute-start.7 = (f32[192,384]{1,0:T(8,128)S(1)}, f32[192,384]{1,0:T(8,128)S(1)}, u32[]{:S(2)}, u32[]{:S(2)}) collective-permute-start(f32[192,384]{1,0:T(8,128)S(1)} %collective-permute-done.5.refs_5_), channel_id=1, source_target_pairs={{0,128},{128,256},{256,384},{384,1},{1,129},{129,257},{257,385},{3... | collective-permute-start | bytes 884744 | tf_op jit(solution)/shard_map/ppermute | solution.py:216
  99.9 6.1 %collective-permute-start.8 = (f32[384,384]{1,0:T(8,128)S(1)}, f32[384,384]{1,0:T(8,128)S(1)}, u32[]{:S(2)}, u32[]{:S(2)}) collective-permute-start(f32[384,384]{1,0:T(8,128)S(1)} %eighth_theirs.1), channel_id=1, source_target_pairs={{0,32},{32,0},{1,33},{33,1},{2,34},{34,2},{3,35},{35,3},{4,36},{36... | collective-permute-start | bytes 1769480 | tf_op jit(solution)/shard_map/ppermute | solution.py:325

commit v8 on v7

--- a/solution.py
+++ b/solution.py
@@ -114,6 +114,12 @@
         copy.wait()
 
 
+def product(a_high, a_low, b_high, b_low):
+    dot = lambda a, b: jnp.dot(a, b, preferred_element_type=F32)
+    both = dot(a_high, jnp.concatenate([b_high, b_low], axis=1))
+    return both[:, :WIDE] + (both[:, WIDE:] + dot(a_low, b_high))
+
+
 def block_of(ring, step):
     at = lax.rem(ring + 8 + step, 8)
     return lax.rem(at, 4), at // 4
@@ -141,21 +147,10 @@
             source = rows_ref.at[:, which, :, at]
             copies.append(pltpu.make_async_copy(source, left_ref.at[core, :, :, at], sems.at[core, k]))
             copies[-1].start()
-    for k in range(DEEP // STEP):
-        copies[2 * k].wait()
-        copies[2 * k + 1].wait()
-        at = slice(STEP * k, STEP * k + STEP)
-        a_high, a_low = in_two(left_ref[:, :, :, at].reshape(2 * WIDE, STEP))
-        b_high, b_low = high_ref[at, :], low_ref[at, :]
-        term = jnp.dot(
-            jnp.concatenate([a_high, a_low, a_high], axis=1),
-            jnp.concatenate([b_high, b_high, b_low], axis=0),
-            preferred_element_type=F32,
-        )
-        if k == 0:
-            part_ref[...] = term
-        else:
-            part_ref[...] += term
+    for copy in copies:
+        copy.wait()
+    a_high, a_low = in_two(left_ref[...].reshape(2 * WIDE, DEEP))
+    part_ref[...] = product(a_high, a_low, high_ref[...], low_ref[...])
     z, _ = block_of(where_ref[2], 4)
     last = left_ref[:, :, :, pl.ds(pl.multiple_of(z * WIDE, 128), WIDE)]
     run_high_ref[...], run_low_ref[...] = in_two(last.reshape(2 * WIDE, WIDE))
@@ -168,11 +163,8 @@
     at = pl.ds(pl.multiple_of(zhi * SHARD, 64), SHARD)
     high_ref[at, :], low_ref[at, :] = in_two(last_ref[...])
     rows = slice(0, WIDE) if mine else slice(WIDE, 2 * WIDE)
-    a_high, a_low, b_high, b_low = a_high_ref[rows, :], a_low_ref[rows, :], high_ref[...], low_ref[...]
-    out_ref[...] = part_ref[rows, :] + jnp.dot(
-        jnp.concatenate([a_high, a_low, a_high], axis=1),
-        jnp.concatenate([b_high, b_high, b_low], axis=0),
-        preferred_element_type=F32,
+    out_ref[...] = part_ref[rows, :] + product(
+        a_high_ref[rows, :], a_low_ref[rows, :], high_ref[...], low_ref[...]
     )
 
 

time: 130 us -> 130 us (level)
  no operation moved by 1% of the time
where the time goes in v8:
time: 130 us; the launch traced here: 129 us
  starting transfers between devices  69.1 us (53%)
  blocking collectives  21.6 us (17%)
  waiting for transfers between devices  20.1 us (15%)
  Pallas kernels  17.8 us (14%)
    ppermute x7, starting transfers between devices, turn(): lax.ppermute(x, ('zl4', 'zhi'), [(index(a), index(a + step)) for a in ran...  42.8 us
    all_to_all x1, blocking collectives, per_device(): lax.all_to_all(packed, ('zb', 'y', 'x'), split_axis=0, concat_axis=0, til...  21.6 us
    ppermute x7, waiting for transfers between devices, turn(): lax.ppermute(x, ('zl4', 'zhi'), [(index(a), index(a + step)) for a in ran...  16.4 us
    all_to_all x1, starting transfers between devices, per_device(): lax.all_to_all(spread, ('y', 'x', 'core'), split_axis=0, concat_axis=0, t...  10.8 us
    all_to_all x1, starting transfers between devices, per_device(): lax.all_to_all(blocks, PLANE, split_axis=0, concat_axis=0, tiled=True)  7.6 us
    pallas_call x1, Pallas kernels, per_device(): call(seven_kernel, 'seven', [shape(2 * WIDE, WIDE)] + [shape(2 * WIDE, WI...  6.53 us
    ppermute x1, starting transfers between devices, per_device(): theirs = lax.ppermute(eighth(False), 'core', swap)  4.45 us
    ppermute x1, starting transfers between devices, per_device(): pair = lax.ppermute(pair, 'zb', swap)  3.55 us
  transfers between devices with their start and end apart: 11, of which 8 were waited for; matrix products, arithmetic and copies ran while one was open for 0% of the time, Pallas kernels for 10%

profile of v8, /device:TPU:1, one launch (start us, length us, event | category | flops | bytes accessed | tf_op | source)
XLA Modules:
  0.0 129.0 jit_solution(16736791359210640544)
XLA Ops:
  0.0 1.9 %blocks.1 = f32[16,12,384]{2,1,0:T(8,128)} custom-call(f32[12,6144]{1,0:T(8,128)} %b_ref.1), custom_call_target="tpu_custom_call" | custom-call | flops 1 | bytes 1048576 | tf_op jit(solution)/shard_map/blocks/pallas_call | solution.py:227
  1.9 7.6 %all-to-all-start.1 = ((f32[16,12,384]{2,1,0:T(8,128)}), f32[16,12,384]{2,1,0:T(8,128)S(1)}, u32[]{:S(2)}, u32[]{:S(2)}) async-start(f32[16,12,384]{2,1,0:T(8,128)} %blocks.1), calls=%async_computation.1 | async-start | bytes 786432 | tf_op jit(solution)/shard_map/all_to_all | solution.py:238
  9.5 0.1 pad_add_fusion.where_ref.refs_0_
  9.6 0.9 halves.1
  10.5 3.5 %collective-permute-start = (f32[12,3072]{1,0:T(8,128)S(1)}, f32[12,3072]{1,0:T(8,128)S(1)}, u32[]{:S(2)}, u32[]{:S(2)}) collective-permute-start(f32[12,3072]{1,0:T(8,128)S(1)} %get-tuple-element.20), channel_id=1, source_target_pairs={{0,64},{64,0},{1,65},{65,1},{2,66},{66,2},{3,67},{67,3},{4,68},{68... | collective-permute-start | bytes 442376 | tf_op jit(solution)/shard_map/ppermute | solution.py:226
  14.0 3.3 %collective-permute-done.pair_ref = f32[12,3072]{1,0:T(8,128)S(1)} collective-permute-done((f32[12,3072]{1,0:T(8,128)S(1)}, f32[12,3072]{1,0:T(8,128)S(1)}, u32[]{:S(2)}, u32[]{:S(2)}) %collective-permute-start) | collective-permute-done | bytes 147488 | tf_op jit(solution)/shard_map/ppermute | solution.py:226
  17.4 2.8 %spread.1 = f32[32,24,1536]{2,1,0:T(8,128)} custom-call(f32[12,3072]{1,0:T(8,128)S(1)} %get-tuple-element.19.own_ref, f32[12,3072]{1,0:T(8,128)S(1)} %collective-permute-done.pair_ref, s32[1,384]{1,0:T(1,128)S(1)} %copy-done.2), custom_call_target="tpu_custom_call" | custom-call | flops 169869312 | bytes 6291456 | tf_op jit(solution)/shard_map/spread/pallas_call | solution.py:257
  20.2 0.0 copy-start.3
  20.3 10.8 %all-to-all-start = ((f32[32,24,1536]{2,1,0:T(8,128)}), f32[32,24,1536]{2,1,0:T(8,128)}, u32[]{:S(2)}, u32[]{:S(2)}) async-start(f32[32,24,1536]{2,1,0:T(8,128)} %spread.1), calls=%async_computation | async-start | bytes 9437184 | tf_op jit(solution)/shard_map/all_to_all | solution.py:268
  31.1 3.7 %collective-permute-start.1 = (f32[192,384]{1,0:T(8,128)S(1)}, f32[192,384]{1,0:T(8,128)S(1)}, u32[]{:S(2)}, u32[]{:S(2)}) collective-permute-start(f32[192,384]{1,0:T(8,128)S(1)} %stack.21.refs_0_), channel_id=1, source_target_pairs={{0,128},{128,256},{256,384},{384,1},{1,129},{129,257},{257,385},{3... | collective-permute-start | bytes 884744 | tf_op jit(solution)/shard_map/ppermute | solution.py:208
  34.8 8.4 %collective-permute-start.2 = (f32[192,384]{1,0:T(8,128)S(1)}, f32[192,384]{1,0:T(8,128)S(1)}, u32[]{:S(2)}, u32[]{:S(2)}) collective-permute-start(f32[192,384]{1,0:T(8,128)S(1)} %stack.21.refs_0_), channel_id=1, source_target_pairs={{0,385},{128,0},{256,128},{384,256},{1,384},{129,1},{257,129},{385... | collective-permute-start | bytes 884744 | tf_op jit(solution)/shard_map/ppermute | solution.py:208
  43.2 7.5 %collective-permute-done.1.refs_1_ = f32[192,384]{1,0:T(8,128)S(1)} collective-permute-done((f32[192,384]{1,0:T(8,128)S(1)}, f32[192,384]{1,0:T(8,128)S(1)}, u32[]{:S(2)}, u32[]{:S(2)}) %collective-permute-start.1) | collective-permute-done | bytes 294944 | tf_op jit(solution)/shard_map/ppermute | solution.py:208
  50.7 2.5 %collective-permute-start.3 = (f32[192,384]{1,0:T(8,128)S(1)}, f32[192,384]{1,0:T(8,128)S(1)}, u32[]{:S(2)}, u32[]{:S(2)}) collective-permute-start(f32[192,384]{1,0:T(8,128)S(1)} %collective-permute-done.1.refs_1_), channel_id=1, source_target_pairs={{0,128},{128,256},{256,384},{384,1},{1,129},{129,257},{257,385},{3... | collective-permute-start | bytes 884744 | tf_op jit(solution)/shard_map/ppermute | solution.py:208
  53.2 1.0 collective-permute-done.2.refs_2_
  54.2 7.9 %collective-permute-start.4 = (f32[192,384]{1,0:T(8,128)S(1)}, f32[192,384]{1,0:T(8,128)S(1)}, u32[]{:S(2)}, u32[]{:S(2)}) collective-permute-start(f32[192,384]{1,0:T(8,128)S(1)} %collective-permute-done.2.refs_2_), channel_id=1, source_target_pairs={{0,385},{128,0},{256,128},{384,256},{1,384},{129,1},{257,129},{385... | collective-permute-start | bytes 884744 | tf_op jit(solution)/shard_map/ppermute | solution.py:208
  62.1 8.9 %collective-permute-start.5 = (f32[192,384]{1,0:T(8,128)S(1)}, f32[192,384]{1,0:T(8,128)S(1)}, u32[]{:S(2)}, u32[]{:S(2)}) collective-permute-start(f32[192,384]{1,0:T(8,128)S(1)} %collective-permute-done.3.refs_3_), channel_id=1, source_target_pairs={{0,128},{128,256},{256,384},{384,1},{1,129},{129,257},{257,385},{3... | collective-permute-start | bytes 884744 | tf_op jit(solution)/shard_map/ppermute | solution.py:208
  71.0 3.3 %collective-permute-done.4.refs_4_ = f32[192,384]{1,0:T(8,128)S(1)} collective-permute-done((f32[192,384]{1,0:T(8,128)S(1)}, f32[192,384]{1,0:T(8,128)S(1)}, u32[]{:S(2)}, u32[]{:S(2)}) %collective-permute-start.4) | collective-permute-done | bytes 294944 | tf_op jit(solution)/shard_map/ppermute | solution.py:208
  74.4 6.5 %collective-permute-start.6 = (f32[192,384]{1,0:T(8,128)S(1)}, f32[192,384]{1,0:T(8,128)S(1)}, u32[]{:S(2)}, u32[]{:S(2)}) collective-permute-start(f32[192,384]{1,0:T(8,128)S(1)} %collective-permute-done.4.refs_4_), channel_id=1, source_target_pairs={{0,385},{128,0},{256,128},{384,256},{1,384},{129,1},{257,129},{385... | collective-permute-start | bytes 884744 | tf_op jit(solution)/shard_map/ppermute | solution.py:208
  80.8 3.6 %collective-permute-done.5.refs_5_ = f32[192,384]{1,0:T(8,128)S(1)} collective-permute-done((f32[192,384]{1,0:T(8,128)S(1)}, f32[192,384]{1,0:T(8,128)S(1)}, u32[]{:S(2)}, u32[]{:S(2)}) %collective-permute-start.5) | collective-permute-done | bytes 294944 | tf_op jit(solution)/shard_map/ppermute | solution.py:208
  84.4 4.9 %collective-permute-start.7 = (f32[192,384]{1,0:T(8,128)S(1)}, f32[192,384]{1,0:T(8,128)S(1)}, u32[]{:S(2)}, u32[]{:S(2)}) collective-permute-start(f32[192,384]{1,0:T(8,128)S(1)} %collective-permute-done.5.refs_5_), channel_id=1, source_target_pairs={{0,128},{128,256},{256,384},{384,1},{1,129},{129,257},{257,385},{3... | collective-permute-start | bytes 884744 | tf_op jit(solution)/shard_map/ppermute | solution.py:208
  89.4 0.7 shifts.1
  90.1 0.4 collective-permute-done.6.refs_6_
  90.5 1.0 place.1
  91.5 6.5 %seven.1 = (f32[768,384]{1,0:T(8,128)S(1)}, bf16[768,384]{1,0:T(8,128)(2,1)S(1)}, bf16[768,384]{1,0:T(8,128)(2,1)S(1)}) custom-call(s32[4]{0:T(128)S(1)} %pad_add_fusion.where_ref.refs_0_, f32[16,2,24,1536]{3,2,1,0:T(8,128)} %bitcast.4.rows_ref, bf16[1536,384]{1,0:T(8,128)(2,1)S(1)} %get-tuple-element.21.high_ref, ...), custom_call_target="tpu_custom_call" | custom-call | flops 2717908992 | bytes 7077888 | tf_op jit(solution)/shard_map/seven/pallas_call | solution.py:290
  98.0 0.6 collective-permute-done.7.refs_4_
  98.6 1.3 eighth_theirs.1
  99.9 4.5 %collective-permute-start.8 = (f32[384,384]{1,0:T(8,128)S(1)}, f32[384,384]{1,0:T(8,128)S(1)}, u32[]{:S(2)}, u32[]{:S(2)}) collective-permute-start(f32[384,384]{1,0:T(8,128)S(1)} %eighth_theirs.1), channel_id=1, source_target_pairs={{0,32},{32,0},{1,33},{33,1},{2,34},{34,2},{3,35},{35,3},{4,36},{36... | collective-permute-start | bytes 1769480 | tf_op jit(solution)/shard_map/ppermute | solution.py:317
  104.4 1.3 eighth_mine.1.own_ref
  105.6 0.3 collective-permute-done.8.other_ref
  106.0 0.6 pack.1
  106.6 21.6 %all_to_all.15.parts_ref = f32[32,36,128]{2,1,0:T(8,128)S(1)} all-to-all(f32[32,36,128]{2,1,0:T(8,128)S(1)} %pack.1), channel_id=1, replica_groups=mesh['zl4'=4,'zb'=2,'core'=2,'y'=4,'x'=4,'zhi'=2] {'zb','y','x'}, dimensions={0} | all-to-all | bytes 1179648 | tf_op jit(solution)/shard_map/all_to_all | solution.py:329
  128.2 0.8 divide.1
  (15 shorter events, 0.1 us)
Async XLA Ops:
  0.0 17.4 %copy-start.2 = (s32[1,384]{1,0:T(1,128)S(1)}, s32[1,384]{1,0:T(1,128)}, u32[]{:S(2)}) copy-start(s32[1,384]{1,0:T(1,128)} %constant.37.clone.source_ref) | copy-start | bytes 4612
  0.0 9.6 %copy-start = (f32[12,6144]{1,0:T(8,128)S(1)}, f32[12,6144]{1,0:T(8,128)}, u32[]{:S(2)}) copy-start(f32[12,6144]{1,0:T(8,128)} %a_ref.1) | copy-start | bytes 884740
  1.9 18.4 %all-to-all-start.1 = ((f32[16,12,384]{2,1,0:T(8,128)}), f32[16,12,384]{2,1,0:T(8,128)S(1)}, u32[]{:S(2)}, u32[]{:S(2)}) async-start(f32[16,12,384]{2,1,0:T(8,128)} %blocks.1), calls=%async_computation.1 | async-start | bytes 786432 | tf_op jit(solution)/shard_map/all_to_all | solution.py:238
  10.5 6.9 %collective-permute-start = (f32[12,3072]{1,0:T(8,128)S(1)}, f32[12,3072]{1,0:T(8,128)S(1)}, u32[]{:S(2)}, u32[]{:S(2)}) collective-permute-start(f32[12,3072]{1,0:T(8,128)S(1)} %get-tuple-element.20), channel_id=1, source_target_pairs={{0,64},{64,0},{1,65},{65,1},{2,66},{66,2},{3,67},{67,3},{4,68},{68... | collective-permute-start | bytes 442376 | tf_op jit(solution)/shard_map/ppermute | solution.py:226
  20.2 69.2 %copy-start.1 = (f32[1536]{0:T(1024)S(1)}, f32[1536]{0:T(1024)}, u32[]{:S(2)}) copy-start(f32[1536]{0:T(1024)} %lanes_ref.1) | copy-start | bytes 18436
  20.2 69.2 %copy-start.3 = (f32[150]{0:T(256)S(1)}, f32[150]{0:T(256)}, u32[]{:S(2)}) copy-start(f32[150]{0:T(256)} %occ_ref.1) | copy-start | bytes 1804
  20.2 69.2 %copy-start.4 = (s32[4]{0:T(128)S(1)}, s32[4]{0:T(128)}, u32[]{:S(2)}) copy-start(s32[4]{0:T(128)} %wi_ref.1) | copy-start | bytes 52
  20.2 69.2 %copy-start.5 = (s32[4]{0:T(128)S(1)}, s32[4]{0:T(128)}, u32[]{:S(2)}) copy-start(s32[4]{0:T(128)} %wj_ref.1) | copy-start | bytes 52
  20.3 71.2 %all-to-all-start = ((f32[32,24,1536]{2,1,0:T(8,128)}), f32[32,24,1536]{2,1,0:T(8,128)}, u32[]{:S(2)}, u32[]{:S(2)}) async-start(f32[32,24,1536]{2,1,0:T(8,128)} %spread.1), calls=%async_computation | async-start | bytes 9437184 | tf_op jit(solution)/shard_map/all_to_all | solution.py:268
  31.1 19.6 %collective-permute-start.1 = (f32[192,384]{1,0:T(8,128)S(1)}, f32[192,384]{1,0:T(8,128)S(1)}, u32[]{:S(2)}, u32[]{:S(2)}) collective-permute-start(f32[192,384]{1,0:T(8,128)S(1)} %stack.21.refs_0_), channel_id=1, source_target_pairs={{0,128},{128,256},{256,384},{384,1},{1,129},{129,257},{257,385},{3... | collective-permute-start | bytes 884744 | tf_op jit(solution)/shard_map/ppermute | solution.py:208
  34.8 19.5 %collective-permute-start.2 = (f32[192,384]{1,0:T(8,128)S(1)}, f32[192,384]{1,0:T(8,128)S(1)}, u32[]{:S(2)}, u32[]{:S(2)}) collective-permute-start(f32[192,384]{1,0:T(8,128)S(1)} %stack.21.refs_0_), channel_id=1, source_target_pairs={{0,385},{128,0},{256,128},{384,256},{1,384},{129,1},{257,129},{385... | collective-permute-start | bytes 884744 | tf_op jit(solution)/shard_map/ppermute | solution.py:208
  50.7 11.4 %collective-permute-start.3 = (f32[192,384]{1,0:T(8,128)S(1)}, f32[192,384]{1,0:T(8,128)S(1)}, u32[]{:S(2)}, u32[]{:S(2)}) collective-permute-start(f32[192,384]{1,0:T(8,128)S(1)} %collective-permute-done.1.refs_1_), channel_id=1, source_target_pairs={{0,128},{128,256},{256,384},{384,1},{1,129},{129,257},{257,385},{3... | collective-permute-start | bytes 884744 | tf_op jit(solution)/shard_map/ppermute | solution.py:208
  54.2 20.1 %collective-permute-start.4 = (f32[192,384]{1,0:T(8,128)S(1)}, f32[192,384]{1,0:T(8,128)S(1)}, u32[]{:S(2)}, u32[]{:S(2)}) collective-permute-start(f32[192,384]{1,0:T(8,128)S(1)} %collective-permute-done.2.refs_2_), channel_id=1, source_target_pairs={{0,385},{128,0},{256,128},{384,256},{1,384},{129,1},{257,129},{385... | collective-permute-start | bytes 884744 | tf_op jit(solution)/shard_map/ppermute | solution.py:208
  62.1 22.3 %collective-permute-start.5 = (f32[192,384]{1,0:T(8,128)S(1)}, f32[192,384]{1,0:T(8,128)S(1)}, u32[]{:S(2)}, u32[]{:S(2)}) collective-permute-start(f32[192,384]{1,0:T(8,128)S(1)} %collective-permute-done.3.refs_3_), channel_id=1, source_target_pairs={{0,128},{128,256},{256,384},{384,1},{1,129},{129,257},{257,385},{3... | collective-permute-start | bytes 884744 | tf_op jit(solution)/shard_map/ppermute | solution.py:208
  74.4 16.1 %collective-permute-start.6 = (f32[192,384]{1,0:T(8,128)S(1)}, f32[192,384]{1,0:T(8,128)S(1)}, u32[]{:S(2)}, u32[]{:S(2)}) collective-permute-start(f32[192,384]{1,0:T(8,128)S(1)} %collective-permute-done.4.refs_4_), channel_id=1, source_target_pairs={{0,385},{128,0},{256,128},{384,256},{1,384},{129,1},{257,129},{385... | collective-permute-start | bytes 884744 | tf_op jit(solution)/shard_map/ppermute | solution.py:208
  84.4 14.2 %collective-permute-start.7 = (f32[192,384]{1,0:T(8,128)S(1)}, f32[192,384]{1,0:T(8,128)S(1)}, u32[]{:S(2)}, u32[]{:S(2)}) collective-permute-start(f32[192,384]{1,0:T(8,128)S(1)} %collective-permute-done.5.refs_5_), channel_id=1, source_target_pairs={{0,128},{128,256},{256,384},{384,1},{1,129},{129,257},{257,385},{3... | collective-permute-start | bytes 884744 | tf_op jit(solution)/shard_map/ppermute | solution.py:208
  99.9 6.1 %collective-permute-start.8 = (f32[384,384]{1,0:T(8,128)S(1)}, f32[384,384]{1,0:T(8,128)S(1)}, u32[]{:S(2)}, u32[]{:S(2)}) collective-permute-start(f32[384,384]{1,0:T(8,128)S(1)} %eighth_theirs.1), channel_id=1, source_target_pairs={{0,32},{32,0},{1,33},{33,1},{2,34},{34,2},{3,35},{35,3},{4,36},{36... | collective-permute-start | bytes 1769480 | tf_op jit(solution)/shard_map/ppermute | solution.py:317

commit v9 on v7

--- a/solution.py
+++ b/solution.py
@@ -184,7 +184,7 @@
             total = own_ref[rows, :] + other_ref[rows, :]
             for g in range(3):
                 at = slice(ROWS * g, ROWS * g + ROWS)
-                out_ref[16 * zb + i, at, :] = total[:, 128 * g : 128 * g + 128]
+                out_ref[16 * zb + i % 4 * 4 + i // 4, at, :] = total[:, 128 * g : 128 * g + 128]
 
 
 def shifts_kernel(where_ref, wi_ref, wj_ref, occ_ref, virt_ref, lanes_ref, row_ref, col_ref):
@@ -273,7 +273,7 @@
         6 << 20,
         [pltpu.VMEM((2, 2 * ROWS, DEEP), F32), pltpu.SemaphoreType.DMA((32,))],
     )(own, pair, jnp.asarray(column_source()))
-    rows = lax.all_to_all(spread, ("y", "x", "core"), split_axis=0, concat_axis=0, tiled=True)
+    rows = lax.all_to_all(spread, ("x", "y", "core"), split_axis=0, concat_axis=0, tiled=True)
 
     row, col = call(
         shifts_kernel,

time: 130 us -> 130 us (level)
  no operation moved by 1% of the time
where the time goes in v9:
time: 130 us; the launch traced here: 129 us
  starting transfers between devices  68.8 us (53%)
  blocking collectives  21.5 us (17%)
  waiting for transfers between devices  20.8 us (16%)
  Pallas kernels  17.6 us (14%)
    ppermute x7, starting transfers between devices, turn(): lax.ppermute(x, ('zl4', 'zhi'), [(index(a), index(a + step)) for a in ran...  42.6 us
    all_to_all x1, blocking collectives, per_device(): lax.all_to_all(packed, ('zb', 'y', 'x'), split_axis=0, concat_axis=0, til...  21.5 us
    ppermute x7, waiting for transfers between devices, turn(): lax.ppermute(x, ('zl4', 'zhi'), [(index(a), index(a + step)) for a in ran...  17.2 us
    all_to_all x1, starting transfers between devices, per_device(): lax.all_to_all(spread, ('x', 'y', 'core'), split_axis=0, concat_axis=0, t...  10.8 us
    all_to_all x1, starting transfers between devices, per_device(): lax.all_to_all(blocks, PLANE, split_axis=0, concat_axis=0, tiled=True)  7.6 us
    pallas_call x1, Pallas kernels, per_device(): call(seven_kernel, 'seven', [shape(2 * WIDE, WIDE)] + [shape(2 * WIDE, WI...  6.26 us
    ppermute x1, starting transfers between devices, per_device(): theirs = lax.ppermute(eighth(False), 'core', swap)  4.28 us
    ppermute x1, starting transfers between devices, per_device(): pair = lax.ppermute(pair, 'zb', swap)  3.55 us
  transfers between devices with their start and end apart: 11, of which 8 were waited for; matrix products, arithmetic and copies ran while one was open for 0% of the time, Pallas kernels for 10%

profile of v9, /device:TPU:1, one launch (start us, length us, event | category | flops | bytes accessed | tf_op | source)
XLA Modules:
  0.0 129.0 jit_solution(12372101167489686460)
XLA Ops:
  0.0 1.9 %blocks.1 = f32[16,12,384]{2,1,0:T(8,128)} custom-call(f32[12,6144]{1,0:T(8,128)} %b_ref.1), custom_call_target="tpu_custom_call" | custom-call | flops 1 | bytes 1048576 | tf_op jit(solution)/shard_map/blocks/pallas_call | solution.py:235
  1.9 7.6 %all-to-all-start.1 = ((f32[16,12,384]{2,1,0:T(8,128)}), f32[16,12,384]{2,1,0:T(8,128)S(1)}, u32[]{:S(2)}, u32[]{:S(2)}) async-start(f32[16,12,384]{2,1,0:T(8,128)} %blocks.1), calls=%async_computation.1 | async-start | bytes 786432 | tf_op jit(solution)/shard_map/all_to_all | solution.py:246
  9.5 0.1 pad_add_fusion.where_ref.refs_0_
  9.6 0.9 halves.1
  10.5 3.5 %collective-permute-start = (f32[12,3072]{1,0:T(8,128)S(1)}, f32[12,3072]{1,0:T(8,128)S(1)}, u32[]{:S(2)}, u32[]{:S(2)}) collective-permute-start(f32[12,3072]{1,0:T(8,128)S(1)} %get-tuple-element.20), channel_id=1, source_target_pairs={{0,64},{64,0},{1,65},{65,1},{2,66},{66,2},{3,67},{67,3},{4,68},{68... | collective-permute-start | bytes 442376 | tf_op jit(solution)/shard_map/ppermute | solution.py:234
  14.0 3.3 %collective-permute-done.pair_ref = f32[12,3072]{1,0:T(8,128)S(1)} collective-permute-done((f32[12,3072]{1,0:T(8,128)S(1)}, f32[12,3072]{1,0:T(8,128)S(1)}, u32[]{:S(2)}, u32[]{:S(2)}) %collective-permute-start) | collective-permute-done | bytes 147488 | tf_op jit(solution)/shard_map/ppermute | solution.py:234
  17.4 2.8 %spread.1 = f32[32,24,1536]{2,1,0:T(8,128)} custom-call(f32[12,3072]{1,0:T(8,128)S(1)} %get-tuple-element.19.own_ref, f32[12,3072]{1,0:T(8,128)S(1)} %collective-permute-done.pair_ref, s32[1,384]{1,0:T(1,128)S(1)} %copy-done.2), custom_call_target="tpu_custom_call" | custom-call | flops 169869312 | bytes 6291456 | tf_op jit(solution)/shard_map/spread/pallas_call | solution.py:265
  20.2 0.0 copy-start.1
  20.3 10.8 %all-to-all-start = ((f32[32,24,1536]{2,1,0:T(8,128)}), f32[32,24,1536]{2,1,0:T(8,128)}, u32[]{:S(2)}, u32[]{:S(2)}) async-start(f32[32,24,1536]{2,1,0:T(8,128)} %spread.1), calls=%async_computation | async-start | bytes 9437184 | tf_op jit(solution)/shard_map/all_to_all | solution.py:276
  31.1 3.7 %collective-permute-start.1 = (f32[192,384]{1,0:T(8,128)S(1)}, f32[192,384]{1,0:T(8,128)S(1)}, u32[]{:S(2)}, u32[]{:S(2)}) collective-permute-start(f32[192,384]{1,0:T(8,128)S(1)} %stack.21.refs_0_), channel_id=1, source_target_pairs={{0,128},{128,256},{256,384},{384,1},{1,129},{129,257},{257,385},{3... | collective-permute-start | bytes 884744 | tf_op jit(solution)/shard_map/ppermute | solution.py:216
  34.8 8.4 %collective-permute-start.2 = (f32[192,384]{1,0:T(8,128)S(1)}, f32[192,384]{1,0:T(8,128)S(1)}, u32[]{:S(2)}, u32[]{:S(2)}) collective-permute-start(f32[192,384]{1,0:T(8,128)S(1)} %stack.21.refs_0_), channel_id=1, source_target_pairs={{0,385},{128,0},{256,128},{384,256},{1,384},{129,1},{257,129},{385... | collective-permute-start | bytes 884744 | tf_op jit(solution)/shard_map/ppermute | solution.py:216
  43.2 7.5 %collective-permute-done.1.refs_1_ = f32[192,384]{1,0:T(8,128)S(1)} collective-permute-done((f32[192,384]{1,0:T(8,128)S(1)}, f32[192,384]{1,0:T(8,128)S(1)}, u32[]{:S(2)}, u32[]{:S(2)}) %collective-permute-start.1) | collective-permute-done | bytes 294944 | tf_op jit(solution)/shard_map/ppermute | solution.py:216
  50.7 2.5 %collective-permute-start.3 = (f32[192,384]{1,0:T(8,128)S(1)}, f32[192,384]{1,0:T(8,128)S(1)}, u32[]{:S(2)}, u32[]{:S(2)}) collective-permute-start(f32[192,384]{1,0:T(8,128)S(1)} %collective-permute-done.1.refs_1_), channel_id=1, source_target_pairs={{0,128},{128,256},{256,384},{384,1},{1,129},{129,257},{257,385},{3... | collective-permute-start | bytes 884744 | tf_op jit(solution)/shard_map/ppermute | solution.py:216
  53.2 1.0 collective-permute-done.2.refs_2_
  54.2 7.9 %collective-permute-start.4 = (f32[192,384]{1,0:T(8,128)S(1)}, f32[192,384]{1,0:T(8,128)S(1)}, u32[]{:S(2)}, u32[]{:S(2)}) collective-permute-start(f32[192,384]{1,0:T(8,128)S(1)} %collective-permute-done.2.refs_2_), channel_id=1, source_target_pairs={{0,385},{128,0},{256,128},{384,256},{1,384},{129,1},{257,129},{385... | collective-permute-start | bytes 884744 | tf_op jit(solution)/shard_map/ppermute | solution.py:216
  62.1 8.9 %collective-permute-start.5 = (f32[192,384]{1,0:T(8,128)S(1)}, f32[192,384]{1,0:T(8,128)S(1)}, u32[]{:S(2)}, u32[]{:S(2)}) collective-permute-start(f32[192,384]{1,0:T(8,128)S(1)} %collective-permute-done.3.refs_3_), channel_id=1, source_target_pairs={{0,128},{128,256},{256,384},{384,1},{1,129},{129,257},{257,385},{3... | collective-permute-start | bytes 884744 | tf_op jit(solution)/shard_map/ppermute | solution.py:216
  71.0 3.3 %collective-permute-done.4.refs_4_ = f32[192,384]{1,0:T(8,128)S(1)} collective-permute-done((f32[192,384]{1,0:T(8,128)S(1)}, f32[192,384]{1,0:T(8,128)S(1)}, u32[]{:S(2)}, u32[]{:S(2)}) %collective-permute-start.4) | collective-permute-done | bytes 294944 | tf_op jit(solution)/shard_map/ppermute | solution.py:216
  74.4 6.5 %collective-permute-start.6 = (f32[192,384]{1,0:T(8,128)S(1)}, f32[192,384]{1,0:T(8,128)S(1)}, u32[]{:S(2)}, u32[]{:S(2)}) collective-permute-start(f32[192,384]{1,0:T(8,128)S(1)} %collective-permute-done.4.refs_4_), channel_id=1, source_target_pairs={{0,385},{128,0},{256,128},{384,256},{1,384},{129,1},{257,129},{385... | collective-permute-start | bytes 884744 | tf_op jit(solution)/shard_map/ppermute | solution.py:216
  80.8 3.7 %collective-permute-done.5.refs_5_ = f32[192,384]{1,0:T(8,128)S(1)} collective-permute-done((f32[192,384]{1,0:T(8,128)S(1)}, f32[192,384]{1,0:T(8,128)S(1)}, u32[]{:S(2)}, u32[]{:S(2)}) %collective-permute-start.5) | collective-permute-done | bytes 294944 | tf_op jit(solution)/shard_map/ppermute | solution.py:216
  84.6 4.8 %collective-permute-start.7 = (f32[192,384]{1,0:T(8,128)S(1)}, f32[192,384]{1,0:T(8,128)S(1)}, u32[]{:S(2)}, u32[]{:S(2)}) collective-permute-start(f32[192,384]{1,0:T(8,128)S(1)} %collective-permute-done.5.refs_5_), channel_id=1, source_target_pairs={{0,128},{128,256},{256,384},{384,1},{1,129},{129,257},{257,385},{3... | collective-permute-start | bytes 884744 | tf_op jit(solution)/shard_map/ppermute | solution.py:216
  89.4 0.7 shifts.1
  90.1 0.3 collective-permute-done.6.refs_6_
  90.4 1.0 place.1
  91.4 6.3 %seven.1 = (f32[768,384]{1,0:T(8,128)S(1)}, bf16[768,384]{1,0:T(8,128)(2,1)S(1)}, bf16[768,384]{1,0:T(8,128)(2,1)S(1)}) custom-call(s32[4]{0:T(128)S(1)} %pad_add_fusion.where_ref.refs_0_, f32[16,2,24,1536]{3,2,1,0:T(8,128)} %bitcast.4.rows_ref, bf16[1536,384]{1,0:T(8,128)(2,1)S(1)} %get-tuple-element.21.high_ref, ...), custom_call_target="tpu_custom_call" | custom-call | flops 2717908992 | bytes 7077888 | tf_op jit(solution)/shard_map/seven/pallas_call | solution.py:298
  97.6 1.3 collective-permute-done.7.refs_4_
  98.9 1.3 %eighth_theirs.1 = f32[384,384]{1,0:T(8,128)S(1)} custom-call(s32[4]{0:T(128)S(1)} %pad_add_fusion.where_ref.refs_0_, f32[768,384]{1,0:T(8,128)S(1)} %get-tuple-element.28.refs_1_, bf16[768,384]{1,0:T(8,128)(2,1)S(1)} %get-tuple-element.29.refs_2_, bf16[768,384]{1,0:T(8,128)(2,1)S(1)} %get-tuple-element.30.refs_3_, f32[192,384]{1,0:T(8,128)S(1)} %collective-permute-done.7.refs_4_), custom_call_target="tpu_custom_call" | custom-call | flops 339738624 | bytes 3145728 | tf_op jit(solution)/shard_map/eighth_theirs/pallas_call | solution.py:313
  100.2 4.3 %collective-permute-start.8 = (f32[384,384]{1,0:T(8,128)S(1)}, f32[384,384]{1,0:T(8,128)S(1)}, u32[]{:S(2)}, u32[]{:S(2)}) collective-permute-start(f32[384,384]{1,0:T(8,128)S(1)} %eighth_theirs.1), channel_id=1, source_target_pairs={{0,32},{32,0},{1,33},{33,1},{2,34},{34,2},{3,35},{35,3},{4,36},{36... | collective-permute-start | bytes 1769480 | tf_op jit(solution)/shard_map/ppermute | solution.py:325
  104.5 1.3 %eighth_mine.1.own_ref = f32[384,384]{1,0:T(8,128)S(1)} custom-call(s32[4]{0:T(128)S(1)} %pad_add_fusion.where_ref.refs_0_, f32[768,384]{1,0:T(8,128)S(1)} %get-tuple-element.28.refs_1_, bf16[768,384]{1,0:T(8,128)(2,1)S(1)} %get-tuple-element.29.refs_2_, bf16[768,384]{1,0:T(8,128)(2,1)S(1)} %get-tuple-element.30.refs_3_, ...), custom_call_target="tpu_custom_call" | custom-call | flops 339738624 | bytes 3145728 | tf_op jit(solution)/shard_map/eighth_mine/pallas_call | solution.py:313
  105.8 0.3 collective-permute-done.8.other_ref
  106.1 0.6 pack.1
  106.8 21.5 %all_to_all.15.parts_ref = f32[32,36,128]{2,1,0:T(8,128)S(1)} all-to-all(f32[32,36,128]{2,1,0:T(8,128)S(1)} %pack.1), channel_id=1, replica_groups=mesh['zl4'=4,'zb'=2,'core'=2,'y'=4,'x'=4,'zhi'=2] {'zb','y','x'}, dimensions={0} | all-to-all | bytes 1179648 | tf_op jit(solution)/shard_map/all_to_all | solution.py:337
  128.2 0.8 divide.1
  (15 shorter events, 0.1 us)
Async XLA Ops:
  0.0 17.4 %copy-start.2 = (s32[1,384]{1,0:T(1,128)S(1)}, s32[1,384]{1,0:T(1,128)}, u32[]{:S(2)}) copy-start(s32[1,384]{1,0:T(1,128)} %constant.37.clone.source_ref) | copy-start | bytes 4612
  0.0 9.6 %copy-start = (f32[12,6144]{1,0:T(8,128)S(1)}, f32[12,6144]{1,0:T(8,128)}, u32[]{:S(2)}) copy-start(f32[12,6144]{1,0:T(8,128)} %a_ref.1) | copy-start | bytes 884740
  1.9 18.4 %all-to-all-start.1 = ((f32[16,12,384]{2,1,0:T(8,128)}), f32[16,12,384]{2,1,0:T(8,128)S(1)}, u32[]{:S(2)}, u32[]{:S(2)}) async-start(f32[16,12,384]{2,1,0:T(8,128)} %blocks.1), calls=%async_computation.1 | async-start | bytes 786432 | tf_op jit(solution)/shard_map/all_to_all | solution.py:246
  10.5 6.9 %collective-permute-start = (f32[12,3072]{1,0:T(8,128)S(1)}, f32[12,3072]{1,0:T(8,128)S(1)}, u32[]{:S(2)}, u32[]{:S(2)}) collective-permute-start(f32[12,3072]{1,0:T(8,128)S(1)} %get-tuple-element.20), channel_id=1, source_target_pairs={{0,64},{64,0},{1,65},{65,1},{2,66},{66,2},{3,67},{67,3},{4,68},{68... | collective-permute-start | bytes 442376 | tf_op jit(solution)/shard_map/ppermute | solution.py:234
  20.2 69.1 %copy-start.1 = (f32[1536]{0:T(1024)S(1)}, f32[1536]{0:T(1024)}, u32[]{:S(2)}) copy-start(f32[1536]{0:T(1024)} %lanes_ref.1) | copy-start | bytes 18436
  20.2 69.1 %copy-start.3 = (f32[150]{0:T(256)S(1)}, f32[150]{0:T(256)}, u32[]{:S(2)}) copy-start(f32[150]{0:T(256)} %occ_ref.1) | copy-start | bytes 1804
  20.2 69.1 %copy-start.4 = (s32[4]{0:T(128)S(1)}, s32[4]{0:T(128)}, u32[]{:S(2)}) copy-start(s32[4]{0:T(128)} %wi_ref.1) | copy-start | bytes 52
  20.2 69.1 %copy-start.5 = (s32[4]{0:T(128)S(1)}, s32[4]{0:T(128)}, u32[]{:S(2)}) copy-start(s32[4]{0:T(128)} %wj_ref.1) | copy-start | bytes 52
  20.3 71.1 %all-to-all-start = ((f32[32,24,1536]{2,1,0:T(8,128)}), f32[32,24,1536]{2,1,0:T(8,128)}, u32[]{:S(2)}, u32[]{:S(2)}) async-start(f32[32,24,1536]{2,1,0:T(8,128)} %spread.1), calls=%async_computation | async-start | bytes 9437184 | tf_op jit(solution)/shard_map/all_to_all | solution.py:276
  31.1 19.6 %collective-permute-start.1 = (f32[192,384]{1,0:T(8,128)S(1)}, f32[192,384]{1,0:T(8,128)S(1)}, u32[]{:S(2)}, u32[]{:S(2)}) collective-permute-start(f32[192,384]{1,0:T(8,128)S(1)} %stack.21.refs_0_), channel_id=1, source_target_pairs={{0,128},{128,256},{256,384},{384,1},{1,129},{129,257},{257,385},{3... | collective-permute-start | bytes 884744 | tf_op jit(solution)/shard_map/ppermute | solution.py:216
  34.8 19.5 %collective-permute-start.2 = (f32[192,384]{1,0:T(8,128)S(1)}, f32[192,384]{1,0:T(8,128)S(1)}, u32[]{:S(2)}, u32[]{:S(2)}) collective-permute-start(f32[192,384]{1,0:T(8,128)S(1)} %stack.21.refs_0_), channel_id=1, source_target_pairs={{0,385},{128,0},{256,128},{384,256},{1,384},{129,1},{257,129},{385... | collective-permute-start | bytes 884744 | tf_op jit(solution)/shard_map/ppermute | solution.py:216
  50.7 11.4 %collective-permute-start.3 = (f32[192,384]{1,0:T(8,128)S(1)}, f32[192,384]{1,0:T(8,128)S(1)}, u32[]{:S(2)}, u32[]{:S(2)}) collective-permute-start(f32[192,384]{1,0:T(8,128)S(1)} %collective-permute-done.1.refs_1_), channel_id=1, source_target_pairs={{0,128},{128,256},{256,384},{384,1},{1,129},{129,257},{257,385},{3... | collective-permute-start | bytes 884744 | tf_op jit(solution)/shard_map/ppermute | solution.py:216
  54.2 20.1 %collective-permute-start.4 = (f32[192,384]{1,0:T(8,128)S(1)}, f32[192,384]{1,0:T(8,128)S(1)}, u32[]{:S(2)}, u32[]{:S(2)}) collective-permute-start(f32[192,384]{1,0:T(8,128)S(1)} %collective-permute-done.2.refs_2_), channel_id=1, source_target_pairs={{0,385},{128,0},{256,128},{384,256},{1,384},{129,1},{257,129},{385... | collective-permute-start | bytes 884744 | tf_op jit(solution)/shard_map/ppermute | solution.py:216
  62.1 22.5 %collective-permute-start.5 = (f32[192,384]{1,0:T(8,128)S(1)}, f32[192,384]{1,0:T(8,128)S(1)}, u32[]{:S(2)}, u32[]{:S(2)}) collective-permute-start(f32[192,384]{1,0:T(8,128)S(1)} %collective-permute-done.3.refs_3_), channel_id=1, source_target_pairs={{0,128},{128,256},{256,384},{384,1},{1,129},{129,257},{257,385},{3... | collective-permute-start | bytes 884744 | tf_op jit(solution)/shard_map/ppermute | solution.py:216
  74.4 16.0 %collective-permute-start.6 = (f32[192,384]{1,0:T(8,128)S(1)}, f32[192,384]{1,0:T(8,128)S(1)}, u32[]{:S(2)}, u32[]{:S(2)}) collective-permute-start(f32[192,384]{1,0:T(8,128)S(1)} %collective-permute-done.4.refs_4_), channel_id=1, source_target_pairs={{0,385},{128,0},{256,128},{384,256},{1,384},{129,1},{257,129},{385... | collective-permute-start | bytes 884744 | tf_op jit(solution)/shard_map/ppermute | solution.py:216
  84.6 14.3 %collective-permute-start.7 = (f32[192,384]{1,0:T(8,128)S(1)}, f32[192,384]{1,0:T(8,128)S(1)}, u32[]{:S(2)}, u32[]{:S(2)}) collective-permute-start(f32[192,384]{1,0:T(8,128)S(1)} %collective-permute-done.5.refs_5_), channel_id=1, source_target_pairs={{0,128},{128,256},{256,384},{384,1},{1,129},{129,257},{257,385},{3... | collective-permute-start | bytes 884744 | tf_op jit(solution)/shard_map/ppermute | solution.py:216
  100.2 5.9 %collective-permute-start.8 = (f32[384,384]{1,0:T(8,128)S(1)}, f32[384,384]{1,0:T(8,128)S(1)}, u32[]{:S(2)}, u32[]{:S(2)}) collective-permute-start(f32[384,384]{1,0:T(8,128)S(1)} %eighth_theirs.1), channel_id=1, source_target_pairs={{0,32},{32,0},{1,33},{33,1},{2,34},{34,2},{3,35},{35,3},{4,36},{36... | collective-permute-start | bytes 1769480 | tf_op jit(solution)/shard_map/ppermute | solution.py:325
